TPU v7x, 32 devices: a whole 2x2x4 slice. The times are simulated.
32 devices in a mesh: fsdp: 4 (over z), seq: 8 (over y, x, core).
Axes of the slice: x: 2, y: 2, z: 4, core: 2. Of those that a mesh axis runs over, the one named last changes fastest.
Arguments:
- hidden_in: bfloat16 [2, 2048, 2048], P(None, 'seq', 'fsdp'), may hold values from -6 to 6
- out_cot: bfloat16 [2, 2048, 2048], P(None, 'seq', 'fsdp'), may hold values from -6 to 6
- doc_lengths: int32 [2, 16], replicated, may hold values from 1 to 1024, 2048 in all within a row
- mixer_gain: float32 [2048], replicated, may hold values from 0.5 to 1.5
- in_proj: bfloat16 [2048, 3, 2048], P('seq', None, 'fsdp'), may hold values from -0.125 to 0.125
- short_filter: float32 [3, 3, 2048], P(None, None, 'fsdp'), may hold values from -3 to 3
- decay_rate: float32 [2048, 16], P('fsdp'), may hold values from 9.765625e-06 to 0.05
- mode_angle: float32 [2048, 16], P('fsdp'), may hold values from -0.05 to 0.05
- residue_re: float32 [2048, 16], P('fsdp'), may hold values from -0.25 to 0.25
- residue_im: float32 [2048, 16], P('fsdp'), may hold values from -0.25 to 0.25
- skip_gain: float32 [2048], P('fsdp'), may hold values from 0.5 to 1.5
- out_proj: bfloat16 [2048, 2048], P('fsdp', 'seq'), may hold values from -0.125 to 0.125
- feed_gain: float32 [2048], replicated, may hold values from 0.5 to 1.5
- gate_proj: bfloat16 [2048, 5632], P('seq', 'fsdp'), may hold values from -0.125 to 0.125
- up_proj: bfloat16 [2048, 5632], P('seq', 'fsdp'), may hold values from -0.125 to 0.125
- down_proj: bfloat16 [5632, 2048], P('fsdp', 'seq'), may hold values from -0.109375 to 0.109375
Outputs:
- block_out: bfloat16 [2, 2048, 2048], P(None, 'seq', 'fsdp')
- hidden_grad: float32 [2, 2048, 2048], P(None, 'seq', 'fsdp')
- mixer_gain_grad: float32 [2048], replicated
- in_proj_grad: float32 [2048, 3, 2048], P('seq', None, 'fsdp')
- short_filter_grad: float32 [3, 3, 2048], P(None, None, 'fsdp')
- decay_rate_grad: float32 [2048, 16], P('fsdp')
- mode_angle_grad: float32 [2048, 16], P('fsdp')
- residue_re_grad: float32 [2048, 16], P('fsdp')
- residue_im_grad: float32 [2048, 16], P('fsdp')
- skip_gain_grad: float32 [2048], P('fsdp')
- out_proj_grad: float32 [2048, 2048], P('fsdp', 'seq')
- feed_gain_grad: float32 [2048], replicated
- gate_proj_grad: float32 [2048, 5632], P('seq', 'fsdp')
- up_proj_grad: float32 [2048, 5632], P('seq', 'fsdp')
- down_proj_grad: float32 [5632, 2048], P('fsdp', 'seq')
Inputs may be any that keep to these rules, and one draw needn't show every extreme that they name: `doc_lengths`: each row lists the 16 documents of one micro-batch in order; they sum to 2048 tokens and one of them is exactly 1024 long.
All inputs are finite; a program needn't handle non-finite values.
Results may differ from a plain program's by a relative error of at most 0.017.
Values may be sent and summed in bfloat16 or wider, within the bound.
No kernel may reach another device: no remote copies, remote signals or barrier semaphores. Data moves between devices by JAX's collectives and lax.ppermute only.
A program may use at most 320 MiB of HBM per device.

v0:
```python
import math

import jax
import jax.numpy as jnp
from jax import lax
from jax.sharding import PartitionSpec as P

norm_eps = 1e-05
block_len = 64
highest = lax.Precision.HIGHEST


def shifted(array, axis, by):
    size = lax.axis_size(axis)
    pairs = [(i, i + by) for i in range(size) if 0 <= i + by < size]
    return lax.ppermute(array, axis, pairs)


def doc_tables(doc_lens, total):
    places = jnp.arange(total, dtype=jnp.int32)
    starts = jnp.cumsum(doc_lens, dtype=jnp.int32) - doc_lens
    before = starts[None, :] <= places[:, None]
    doc_ids = jnp.sum(before.astype(jnp.int32), axis=1, dtype=jnp.int32) - 1
    begins = jnp.max(jnp.where(before, starts[None, :], 0), axis=1)
    return (doc_ids, places - begins)


def chain_step(earlier_part, later_part):
    early_mul_re, early_mul_im, early_sum_re, early_sum_im = earlier_part
    late_mul_re, late_mul_im, late_sum_re, late_sum_im = later_part
    return (
        late_mul_re * early_mul_re - late_mul_im * early_mul_im,
        late_mul_re * early_mul_im + late_mul_im * early_mul_re,
        late_mul_re * early_sum_re - late_mul_im * early_sum_im + late_sum_re,
        late_mul_re * early_sum_im + late_mul_im * early_sum_re + late_sum_im,
    )


def conv_group(values, doc_ids, rates, angles, res_real, res_imag):
    length, group = values.shape
    count = length // block_len
    ramp = jnp.arange(block_len + 1, dtype=jnp.float32)
    fading = jnp.exp(-rates[:, :, None] * ramp)
    pow_re = fading * jnp.cos(angles[:, :, None] * ramp)
    pow_im = fading * jnp.sin(angles[:, :, None] * ramp)
    within = jnp.arange(block_len, dtype=jnp.int32)
    spread = within[:, None] - within[None, :]
    lags = jnp.maximum(spread, 0).astype(jnp.float32)
    kernel = jnp.exp(-rates[:, :, None, None] * lags) * (
        res_real[:, :, None, None] * jnp.cos(angles[:, :, None, None] * lags)
        - res_imag[:, :, None, None] * jnp.sin(angles[:, :, None, None] * lags)
    )
    toeplitz = jnp.sum(kernel, axis=1)
    blocks = values.reshape(count, block_len, group)
    doc_blocks = doc_ids.reshape(count, block_len)
    same_doc = ((doc_blocks[:, :, None] == doc_blocks[:, None, :]) & (spread >= 0)[None]).astype(
        jnp.float32
    )
    masked = toeplitz[None] * same_doc[:, None]
    inner = jnp.einsum("bgts,bsg->btg", masked, blocks, precision=highest)
    ends = doc_blocks[:, -1]
    earlier = jnp.concatenate([jnp.full((1,), -1, dtype=jnp.int32), ends[:-1]])
    tail = (doc_blocks == ends[:, None]).astype(jnp.float32)
    rev_re = pow_re[:, :, block_len - 1 :: -1]
    rev_im = pow_im[:, :, block_len - 1 :: -1]
    weighted = blocks * tail[:, :, None]
    end_re = jnp.einsum("bjg,gkj->bgk", weighted, rev_re, precision=highest)
    end_im = jnp.einsum("bjg,gkj->bgk", weighted, rev_im, precision=highest)
    keep = (ends == earlier).astype(jnp.float32)[:, None, None]
    carry_re = keep * pow_re[None, :, :, block_len]
    carry_im = keep * pow_im[None, :, :, block_len]
    scanned = lax.associative_scan(chain_step, (carry_re, carry_im, end_re, end_im), axis=0)
    state_re, state_im = (scanned[2], scanned[3])
    zero_state = jnp.zeros((1,) + state_re.shape[1:], dtype=jnp.float32)
    prior_re = jnp.concatenate([zero_state, state_re[:-1]], axis=0)
    prior_im = jnp.concatenate([zero_state, state_im[:-1]], axis=0)
    coef_re = res_real[None] * prior_re - res_imag[None] * prior_im
    coef_im = res_real[None] * prior_im + res_imag[None] * prior_re
    outer = jnp.einsum("bgk,gkj->bjg", coef_re, pow_re[:, :, 1:], precision=highest) - jnp.einsum(
        "bgk,gkj->bjg", coef_im, pow_im[:, :, 1:], precision=highest
    )
    alive = (doc_blocks == earlier[:, None]).astype(jnp.float32)
    return (inner + outer * alive[:, :, None]).reshape(length, group)


def long_conv(values, doc_ids, rates, angles, res_real, res_imag, skip_part):
    length, chans = values.shape
    group = math.gcd(chans, 16)
    folds = chans // group
    stacked = values.reshape(length, folds, group).transpose(1, 0, 2)

    def per_group(items):
        return conv_group(items[0], doc_ids, items[1], items[2], items[3], items[4])

    mapped = lax.map(
        jax.checkpoint(per_group),
        (
            stacked,
            rates.reshape(folds, group, -1),
            angles.reshape(folds, group, -1),
            res_real.reshape(folds, group, -1),
            res_imag.reshape(folds, group, -1),
        ),
    )
    return mapped.transpose(1, 0, 2).reshape(length, chans) + skip_part[None, :] * values


def rms_scale(values):
    return lax.rsqrt(jnp.mean(values * values, axis=-1, keepdims=True) + norm_eps)


def norm_back(values, scale, gain, grad_in):
    weighted = gain * grad_in
    d_values = scale * weighted - values * scale * scale * scale * jnp.mean(
        weighted * values, axis=-1, keepdims=True
    )
    return (d_values, jnp.sum(values * scale * grad_in, axis=0))


def row_total(partial_rows):
    return lax.psum(partial_rows, "fsdp")


def to_channels(token_side):
    return lax.all_to_all(token_side, "seq", split_axis=1, concat_axis=0, tiled=True)


def to_tokens(channel_side):
    return lax.all_to_all(channel_side, "seq", split_axis=0, concat_axis=1, tiled=True)


def contract_first(left, right):
    return lax.dot_general(
        left, right, (((0,), (0,)), ((), ())), preferred_element_type=jnp.float32
    )


def contract_last(left, right):
    return lax.dot_general(
        left, right, (((1,), (1,)), ((), ())), preferred_element_type=jnp.float32
    )


def on_device(
    hidden_in,
    out_cot,
    doc_lengths,
    mixer_gain,
    in_proj,
    short_filter,
    decay_rate,
    mode_angle,
    residue_re,
    residue_im,
    skip_gain,
    out_proj,
    feed_gain,
    gate_proj,
    up_proj,
    down_proj,
):
    batches = hidden_in.shape[0]
    rows_here = hidden_in.shape[1]
    width_share = hidden_in.shape[2]
    seq_count = lax.axis_size("seq")
    seq_len = rows_here * seq_count
    chan_here = width_share // seq_count
    seq_rank = lax.axis_index("seq")
    fsdp_rank = lax.axis_index("fsdp")
    full_in, full_cot = (
        lax.all_gather(hidden_in, "fsdp", axis=2, tiled=True),
        lax.all_gather(out_cot, "fsdp", axis=2, tiled=True),
    )
    chan_start = seq_rank * chan_here
    rates = lax.dynamic_slice_in_dim(decay_rate, chan_start, chan_here, 0)
    angles = lax.dynamic_slice_in_dim(mode_angle, chan_start, chan_here, 0)
    res_real = lax.dynamic_slice_in_dim(residue_re, chan_start, chan_here, 0)
    res_imag = lax.dynamic_slice_in_dim(residue_im, chan_start, chan_here, 0)
    skips = lax.dynamic_slice_in_dim(skip_gain, chan_start, chan_here, 0)
    d_mixer_gain = jnp.zeros(mixer_gain.shape, jnp.float32)
    d_feed_gain = jnp.zeros(feed_gain.shape, jnp.float32)
    d_short = jnp.zeros(short_filter.shape, jnp.float32)
    d_rates = jnp.zeros(rates.shape, jnp.float32)
    d_angles = jnp.zeros(angles.shape, jnp.float32)
    d_res_real = jnp.zeros(res_real.shape, jnp.float32)
    d_res_imag = jnp.zeros(res_imag.shape, jnp.float32)
    d_skips = jnp.zeros(skips.shape, jnp.float32)
    shard_totals = tuple(
        (
            jnp.zeros(piece.shape, jnp.float32)
            for piece in (in_proj, out_proj, gate_proj, up_proj, down_proj)
        )
    )
    outputs = []
    in_grads = []
    for micro in range(batches):
        gathered = (
            lax.all_gather(in_proj, "seq", axis=0, tiled=True),
            lax.all_gather(out_proj, "seq", axis=1, tiled=True),
            lax.all_gather(gate_proj, "seq", axis=0, tiled=True),
            lax.all_gather(up_proj, "seq", axis=0, tiled=True),
            lax.all_gather(down_proj, "seq", axis=1, tiled=True),
        )
        w_in, w_out, w_gate, w_up, w_down = gathered
        doc_ids, places = doc_tables(doc_lengths[micro], seq_len)
        place_here = lax.dynamic_slice_in_dim(places, seq_rank * rows_here, rows_here, 0)
        masks = [(place_here >= lag_tap).astype(jnp.float32)[:, None, None] for lag_tap in range(3)]
        resid = full_in[micro].astype(jnp.float32)
        scale_one = rms_scale(resid)
        normed_one = (resid * scale_one * mixer_gain).astype(jnp.bfloat16)
        project = jnp.einsum("td,dje->tje", normed_one, w_in, preferred_element_type=jnp.float32)
        before = shifted(project[-2:], "seq", 1)
        extended = jnp.concatenate([before, project], axis=0)
        conv_out = sum(
            (
                short_filter[lag_tap][None]
                * masks[lag_tap]
                * extended[2 - lag_tap : 2 - lag_tap + rows_here]
                for lag_tap in range(3)
            )
        )
        gate_one = conv_out[:, 0]
        gate_two = conv_out[:, 1]
        values = conv_out[:, 2]
        product = (gate_two * values).astype(jnp.bfloat16)
        channel_in = to_channels(product).astype(jnp.float32)

        def mixer(signal, rate_part, angle_part, real_part, imag_part, skip_part):
            return long_conv(
                signal, doc_ids, rate_part, angle_part, real_part, imag_part, skip_part
            )

        channel_out, mixer_back = jax.vjp(
            mixer, channel_in, rates, angles, res_real, res_imag, skips
        )
        mixed = to_tokens(channel_out.astype(jnp.bfloat16)).astype(jnp.float32)
        gated = (gate_one * mixed).astype(jnp.bfloat16)
        stream = resid + row_total(jnp.dot(gated, w_out, preferred_element_type=jnp.float32))
        scale_two = rms_scale(stream)
        normed_two = (stream * scale_two * feed_gain).astype(jnp.bfloat16)
        gate_pre = jnp.dot(normed_two, w_gate, preferred_element_type=jnp.float32)
        up_pre = jnp.dot(normed_two, w_up, preferred_element_type=jnp.float32)
        sigmoid_vals = jax.nn.sigmoid(gate_pre)
        activated = gate_pre * sigmoid_vals
        hidden = (activated * up_pre).astype(jnp.bfloat16)
        down_part = lax.psum_scatter(
            jnp.dot(hidden, w_down, preferred_element_type=jnp.float32).astype(jnp.bfloat16),
            "fsdp",
            scatter_dimension=1,
            tiled=True,
        ).astype(jnp.float32)
        stream_share = lax.dynamic_slice_in_dim(stream, fsdp_rank * width_share, width_share, 1)
        outputs.append((stream_share + down_part).astype(jnp.bfloat16))
        cot_rows = full_cot[micro]
        d_hidden = contract_last(cot_rows, w_down)
        grad_down = contract_first(hidden, cot_rows)
        d_gate = (
            d_hidden * up_pre * sigmoid_vals * (1.0 + gate_pre * (1.0 - sigmoid_vals))
        ).astype(jnp.bfloat16)
        d_up = (d_hidden * activated).astype(jnp.bfloat16)
        grad_gate = contract_first(normed_two, d_gate)
        grad_up = contract_first(normed_two, d_up)
        d_normed_two = row_total(contract_last(d_gate, w_gate) + contract_last(d_up, w_up))
        d_stream, gain_part = norm_back(stream, scale_two, feed_gain, d_normed_two)
        d_stream = d_stream + cot_rows.astype(jnp.float32)
        d_feed_gain = d_feed_gain + gain_part
        d_mix = d_stream.astype(jnp.bfloat16)
        grad_out = contract_first(gated, d_mix)
        d_gated = contract_last(d_mix, w_out)
        d_mixed = (d_gated * gate_one).astype(jnp.bfloat16)
        d_gate_one = d_gated * mixed
        back_in = to_channels(d_mixed).astype(jnp.float32)
        d_signal, d_rate, d_angle, d_real, d_imag, d_skip = mixer_back(back_in)
        d_rates = d_rates + d_rate
        d_angles = d_angles + d_angle
        d_res_real = d_res_real + d_real
        d_res_imag = d_res_imag + d_imag
        d_skips = d_skips + d_skip
        d_product = to_tokens(d_signal.astype(jnp.bfloat16)).astype(jnp.float32)
        d_conv = jnp.stack([d_gate_one, d_product * values, d_product * gate_two], axis=1)
        d_short = d_short + jnp.stack(
            [
                jnp.sum(
                    masks[lag_tap] * extended[2 - lag_tap : 2 - lag_tap + rows_here] * d_conv,
                    axis=0,
                )
                for lag_tap in range(3)
            ]
        )
        spread_back = sum(
            (
                jnp.pad(
                    short_filter[lag_tap][None] * masks[lag_tap] * d_conv,
                    ((2 - lag_tap, lag_tap), (0, 0), (0, 0)),
                )
                for lag_tap in range(3)
            )
        )
        returned = shifted(spread_back[:2], "seq", -1)
        d_project = (
            spread_back[2:] + jnp.pad(returned, ((rows_here - 2, 0), (0, 0), (0, 0)))
        ).astype(jnp.bfloat16)
        grad_in = jnp.einsum(
            "td,tje->dje", normed_one, d_project, preferred_element_type=jnp.float32
        )
        d_normed_one = row_total(
            jnp.einsum("tje,dje->td", d_project, w_in, preferred_element_type=jnp.float32)
        )
        d_resid, gain_part = norm_back(resid, scale_one, mixer_gain, d_normed_one)
        d_mixer_gain = d_mixer_gain + gain_part
        in_grads.append(
            lax.dynamic_slice_in_dim(d_resid + d_stream, fsdp_rank * width_share, width_share, 1)
        )
        summed = (
            lax.psum_scatter(
                grad_in.astype(jnp.bfloat16), "seq", scatter_dimension=0, tiled=True
            ).astype(jnp.float32),
            lax.psum_scatter(
                grad_out.astype(jnp.bfloat16), "seq", scatter_dimension=1, tiled=True
            ).astype(jnp.float32),
            lax.psum_scatter(
                grad_gate.astype(jnp.bfloat16), "seq", scatter_dimension=0, tiled=True
            ).astype(jnp.float32),
            lax.psum_scatter(
                grad_up.astype(jnp.bfloat16), "seq", scatter_dimension=0, tiled=True
            ).astype(jnp.float32),
            lax.psum_scatter(
                grad_down.astype(jnp.bfloat16), "seq", scatter_dimension=1, tiled=True
            ).astype(jnp.float32),
        )
        shard_totals = tuple((total + piece for total, piece in zip(shard_totals, summed)))
    small = (
        lax.psum(d_mixer_gain.astype(jnp.bfloat16), "seq").astype(jnp.float32),
        lax.psum(d_feed_gain.astype(jnp.bfloat16), "seq").astype(jnp.float32),
        lax.psum(d_short.astype(jnp.bfloat16), "seq").astype(jnp.float32),
    )
    filters = (
        lax.all_gather(d_rates, "seq", axis=0, tiled=True),
        lax.all_gather(d_angles, "seq", axis=0, tiled=True),
        lax.all_gather(d_res_real, "seq", axis=0, tiled=True),
        lax.all_gather(d_res_imag, "seq", axis=0, tiled=True),
        lax.all_gather(d_skips, "seq", axis=0, tiled=True),
    )
    return (
        jnp.stack(outputs),
        jnp.stack(in_grads),
        small[0],
        shard_totals[0],
        small[2],
        filters[0],
        filters[1],
        filters[2],
        filters[3],
        filters[4],
        shard_totals[1],
        small[1],
        shard_totals[2],
        shard_totals[3],
        shard_totals[4],
    )


def solution(mesh):
    in_specs = (
        P(None, "seq", "fsdp"),
        P(None, "seq", "fsdp"),
        P(),
        P(),
        P("seq", None, "fsdp"),
        P(None, None, "fsdp"),
        P("fsdp", None),
        P("fsdp", None),
        P("fsdp", None),
        P("fsdp", None),
        P("fsdp"),
        P("fsdp", "seq"),
        P(),
        P("seq", "fsdp"),
        P("seq", "fsdp"),
        P("fsdp", "seq"),
    )
    out_specs = (
        P(None, "seq", "fsdp"),
        P(None, "seq", "fsdp"),
        P(),
        P("seq", None, "fsdp"),
        P(None, None, "fsdp"),
        P("fsdp", None),
        P("fsdp", None),
        P("fsdp", None),
        P("fsdp", None),
        P("fsdp"),
        P("fsdp", "seq"),
        P(),
        P("seq", "fsdp"),
        P("seq", "fsdp"),
        P("fsdp", "seq"),
    )
    return jax.shard_map(
        on_device, mesh=mesh, in_specs=in_specs, out_specs=out_specs, check_vma=False
    )
```

profile of v0, /device:TPU:0, one launch (start us, length us, event | category | flops | bytes accessed | tf_op | source)
XLA Modules:
  0.0 3751.7 jit_solution(7686039242813314933)
XLA Ops:
  17.7 40.6 %all-gather.12.cloned.1.call-done = bf16[2,256,2048]{2,1,0:T(8,128)(2,1)} async-done(((bf16[2,256,512]{2,1,0:T(8,128)(2,1)}), bf16[2,256,2048]{2,1,0:T(8,128)(2,1)}) %all-gather.12.cloned.1.call-update) | async-done | bytes 2097168 | tf_op jit(solution)/shard_map/all_gather | solution.py:171
  60.5 44.0 %all-gather.14.cloned.1.call-done = bf16[2048,3,512]{2,0,1:T(8,128)(2,1)} async-done(((bf16[256,3,512]{2,0,1:T(8,128)(2,1)}), bf16[2048,3,512]{2,0,1:T(8,128)(2,1)}) %all-gather.14.cloned.1.call-update) | async-done | bytes 6291472 | tf_op jit(solution)/shard_map/all_gather | solution.py:198
  145.8 512.2 %while.72 = (s32[]{:T(128)}, f32[4,2048,16]{1,2,0:T(8,128)}, f32[4,2048,16]{1,2,0:T(8,128)}, f32[4,16,16]{2,1,0:T(8,128)}, f32[4,16,16]{2,1,0:T(8,128)}, /*index...) while((s32[]{:T(128)}, f32[4,2048,16]{1,2,0:T(8,128)}, ...), condition=%wide.region_6.7_spmd.clone.clone, body=%wide.region_4.6_spmd.clone.clone.sunk | while | flops 60626688 | bytes 7290541 | solution.py:95
  224.2 33.1 fusion.667
  257.4 26.1 fusion.668
  340.8 33.1 fusion.667
  457.5 33.1 fusion.667
  574.1 33.1 fusion.667
  661.1 475.0 %while.73 = (s32[]{:T(128)}, f32[4,2048,16]{1,2,0:T(8,128)}, f32[4,2048,16]{1,2,0:T(8,128)}, f32[4,16,16]{2,1,0:T(8,128)}, f32[4,16,16]{2,1,0:T(8,128)}, /*index...) while((s32[]{:T(128)}, f32[4,2048,16]{1,2,0:T(8,128)}, ...), condition=%wide.region_16.17_spmd.clone.clone, body=%wide.region_14.16_spmd.clone.clone.sunk | while | flops 60626688 | bytes 7224417 | solution.py:95
  718.2 33.1 fusion.683
  836.3 33.1 fusion.683
  954.3 33.1 fusion.683
  1072.3 33.1 fusion.683
  1173.3 151.7 %all-reduce.265.cloned.1.call-done = (f32[256,2048]{1,0:T(8,128)}, f32[256,2048]{1,0:T(8,128)}) async-done(((f32[256,2048]{1,0:T(8,128)}, f32[256,2048]{1,0:T(8,128)}), (f32[256,2048]{1,0:T(8,128)}, f32[256,2048]{1,0:T(8,128)})) %all-reduce.265.cloned.1.call-update) | async-done | bytes 4194320 | tf_op jit(solution)/shard_map/psum | solution.py:121
  1331.2 38.1 %all-gather.18.cloned.1.call-done = bf16[2048,1408]{1,0:T(8,128)(2,1)} async-done(((bf16[256,1408]{1,0:T(8,128)(2,1)}), bf16[2048,1408]{1,0:T(8,128)(2,1)}) %all-gather.18.cloned.1.call-update) | async-done | bytes 5767184 | tf_op jit(solution)/shard_map/all_gather | solution.py:200
  1375.1 39.4 %all-gather.20.cloned.1.call-done = bf16[2048,1408]{1,0:T(8,128)(2,1)} async-done(((bf16[256,1408]{1,0:T(8,128)(2,1)}), bf16[2048,1408]{1,0:T(8,128)(2,1)}) %all-gather.20.cloned.1.call-update) | async-done | bytes 5767184 | tf_op jit(solution)/shard_map/all_gather | solution.py:201
  1426.4 35.7 all-gather.24.cloned.1.call-done
  1462.1 45.1 %all-gather.22.cloned.1.call-done = bf16[1408,2048]{1,0:T(8,128)(2,1)} async-done(((bf16[1408,256]{1,0:T(8,128)(2,1)}), bf16[1408,2048]{1,0:T(8,128)(2,1)}) %all-gather.22.cloned.1.call-update) | async-done | bytes 5767184 | tf_op jit(solution)/shard_map/all_gather | solution.py:202
  1543.8 143.9 %all-reduce.263.cloned.1.call-done = (f32[256,2048]{1,0:T(8,128)}, f32[256,2048]{1,0:T(8,128)}) async-done(((f32[256,2048]{1,0:T(8,128)}, f32[256,2048]{1,0:T(8,128)}), (f32[256,2048]{1,0:T(8,128)}, f32[256,2048]{1,0:T(8,128)})) %all-reduce.263.cloned.1.call-update) | async-done | bytes 4194320 | tf_op jit(solution)/shard_map/psum | solution.py:121
  1760.0 819.3 %while.70 = (s32[]{:T(128)}, f32[4,2048,16]{1,2,0:T(8,128)}, f32[4,16,16]{2,1,0:T(8,128)}, f32[4,16,16]{2,1,0:T(8,128)}, f32[4,16,16]{2,1,0:T(8,128)}, /*index=5...) while((s32[]{:T(128)}, f32[4,2048,16]{1,2,0:T(8,128)}, ...), condition=%wide.region_39.40_spmd, body=%wide.region_22.39_spmd.sunk | while | flops 125805952 | bytes 20896408 | solution.py:95
  1891.1 44.4 %fusion.602 = (f32[16,16]{1,0:T(8,128)}, f32[16,16]{1,0:T(8,128)}, f32[16,16]{1,0:T(8,128)}, f32[16,16]{1,0:T(8,128)}, f32[16,16]{1,0:T(8,128)}, /*index=5*/f32[16,64,64]{2,1,0:T(8,128)S(1)}) fusion(f32[16,64,64]{2,1,0:T(8,128)S(1)} %multiply_reduce_fusion.40, f32[16,16]{1,0:T(8,128)S(1)} %copy-done.152, f32[64,64]{1,0:T(8,128)S(1)} %maximum_convert_fusion.4, ...), kind=kLoop, calls=%fused_computation.20.clone.1 | loop fusion | flops 27196160 | bytes 549888 | tf_op jit(solution)/shard_map/transpose(jvp())/while/body/eval_jaxpr/checkpoint/reduce_sum | solution.py:51
  2090.9 44.4 %fusion.602 = (f32[16,16]{1,0:T(8,128)}, f32[16,16]{1,0:T(8,128)}, f32[16,16]{1,0:T(8,128)}, f32[16,16]{1,0:T(8,128)}, f32[16,16]{1,0:T(8,128)}, /*index=5*/f32[16,64,64]{2,1,0:T(8,128)S(1)}) fusion(f32[16,64,64]{2,1,0:T(8,128)S(1)} %multiply_reduce_fusion.40, f32[16,16]{1,0:T(8,128)S(1)} %copy-done.152, f32[64,64]{1,0:T(8,128)S(1)} %maximum_convert_fusion.4, ...), kind=kLoop, calls=%fused_computation.20.clone.1 | loop fusion | flops 27196160 | bytes 549888 | tf_op jit(solution)/shard_map/transpose(jvp())/while/body/eval_jaxpr/checkpoint/reduce_sum | solution.py:51
  2290.5 44.4 %fusion.602 = (f32[16,16]{1,0:T(8,128)}, f32[16,16]{1,0:T(8,128)}, f32[16,16]{1,0:T(8,128)}, f32[16,16]{1,0:T(8,128)}, f32[16,16]{1,0:T(8,128)}, /*index=5*/f32[16,64,64]{2,1,0:T(8,128)S(1)}) fusion(f32[16,64,64]{2,1,0:T(8,128)S(1)} %multiply_reduce_fusion.40, f32[16,16]{1,0:T(8,128)S(1)} %copy-done.152, f32[64,64]{1,0:T(8,128)S(1)} %maximum_convert_fusion.4, ...), kind=kLoop, calls=%fused_computation.20.clone.1 | loop fusion | flops 27196160 | bytes 549888 | tf_op jit(solution)/shard_map/transpose(jvp())/while/body/eval_jaxpr/checkpoint/reduce_sum | solution.py:51
  2490.0 44.4 %fusion.602 = (f32[16,16]{1,0:T(8,128)}, f32[16,16]{1,0:T(8,128)}, f32[16,16]{1,0:T(8,128)}, f32[16,16]{1,0:T(8,128)}, f32[16,16]{1,0:T(8,128)}, /*index=5*/f32[16,64,64]{2,1,0:T(8,128)S(1)}) fusion(f32[16,64,64]{2,1,0:T(8,128)S(1)} %multiply_reduce_fusion.40, f32[16,16]{1,0:T(8,128)S(1)} %copy-done.152, f32[64,64]{1,0:T(8,128)S(1)} %maximum_convert_fusion.4, ...), kind=kLoop, calls=%fused_computation.20.clone.1 | loop fusion | flops 27196160 | bytes 549888 | tf_op jit(solution)/shard_map/transpose(jvp())/while/body/eval_jaxpr/checkpoint/reduce_sum | solution.py:51
  2584.0 825.8 %while.71 = (s32[]{:T(128)}, f32[4,2048,16]{1,2,0:T(8,128)}, f32[4,16,16]{2,1,0:T(8,128)}, f32[4,16,16]{2,1,0:T(8,128)}, f32[4,16,16]{2,1,0:T(8,128)}, /*index=5...) while((s32[]{:T(128)}, f32[4,2048,16]{1,2,0:T(8,128)}, ...), condition=%wide.region_61.62_spmd, body=%wide.region_44.61_spmd.sunk | while | flops 125805952 | bytes 20896408 | solution.py:95
  2714.5 44.4 %fusion.647 = (f32[16,16]{1,0:T(8,128)}, f32[16,16]{1,0:T(8,128)}, f32[16,16]{1,0:T(8,128)}, f32[16,16]{1,0:T(8,128)}, f32[16,16]{1,0:T(8,128)}, /*index=5*/f32[16,64,64]{2,1,0:T(8,128)S(1)}) fusion(f32[16,64,64]{2,1,0:T(8,128)S(1)} %multiply_reduce_fusion.44, f32[16,16]{1,0:T(8,128)S(1)} %copy-done.155, f32[64,64]{1,0:T(8,128)S(1)} %maximum_convert_fusion.5, ...), kind=kLoop, calls=%fused_computation.272.clone.1 | loop fusion | flops 27196160 | bytes 549888 | tf_op jit(solution)/shard_map/transpose(jvp())/while/body/eval_jaxpr/checkpoint/reduce_sum | solution.py:51
  2914.1 44.4 %fusion.647 = (f32[16,16]{1,0:T(8,128)}, f32[16,16]{1,0:T(8,128)}, f32[16,16]{1,0:T(8,128)}, f32[16,16]{1,0:T(8,128)}, f32[16,16]{1,0:T(8,128)}, /*index=5*/f32[16,64,64]{2,1,0:T(8,128)S(1)}) fusion(f32[16,64,64]{2,1,0:T(8,128)S(1)} %multiply_reduce_fusion.44, f32[16,16]{1,0:T(8,128)S(1)} %copy-done.155, f32[64,64]{1,0:T(8,128)S(1)} %maximum_convert_fusion.5, ...), kind=kLoop, calls=%fused_computation.272.clone.1 | loop fusion | flops 27196160 | bytes 549888 | tf_op jit(solution)/shard_map/transpose(jvp())/while/body/eval_jaxpr/checkpoint/reduce_sum | solution.py:51
  3113.7 44.4 %fusion.647 = (f32[16,16]{1,0:T(8,128)}, f32[16,16]{1,0:T(8,128)}, f32[16,16]{1,0:T(8,128)}, f32[16,16]{1,0:T(8,128)}, f32[16,16]{1,0:T(8,128)}, /*index=5*/f32[16,64,64]{2,1,0:T(8,128)S(1)}) fusion(f32[16,64,64]{2,1,0:T(8,128)S(1)} %multiply_reduce_fusion.44, f32[16,16]{1,0:T(8,128)S(1)} %copy-done.155, f32[64,64]{1,0:T(8,128)S(1)} %maximum_convert_fusion.5, ...), kind=kLoop, calls=%fused_computation.272.clone.1 | loop fusion | flops 27196160 | bytes 549888 | tf_op jit(solution)/shard_map/transpose(jvp())/while/body/eval_jaxpr/checkpoint/reduce_sum | solution.py:51
  3313.3 44.4 %fusion.647 = (f32[16,16]{1,0:T(8,128)}, f32[16,16]{1,0:T(8,128)}, f32[16,16]{1,0:T(8,128)}, f32[16,16]{1,0:T(8,128)}, f32[16,16]{1,0:T(8,128)}, /*index=5*/f32[16,64,64]{2,1,0:T(8,128)S(1)}) fusion(f32[16,64,64]{2,1,0:T(8,128)S(1)} %multiply_reduce_fusion.44, f32[16,16]{1,0:T(8,128)S(1)} %copy-done.155, f32[64,64]{1,0:T(8,128)S(1)} %maximum_convert_fusion.5, ...), kind=kLoop, calls=%fused_computation.272.clone.1 | loop fusion | flops 27196160 | bytes 549888 | tf_op jit(solution)/shard_map/transpose(jvp())/while/body/eval_jaxpr/checkpoint/reduce_sum | solution.py:51
  3542.0 70.2 %all-reduce.261.cloned.1.call-done = (f32[256,2048]{1,0:T(8,128)}, f32[256,2048]{1,0:T(8,128)}) async-done(((f32[256,2048]{1,0:T(8,128)}, f32[256,2048]{1,0:T(8,128)}), (f32[256,2048]{1,0:T(8,128)}, f32[256,2048]{1,0:T(8,128)})) %all-reduce.261.cloned.1.call-update) | async-done | bytes 4194320 | tf_op jit(solution)/shard_map/psum | solution.py:121
  3649.1 27.6 reduce-scatter.19.cloned.1.call-done
  3676.8 65.1 %reduce-scatter.17.cloned.1.call-done = bf16[256,3,512]{2,0,1:T(8,128)(2,1)} async-done(((bf16[2048,3,512]{2,0,1:T(8,128)(2,1)}), bf16[256,3,512]{2,0,1:T(8,128)(2,1)}) %reduce-scatter.17.cloned.1.call-update) | async-done | bytes 786448 | tf_op jit(solution)/shard_map/reduce_scatter | solution.py:315
  (4286 shorter events, 2270.4 us)
Async XLA Ops:
  7.2 51.1 %all-gather.12.cloned.1.call-start = ((), (), s32[]{:S(2)}) async-start(), calls=%async_computation.20 | async-start | bytes 2621440 | tf_op jit(solution)/shard_map/all_gather | solution.py:171
  7.9 96.5 %all-gather.14.cloned.1.call-start = ((), (), s32[]{:S(2)}) async-start(), calls=%async_computation.21 | async-start | bytes 7077888 | tf_op jit(solution)/shard_map/all_gather | solution.py:198
  8.7 1155.9 %all-gather.16.cloned.1.call-start = ((), (), s32[]{:S(2)}) async-start(), calls=%async_computation.22 | async-start | bytes 2359296 | tf_op jit(solution)/shard_map/all_gather | solution.py:199
  109.3 12.7 collective-permute-start
  114.5 7.4 collective-permute-start.1
  129.3 10.3 all-to-all-start
  139.6 518.4 %all-to-all-start.2 = ((bf16[256,8,64]{0,2,1:T(8,128)(2,1)}), bf16[256,8,64]{0,2,1:T(8,128)(2,1)}, u32[]{:S(2)}, u32[]{:S(2)}) async-start(bf16[256,8,64]{0,2,1:T(8,128)(2,1)} %bitcast.77), calls=%async_computation.3 | async-start | bytes 524288 | tf_op jit(solution)/shard_map/all_to_all | solution.py:125
  1151.4 10.3 all-to-all-start.1
  1154.9 170.2 %all-reduce.265.cloned.1.call-start = ((), (), s32[]{:S(2)}) async-start(), calls=%async_computation.41 | async-start | bytes 8388608 | tf_op jit(solution)/shard_map/psum | solution.py:121
  1170.4 198.9 %all-gather.18.cloned.1.call-start = ((), (), s32[]{:S(2)}) async-start(), calls=%async_computation.23 | async-start | bytes 6488064 | tf_op jit(solution)/shard_map/all_gather | solution.py:200
  1171.0 243.5 %all-gather.20.cloned.1.call-start = ((), (), s32[]{:S(2)}) async-start(), calls=%async_computation.24 | async-start | bytes 6488064 | tf_op jit(solution)/shard_map/all_gather | solution.py:201
  1171.6 290.6 %all-gather.24.cloned.1.call-start = ((), (), s32[]{:S(2)}) async-start(), calls=%async_computation.28 | async-start | bytes 2621440 | tf_op jit(solution)/shard_map/all_gather | solution.py:172
  1172.3 335.0 %all-gather.22.cloned.1.call-start = ((), (), s32[]{:S(2)}) async-start(), calls=%async_computation.25 | async-start | bytes 6488064 | tf_op jit(solution)/shard_map/all_gather | solution.py:202
  1173.1 514.6 %all-reduce.263.cloned.1.call-start = ((), (), s32[]{:S(2)}) async-start(), calls=%async_computation.40 | async-start | bytes 8388608 | tf_op jit(solution)/shard_map/psum | solution.py:121
  1532.1 1941.4 %reduce-scatter.15.cloned.1.call-start = ((), (), s32[]{:S(2)}) async-start(), calls=%async_computation.27 | async-start | bytes 1310720 | tf_op jit(solution)/shard_map/reduce_scatter | solution.py:246
  1537.8 1936.9 %reduce-scatter.13.cloned.1.call-start = ((), (), s32[]{:S(2)}) async-start(), calls=%async_computation.26 | async-start | bytes 1310720 | tf_op jit(solution)/shard_map/reduce_scatter | solution.py:246
  1543.7 1988.6 %reduce-scatter.23.cloned.1.call-start = ((), (), s32[]{:S(2)}) async-start(), calls=%async_computation.32 | async-start | bytes 2359296 | tf_op jit(solution)/shard_map/reduce_scatter | solution.py:318
  1698.9 1833.4 %reduce-scatter.21.cloned.1.call-start = ((), (), s32[]{:S(2)}) async-start(), calls=%async_computation.31 | async-start | bytes 2359296 | tf_op jit(solution)/shard_map/reduce_scatter | solution.py:318
  1702.6 1831.6 %reduce-scatter.27.cloned.1.call-start = ((), (), s32[]{:S(2)}) async-start(), calls=%async_computation.34 | async-start | bytes 6488064 | tf_op jit(solution)/shard_map/reduce_scatter | solution.py:321
  1708.3 1825.9 %reduce-scatter.25.cloned.1.call-start = ((), (), s32[]{:S(2)}) async-start(), calls=%async_computation.33 | async-start | bytes 6488064 | tf_op jit(solution)/shard_map/reduce_scatter | solution.py:321
  1713.8 1822.9 %reduce-scatter.31.cloned.1.call-start = ((), (), s32[]{:S(2)}) async-start(), calls=%async_computation.36 | async-start | bytes 6488064 | tf_op jit(solution)/shard_map/reduce_scatter | solution.py:324
  1719.2 1817.5 %reduce-scatter.29.cloned.1.call-start = ((), (), s32[]{:S(2)}) async-start(), calls=%async_computation.35 | async-start | bytes 6488064 | tf_op jit(solution)/shard_map/reduce_scatter | solution.py:324
  1724.7 1814.7 %reduce-scatter.35.cloned.1.call-start = ((), (), s32[]{:S(2)}) async-start(), calls=%async_computation.38 | async-start | bytes 6488064 | tf_op jit(solution)/shard_map/reduce_scatter | solution.py:327
  1730.5 1808.8 %reduce-scatter.33.cloned.1.call-start = ((), (), s32[]{:S(2)}) async-start(), calls=%async_computation.37 | async-start | bytes 6488064 | tf_op jit(solution)/shard_map/reduce_scatter | solution.py:327
  1741.6 10.7 all-to-all-start.4
  1752.2 827.1 %all-to-all-start.6 = ((bf16[256,8,64]{0,2,1:T(8,128)(2,1)}), bf16[256,8,64]{0,2,1:T(8,128)(2,1)}, u32[]{:S(2)}, u32[]{:S(2)}) async-start(bf16[256,8,64]{0,2,1:T(8,128)(2,1)} %bitcast.101), calls=%async_computation.8 | async-start | bytes 524288 | tf_op jit(solution)/shard_map/all_to_all | solution.py:125
  3425.2 11.1 all-to-all-start.5
  3429.4 182.8 %all-reduce.261.cloned.1.call-start = ((), (), s32[]{:S(2)}) async-start(), calls=%async_computation.39 | async-start | bytes 8388608 | tf_op jit(solution)/shard_map/psum | solution.py:121
  3444.6 5.6 collective-permute-start.3
  3448.6 5.5 collective-permute-start.2
  3457.3 219.5 %reduce-scatter.19.cloned.1.call-start = ((), (), s32[]{:S(2)}) async-start(), calls=%async_computation.30 | async-start | bytes 7077888 | tf_op jit(solution)/shard_map/reduce_scatter | solution.py:315
  3464.9 277.0 %reduce-scatter.17.cloned.1.call-start = ((), (), s32[]{:S(2)}) async-start(), calls=%async_computation.29 | async-start | bytes 7077888 | tf_op jit(solution)/shard_map/reduce_scatter | solution.py:315
  (803 other events, 4914.3 us)
Sparse Core Ops, SparseCore 0:
  9.6 48.6 all-gather.11
  60.2 44.2 all-gather.13
  106.3 28.1 all-gather.15
  1170.5 154.4 all-reduce.264
  1326.9 42.3 all-gather.17
  1371.2 43.3 all-gather.19
  1416.2 45.9 all-gather.23
  1464.2 43.0 all-gather.21
  1532.2 155.3 all-reduce.262
  1690.4 26.1 reduce-scatter.14
  1719.5 25.7 reduce-scatter.12
  1748.5 39.8 reduce-scatter.22
  1792.1 41.2 reduce-scatter.20
  1836.7 59.0 reduce-scatter.26
  1899.4 59.0 reduce-scatter.24
  1961.8 59.0 reduce-scatter.30
  2024.5 59.0 reduce-scatter.28
  2086.9 59.0 reduce-scatter.34
  2149.8 59.0 reduce-scatter.32
  3457.4 154.7 all-reduce.260
  3616.0 60.7 reduce-scatter.18
  3680.2 61.7 reduce-scatter.16
where the time goes:
time: 3800 us; the launch traced here: 3750 us
  local copies, waits for them, and re-layouts  1230 us (32%)
  other arithmetic  1030 us (27%)
  waiting for transfers between devices  727 us (19%)
  matrix products  507 us (13%)
  loops' own time  117 us (3%)
  blocking collectives  96.5 us (3%)
    pad x608, local copies, waits for them, and re-layouts, conv_group(): lax.associative_scan(chain_step, (carry_re, carry_im, end_re, end_im), ax...  814 us
    psum x3, waiting for transfers between devices, row_total(): return lax.psum(partial_rows, 'fsdp')  366 us
    reduce_sum x8, other arithmetic, conv_group(): res_imag[:, :, None, None] * jnp.sin(angles[:, :, None, None] * lags)  355 us
    dot_general x16, matrix products, conv_group(): inner = jnp.einsum('bgts,bsg->btg', masked, blocks, precision=highest)  317 us
    reduce_sum x8, other arithmetic, conv_group(): toeplitz = jnp.sum(kernel, axis=1)  264 us
    slice x464, local copies, waits for them, and re-layouts, conv_group(): lax.associative_scan(chain_step, (carry_re, carry_im, end_re, end_im), ax...  184 us
    another operation x4, loops' own time, long_conv(): lax.map(jax.checkpoint(per_group), (stacked, rates.reshape(folds, group,...  117 us
    reduce_scatter x2, waiting for transfers between devices, on_device(): lax.psum_scatter(grad_in.astype(jnp.bfloat16), 'seq', scatter_dimension=0...  92.8 us

commit v1 on v0

v1 whole, which is shorter than its diff:
```python
import functools

import jax
import jax.numpy as jnp
from jax import lax
from jax.experimental import pallas as pl
from jax.experimental.pallas import tpu as pltpu
from jax.sharding import PartitionSpec as P

norm_eps = 1e-05
half_modes = 8
f32 = jnp.float32
bf16 = jnp.bfloat16


def widen(src_ref, dst_ref, count):
    total, chans = src_ref.shape[0], src_ref.shape[1] // count
    rows = min(256, total)

    def body(block, _):
        base = pl.multiple_of(block * rows, rows)
        part = src_ref[pl.ds(base, rows), :].astype(f32)
        for m in range(count):
            own = part[:, m * chans : (m + 1) * chans]
            dst_ref[m, pl.ds(base, rows), :] = jnp.concatenate([own, own], axis=1)
        return 0

    lax.fori_loop(0, total // rows, body, 0)


def narrow(src_ref, direct_ref, skip, dst_ref, count):
    total, chans = direct_ref.shape[0], direct_ref.shape[1] // count
    rows = min(256, total)

    def body(block, _):
        base = pl.multiple_of(block * rows, rows)
        parts = []
        for m in range(count):
            wide = src_ref[m, pl.ds(base, rows), :]
            parts.append(wide[:, :chans] + wide[:, chans:])
        summed = jnp.concatenate(parts, axis=1) if count > 1 else parts[0]
        direct = direct_ref[pl.ds(base, rows), :].astype(f32)
        dst_ref[pl.ds(base, rows), :] = (summed + skip * direct).astype(bf16)
        return 0

    lax.fori_loop(0, total // rows, body, 0)


def scan_kernel(count, step, keep_ref, u_ref, par_ref, skip_ref, y_ref, u_wide, y_wide):
    total = u_ref.shape[0]
    turn_re, turn_im, res_re, res_im = (par_ref[i] for i in range(4))
    widen(u_ref, u_wide, count)

    def body(block, states):
        states = list(states)
        base = pl.multiple_of(block * step, step)
        for i in range(step):
            for m in range(count):
                x_re, x_im = states[m]
                keep = keep_ref[m, base + i]
                mul_re, mul_im = turn_re * keep, turn_im * keep
                new_re = mul_re * x_re + (u_wide[m, pl.ds(base + i, 1), :] - mul_im * x_im)
                new_im = mul_re * x_im + mul_im * x_re
                y_wide[m, pl.ds(base + i, 1), :] = jnp.sum(
                    res_re * new_re - res_im * new_im, axis=0, keepdims=True
                )
                states[m] = (new_re, new_im)
        return tuple(states)

    zero = jnp.zeros(turn_re.shape, f32)
    lax.fori_loop(0, total // step, body, tuple((zero, zero) for _ in range(count)))
    narrow(y_wide, u_ref, skip_ref[...], y_ref, count)


def back_kernel(
    count, step, keep_ref, u_ref, g_ref, par_ref, skip_ref, d_ref, sums_ref, skip_sum_ref, u_wide, g_wide, d_wide
):
    total = u_ref.shape[0]
    blocks = total // step
    turn_re, turn_im, res_re, res_im = (par_ref[i] for i in range(4))
    zero = jnp.zeros(turn_re.shape, f32)
    widen(u_ref, u_wide, count)
    widen(g_ref, g_wide, count)

    def body(block, carry):
        ahead, behind, sums = list(carry[0]), list(carry[1]), carry[2]
        base = pl.multiple_of(block * step, step)
        rear = pl.multiple_of((blocks - 1 - block) * step, step)
        for i in range(step):
            j = step - 1 - i
            for m in range(count):
                x_re, x_im, w_re, w_im = ahead[m]
                keep = keep_ref[m, base + i]
                mul_re, mul_im = turn_re * keep, turn_im * keep
                sum_re, sum_im = w_re + x_re, w_im + x_im
                w_re, w_im = mul_re * sum_re - mul_im * sum_im, mul_re * sum_im + mul_im * sum_re
                x_re, x_im = (
                    mul_re * x_re + (u_wide[m, pl.ds(base + i, 1), :] - mul_im * x_im),
                    mul_re * x_im + mul_im * x_re,
                )
                ahead[m] = (x_re, x_im, w_re, w_im)
                cot = g_wide[m, pl.ds(base + i, 1), :]
                sums = (
                    sums[0] + cot * x_re,
                    sums[1] + cot * x_im,
                    sums[2] + cot * w_re,
                    sums[3] + cot * w_im,
                )
                z_re, z_im, keep = behind[m]
                mul_re, mul_im = turn_re * keep, turn_im * keep
                z_re, z_im = (
                    mul_re * z_re + (g_wide[m, pl.ds(rear + j, 1), :] - mul_im * z_im),
                    mul_re * z_im + mul_im * z_re,
                )
                behind[m] = (z_re, z_im, keep_ref[m, rear + j])
                d_wide[m, pl.ds(rear + j, 1), :] = jnp.sum(res_re * z_re - res_im * z_im, axis=0, keepdims=True)
        return tuple(ahead), tuple(behind), sums

    start = (
        tuple((zero, zero, zero, zero) for _ in range(count)),
        tuple((zero, zero, jnp.float32(0)) for _ in range(count)),
        (zero, zero, zero, zero),
    )
    _, _, (g_re, g_im, lag_re, lag_im) = lax.fori_loop(0, blocks, body, start)
    sums_ref[0] = res_im * lag_im - res_re * lag_re
    sums_ref[1] = zero - (res_re * lag_im + res_im * lag_re)
    sums_ref[2] = g_re
    sums_ref[3] = zero - g_im
    narrow(d_wide, g_ref, skip_ref[...], d_ref, count)
    skip_sum_ref[...] = jnp.sum(u_ref[...].astype(f32) * g_ref[...].astype(f32), axis=0, keepdims=True)


def in_vmem():
    return pl.BlockSpec(memory_space=pltpu.VMEM)


def long_conv(u, keep, params, skips, count):
    total, width = u.shape
    return pl.pallas_call(
        functools.partial(scan_kernel, count, 16),
        out_shape=jax.ShapeDtypeStruct(u.shape, bf16),
        in_specs=[pl.BlockSpec(memory_space=pltpu.SMEM)] + [in_vmem()] * 3,
        out_specs=in_vmem(),
        scratch_shapes=[pltpu.VMEM((count, total, 2 * width // count), f32)] * 2,
        compiler_params=pltpu.CompilerParams(vmem_limit_bytes=48 << 20),
    )(keep, u, params, skips)


def long_conv_back(u, g, keep, params, skips, count):
    total, width = u.shape
    return pl.pallas_call(
        functools.partial(back_kernel, count, 16),
        out_shape=(
            jax.ShapeDtypeStruct(u.shape, bf16),
            jax.ShapeDtypeStruct(params.shape, f32),
            jax.ShapeDtypeStruct((1, width), f32),
        ),
        in_specs=[pl.BlockSpec(memory_space=pltpu.SMEM)] + [in_vmem()] * 4,
        out_specs=(in_vmem(),) * 3,
        scratch_shapes=[pltpu.VMEM((count, total, 2 * width // count), f32)] * 3,
        compiler_params=pltpu.CompilerParams(vmem_limit_bytes=48 << 20),
    )(keep, u, g, params, skips)


def pack_modes(rates, angles, res_re, res_im):
    def on_lanes(part):
        turned = part.T
        return jnp.concatenate([turned[:half_modes], turned[half_modes:]], axis=1)

    fading = jnp.exp(-rates)
    return jnp.stack(
        [on_lanes(part) for part in (fading * jnp.cos(angles), fading * jnp.sin(angles), res_re, res_im)]
    )


def shifted(array, axis, by):
    size = lax.axis_size(axis)
    pairs = [(i, i + by) for i in range(size) if 0 <= i + by < size]
    return lax.ppermute(array, axis, pairs)


def places_of(doc_lens, total):
    tokens = jnp.arange(total, dtype=jnp.int32)
    starts = jnp.cumsum(doc_lens, dtype=jnp.int32) - doc_lens
    begins = jnp.max(jnp.where(starts[None, :] <= tokens[:, None], starts[None, :], 0), axis=1)
    return tokens - begins


def dot_rows(left, right):
    return lax.dot_general(left, right, (((1,), (1,)), ((), ())), preferred_element_type=f32)


def dot_tokens(left, right):
    return lax.dot_general(left, right, (((0,), (0,)), ((), ())), preferred_element_type=f32)


def dot(left, right):
    return jnp.dot(left, right, preferred_element_type=f32)


def gather_share(share):
    return lax.all_gather(share, "fsdp", axis=1, tiled=True)


def scatter_share(partial_sums):
    return lax.psum_scatter(partial_sums.astype(bf16), "fsdp", scatter_dimension=1, tiled=True).astype(f32)


def gather_weight(shard):
    return lax.all_gather(shard, "seq", axis=0, tiled=True)


def scatter_weight(grad):
    return lax.psum_scatter(grad.astype(bf16), "seq", scatter_dimension=0, tiled=True).astype(f32)


def to_channels(token_side, batches):
    rows, chans = token_side.shape[0] // batches, token_side.shape[1]
    count = lax.axis_size("seq")
    part = chans // count
    pieces = token_side.reshape(batches, rows, count, part).transpose(2, 1, 0, 3)
    sent = lax.all_to_all(pieces.reshape(count, rows, batches * part), "seq", split_axis=0, concat_axis=0)
    return sent.reshape(count * rows, batches * part)


def to_tokens(channel_side, batches):
    total, width = channel_side.shape
    count = lax.axis_size("seq")
    rows, part = total // count, width // batches
    sent = lax.all_to_all(channel_side.reshape(count, rows, width), "seq", split_axis=0, concat_axis=0)
    return sent.reshape(count, rows, batches, part).transpose(2, 1, 0, 3).reshape(batches * rows, count * part)


def on_device(
    hidden_in,
    out_cot,
    doc_lengths,
    mixer_gain,
    in_proj,
    short_filter,
    decay_rate,
    mode_angle,
    residue_re,
    residue_im,
    skip_gain,
    out_proj,
    feed_gain,
    gate_proj,
    up_proj,
    down_proj,
):
    batches, rows, share = hidden_in.shape
    tokens = batches * rows
    width = mixer_gain.shape[0]
    seq_count = lax.axis_size("seq")
    seq_rank = lax.axis_index("seq")
    fsdp_rank = lax.axis_index("fsdp")
    total = rows * seq_count
    chan_here = share // seq_count
    d_rows = in_proj.shape[0]

    x_share = hidden_in.reshape(tokens, share)
    cot_share = out_cot.reshape(tokens, share)
    x_all = gather_share(x_share).astype(f32)
    w_in = gather_weight(in_proj.reshape(d_rows, 3 * share))
    w_out = gather_weight(out_proj.T)
    w_gate = gather_weight(gate_proj)
    w_up = gather_weight(up_proj)
    w_down = gather_weight(down_proj.T)
    cot_all = gather_share(cot_share)

    places = jnp.stack([places_of(doc_lengths[m], total) for m in range(batches)])
    keep = (places > 0).astype(f32)
    places_here = lax.dynamic_slice_in_dim(places, seq_rank * rows, rows, 1)
    masks = [(places_here >= lag).astype(f32)[:, :, None] for lag in range(3)]
    taps = short_filter.reshape(3, 3 * share)

    def own_channels(part):
        return lax.dynamic_slice_in_dim(part, seq_rank * chan_here, chan_here, 0)

    modes = pack_modes(*(own_channels(part) for part in (decay_rate, mode_angle, residue_re, residue_im)))
    skips = jnp.tile(own_channels(skip_gain), batches)[None]

    scale_one = lax.rsqrt(jnp.mean(x_all * x_all, axis=-1, keepdims=True) + norm_eps)
    unit_one = x_all * scale_one
    normed_one = (unit_one * mixer_gain).astype(bf16)
    project = dot(normed_one, w_in).reshape(batches, rows, 3 * share)
    extended = jnp.concatenate([shifted(project[:, -2:], "seq", 1), project], axis=1)
    lagged = [extended[:, 2 - lag : 2 - lag + rows] for lag in range(3)]
    conv = sum(taps[lag] * masks[lag] * lagged[lag] for lag in range(3)).reshape(tokens, 3 * share)
    gate_one, gate_two, values = (conv[:, j * share : (j + 1) * share] for j in range(3))
    channel_in = to_channels((gate_two * values).astype(bf16), batches)
    channel_out = long_conv(channel_in, keep, modes, skips, batches)
    mixed = to_tokens(channel_out, batches).astype(f32)
    gated = (gate_one * mixed).astype(bf16)
    stream = x_share.astype(f32) + scatter_share(dot_rows(gated, w_out))
    stream_all = gather_share(stream.astype(bf16)).astype(f32)
    scale_two = lax.rsqrt(jnp.mean(stream_all * stream_all, axis=-1, keepdims=True) + norm_eps)
    unit_two = stream_all * scale_two
    normed_two = (unit_two * feed_gain).astype(bf16)
    gate_pre = dot(normed_two, w_gate)
    up_pre = dot(normed_two, w_up)
    sigmoid = jax.nn.sigmoid(gate_pre)
    activated = gate_pre * sigmoid
    hidden = (activated * up_pre).astype(bf16)
    block_out = stream + scatter_share(dot_rows(hidden, w_down))

    d_hidden = dot(cot_all, w_down)
    d_gate = (d_hidden * up_pre * sigmoid * (1.0 + gate_pre * (1.0 - sigmoid))).astype(bf16)
    d_up = (d_hidden * activated).astype(bf16)
    grad_down = dot_tokens(cot_all, hidden)
    grad_gate = dot_tokens(normed_two, d_gate)
    grad_up = dot_tokens(normed_two, d_up)
    part_two = dot_rows(d_gate, w_gate) + dot_rows(d_up, w_up)
    along_two = lax.psum(
        jnp.sum(d_gate.astype(f32) * gate_pre + d_up.astype(f32) * up_pre, axis=-1, keepdims=True), "fsdp"
    )
    feed_gain_part = jnp.sum(unit_two * part_two, axis=0)

    def own_features(part):
        return lax.dynamic_slice_in_dim(part, fsdp_rank * share, share, 0)

    d_stream = (
        cot_share.astype(f32)
        + scale_two * own_features(feed_gain) * scatter_share(part_two)
        - stream * (scale_two * scale_two * along_two / width)
    )
    d_mix = gather_share(d_stream.astype(bf16))

    grad_out = dot_tokens(d_mix, gated)
    d_gated = dot(d_mix, w_out)
    d_gate_one = d_gated * mixed
    back_in = to_channels((d_gated * gate_one).astype(bf16), batches)
    back_out, mode_sums, skip_sums = long_conv_back(channel_in, back_in, keep, modes, skips, batches)
    d_product = to_tokens(back_out, batches).astype(f32)
    d_conv = jnp.concatenate([d_gate_one, d_product * values, d_product * gate_two], axis=1)
    d_conv = d_conv.reshape(batches, rows, 3 * share)
    short_part = jnp.stack([jnp.sum(masks[lag] * lagged[lag] * d_conv, axis=(0, 1)) for lag in range(3)])
    spread = sum(
        jnp.pad(taps[lag] * masks[lag] * d_conv, ((0, 0), (2 - lag, lag), (0, 0))) for lag in range(3)
    )
    returned = shifted(spread[:, :2], "seq", -1)
    d_project = spread[:, 2:] + jnp.pad(returned, ((0, 0), (rows - 2, 0), (0, 0)))
    d_project = d_project.astype(bf16).reshape(tokens, 3 * share)
    along_one = lax.psum(
        jnp.sum(d_project.astype(f32) * project.reshape(tokens, 3 * share), axis=-1, keepdims=True), "fsdp"
    )
    grad_in = dot_tokens(normed_one, d_project)
    part_one = dot_rows(d_project, w_in)
    mixer_gain_part = jnp.sum(unit_one * part_one, axis=0)
    d_x = (
        d_stream
        + scale_one * own_features(mixer_gain) * scatter_share(part_one)
        - x_share.astype(f32) * (scale_one * scale_one * along_one / width)
    )

    in_grad = scatter_weight(grad_in).reshape(d_rows, 3, share)
    out_grad = scatter_weight(grad_out).T
    gate_grad = scatter_weight(grad_gate)
    up_grad = scatter_weight(grad_up)
    down_grad = scatter_weight(grad_down).T
    gains = lax.psum(jnp.stack([mixer_gain_part, feed_gain_part]), ("fsdp", "seq"))
    short_grad = lax.psum(short_part, "seq").reshape(3, 3, share)
    skip_own = jnp.sum(skip_sums.reshape(batches, chan_here), axis=0)
    skip_rows = jnp.zeros((half_modes, 2 * chan_here), f32).at[0, :chan_here].set(skip_own)
    filters = jnp.concatenate([mode_sums, skip_rows[None]], axis=0)
    filters = lax.all_gather(filters, "seq", axis=0)
    by_chan = filters.reshape(seq_count, 5, half_modes, 2, chan_here).transpose(1, 0, 4, 3, 2)
    by_chan = by_chan.reshape(5, share, 2 * half_modes)
    return (
        block_out.astype(bf16).reshape(hidden_in.shape),
        d_x.reshape(hidden_in.shape),
        gains[0],
        in_grad,
        short_grad,
        by_chan[0],
        by_chan[1],
        by_chan[2],
        by_chan[3],
        by_chan[4, :, 0],
        out_grad,
        gains[1],
        gate_grad,
        up_grad,
        down_grad,
    )


def solution(mesh):
    tokens = P(None, "seq", "fsdp")
    chan_rows = P("fsdp", None)
    d_rows = P("seq", "fsdp")
    d_cols = P("fsdp", "seq")
    in_specs = (
        tokens,
        tokens,
        P(),
        P(),
        P("seq", None, "fsdp"),
        P(None, None, "fsdp"),
        chan_rows,
        chan_rows,
        chan_rows,
        chan_rows,
        P("fsdp"),
        d_cols,
        P(),
        d_rows,
        d_rows,
        d_cols,
    )
    out_specs = (
        tokens,
        tokens,
        P(),
        P("seq", None, "fsdp"),
        P(None, None, "fsdp"),
        chan_rows,
        chan_rows,
        chan_rows,
        chan_rows,
        P("fsdp"),
        d_cols,
        P(),
        d_rows,
        d_rows,
        d_cols,
    )
    return jax.shard_map(on_device, mesh=mesh, in_specs=in_specs, out_specs=out_specs, check_vma=False)
```

time: 3800 us -> 969 us (0.26); the launches traced: 3750 us -> 961 us
  local copies, waits for them, and re-layouts: 1230 us -> 30.6 us
  other arithmetic: 1030 us -> 37.2 us
  matrix products: 507 us -> 98.2 us
  waiting for transfers between devices: 727 us -> 590 us
  loops' own time: 117 us -> 0 us
  Pallas kernels: 0 us -> 45 us
  blocking collectives: 96.5 us -> 135 us
    pad x608 -> x0, local copies, waits for them, and re-layouts: 814 us -> none  [conv_group(): lax.associative_scan(chain_step, (carry_re, carry_im, end_re, end_im), ax...]
    reduce_sum x58 -> x4, other arithmetic: 707 us -> 7.77 us  [the longest x1 3.6 us: on_device(): jnp.sum(masks[lag] * lagged[lag] * d_conv, axis=(0, 1))]
    dot_general x158 -> x15, matrix products: 507 us -> 98.2 us  [the longest x5 38 us: dot(): return jnp.dot(left, right, preferred_element_type=f32)]
    psum x3 -> x0, waiting for transfers between devices: 366 us -> none  [row_total(): return lax.psum(partial_rows, 'fsdp')]
    slice x551 -> x9, local copies, waits for them, and re-layouts: 222 us -> 1.25 us  [the longest x1 0.61 us: on_device(): gains[1]]
    reduce_scatter x12 -> x9, waiting for transfers between devices: 92.9 us -> 252 us  [the longest x4 164 us: scatter_share(): lax.psum_scatter(partial_sums.astype(bf16), 'fsdp', scatter_dimension=1,...]
    another operation x4 -> x0, loops' own time: 117 us -> none  [long_conv(): lax.map(jax.checkpoint(per_group), (stacked, rates.reshape(folds, group,...]
    add x325 -> x2, other arithmetic: 100 us -> 2.59 us  [the longest x1 1.43 us: on_device(): sum((taps[lag] * masks[lag] * lagged[lag] for lag in range(3)))]
where the time goes in v1:
time: 969 us; the launch traced here: 961 us
  waiting for transfers between devices  590 us (61%)
  blocking collectives  135 us (14%)
  matrix products  98.2 us (10%)
  Pallas kernels  45 us (5%)
  other arithmetic  37.2 us (4%)
  local copies, waits for them, and re-layouts  30.6 us (3%)
  between operations  15.1 us (2%)
  starting transfers between devices  10.2 us (1%)
    all_gather x5, waiting for transfers between devices, gather_weight(): return lax.all_gather(shard, 'seq', axis=0, tiled=True)  170 us
    reduce_scatter x4, waiting for transfers between devices, scatter_share(): lax.psum_scatter(partial_sums.astype(bf16), 'fsdp', scatter_dimension=1,...  164 us
    all_gather x4, waiting for transfers between devices, gather_share(): return lax.all_gather(share, 'fsdp', axis=1, tiled=True)  148 us
    reduce_scatter x5, waiting for transfers between devices, scatter_weight(): lax.psum_scatter(grad.astype(bf16), 'seq', scatter_dimension=0, tiled=True)  88.3 us
    psum x1, blocking collectives, on_device(): lax.psum(jnp.stack([mixer_gain_part, feed_gain_part]), ('fsdp', 'seq'))  39.9 us
    dot_general x5, matrix products, dot(): return jnp.dot(left, right, preferred_element_type=f32)  38 us
    dot_general x5, matrix products, dot_tokens(): lax.dot_general(left, right, (((0,), (0,)), ((), ())), preferred_element_...  33.8 us
    pallas_call x1, Pallas kernels, long_conv_back(): pl.pallas_call(functools.partial(back_kernel, count, 16), out_shape=(jax....  29.9 us
  transfers between devices with their start and end apart: 21, of which 17 were waited for; matrix products, arithmetic and copies ran while one was open for 14% of the time, Pallas kernels for 5%

profile of v1, /device:TPU:0, one launch (start us, length us, event | category | flops | bytes accessed | tf_op | source)
XLA Modules:
  0.0 961.1 jit_solution(1713909991029459701)
XLA Ops:
  13.5 44.8 %all-gather.11.cloned.1.call-done = bf16[512,2048]{1,0:T(8,128)(2,1)} async-done(((bf16[512,512]{1,0:T(8,128)(2,1)}), bf16[512,2048]{1,0:T(8,128)(2,1)}) %all-gather.11.cloned.1.call-update) | async-done | bytes 2097168 | tf_op jit(solution)/shard_map/all_gather | solution.py:202
  60.4 45.8 %all-gather.13.cloned.1.call-done = bf16[2048,1536]{0,1:T(8,128)(2,1)} async-done(((bf16[256,1536]{0,1:T(8,128)(2,1)}), bf16[2048,1536]{0,1:T(8,128)(2,1)}) %all-gather.13.cloned.1.call-update) | async-done | bytes 6291472 | tf_op jit(solution)/shard_map/all_gather | solution.py:210
  126.1 14.3 %all-to-all-done = bf16[8,256,128]{1,2,0:T(8,128)(2,1)S(1)} async-done(((bf16[8,256,128]{1,2,0:T(8,128)(2,1)}), bf16[8,256,128]{1,2,0:T(8,128)(2,1)S(1)}, u32[]{:S(2)}, u32[]{:S(2)}) %all-to-all-start) | async-done | bytes 524320 | tf_op jit(solution)/shard_map/all_to_all | solution.py:222
  140.7 15.1 %shard_map.271 = bf16[2048,128]{1,0:T(8,128)(2,1)S(1)} custom-call(f32[2,2048]{1,0:T(2,128)S(1)} %compare_convert_fusion.keep_ref, bf16[2048,128]{1,0:T(8,128)(2,1)S(1)} %bitcast.143, f32[4,8,128]{2,1,0:T(8,128)S(1)} %pad_maximum_fusion.3.par_ref, f32[1,128]{1,0:T(1,128)S(1)} %broadcast_in_dim_tile.3.skip_ref), custom_call_target="tpu_custom_call" | custom-call | tf_op jit(solution)/shard_map/pallas_call | solution.py:139
  156.0 12.2 %all_to_all.20 = bf16[8,256,128]{1,2,0:T(8,128)(2,1)S(1)} all-to-all(bf16[8,256,128]{1,2,0:T(8,128)(2,1)S(1)} %copy.89), channel_id=1, replica_groups=mesh['fsdp'=4,'seq'=8] {'seq'}, dimensions={0} | all-to-all | bytes 1048576 | tf_op jit(solution)/shard_map/all_to_all | solution.py:230
  180.1 42.1 %reduce-scatter.10.cloned.1.call-done = bf16[512,512]{1,0:T(8,128)(2,1)} async-done(((bf16[512,2048]{1,0:T(8,128)(2,1)}), bf16[512,512]{1,0:T(8,128)(2,1)}) %reduce-scatter.10.cloned.1.call-update) | async-done | bytes 524304 | tf_op jit(solution)/shard_map/reduce_scatter | solution.py:206
  225.9 43.0 %all-gather.25.cloned.1.call-done = bf16[512,2048]{1,0:T(8,128)(2,1)} async-done(((bf16[512,512]{1,0:T(8,128)(2,1)}), bf16[512,2048]{1,0:T(8,128)(2,1)}) %all-gather.25.cloned.1.call-update) | async-done | bytes 2097168 | tf_op jit(solution)/shard_map/all_gather | solution.py:202
  268.9 45.0 %all-gather.23.cloned.1.call-done = bf16[2048,1408]{0,1:T(8,128)(2,1)} async-done(((bf16[256,1408]{0,1:T(8,128)(2,1)}), bf16[2048,1408]{0,1:T(8,128)(2,1)}) %all-gather.23.cloned.1.call-update) | async-done | bytes 5767184 | tf_op jit(solution)/shard_map/all_gather | solution.py:210
  313.9 8.3 fusion.45
  322.2 39.9 %all-gather.17.cloned.1.call-done = bf16[512,2048]{1,0:T(8,128)(2,1)} async-done(((bf16[512,512]{1,0:T(8,128)(2,1)}), bf16[512,2048]{1,0:T(8,128)(2,1)}) %all-gather.17.cloned.1.call-update) | async-done | bytes 2097168 | tf_op jit(solution)/shard_map/all_gather | solution.py:202
  364.2 42.0 %all-gather.19.cloned.1.call-done = bf16[2048,1408]{1,0:T(8,128)(2,1)} async-done(((bf16[256,1408]{1,0:T(8,128)(2,1)}), bf16[2048,1408]{1,0:T(8,128)(2,1)}) %all-gather.19.cloned.1.call-update) | async-done | bytes 5767184 | tf_op jit(solution)/shard_map/all_gather | solution.py:210
  406.2 8.5 fusion.33
  414.7 36.9 %all-gather.21.cloned.1.call-done = bf16[2048,1408]{1,0:T(8,128)(2,1)} async-done(((bf16[256,1408]{1,0:T(8,128)(2,1)}), bf16[2048,1408]{1,0:T(8,128)(2,1)}) %all-gather.21.cloned.1.call-update) | async-done | bytes 5767184 | tf_op jit(solution)/shard_map/all_gather | solution.py:210
  451.6 9.4 add_reduce_fusion
  470.9 11.7 %psum.28 = f32[512,1]{0,1:T(1,128)S(1)} all-reduce(f32[512,1]{0,1:T(1,128)S(1)} %bitcast.187), channel_id=1, replica_groups=mesh['fsdp'=4,'seq'=8] {'fsdp'}, use_global_device_ids=true, to_apply=%region_10.11 | all-reduce | flops 512 | bytes 4096 | tf_op jit(solution)/shard_map/psum | solution.py:315
  482.6 32.3 %reduce-scatter.14.cloned.1.call-done = bf16[512,512]{1,0:T(8,128)(2,1)} async-done(((bf16[512,2048]{1,0:T(8,128)(2,1)}), bf16[512,512]{1,0:T(8,128)(2,1)}) %reduce-scatter.14.cloned.1.call-update) | async-done | bytes 524304 | tf_op jit(solution)/shard_map/reduce_scatter | solution.py:206
  517.7 8.0 convolution_convert_fusion.2
  527.3 6.9 convolution_convert_fusion.1
  542.2 20.4 %all-gather.27.cloned.1.call-done = bf16[512,2048]{1,0:T(8,128)(2,1)} async-done(((bf16[512,512]{1,0:T(8,128)(2,1)}), bf16[512,2048]{1,0:T(8,128)(2,1)}) %all-gather.27.cloned.1.call-update) | async-done | bytes 2097168 | tf_op jit(solution)/shard_map/all_gather | solution.py:202
  567.0 8.0 convolution_convert_fusion.6
  581.0 17.0 %all_to_all.21 = bf16[8,256,128]{1,2,0:T(8,128)(2,1)S(1)} all-to-all(bf16[8,256,128]{1,2,0:T(8,128)(2,1)S(1)} %bitcast.167), channel_id=1, replica_groups=mesh['fsdp'=4,'seq'=8] {'seq'}, dimensions={0} | all-to-all | bytes 1048576 | tf_op jit(solution)/shard_map/all_to_all | solution.py:222
  598.2 29.9 %shard_map.272 = (bf16[2048,128]{1,0:T(8,128)(2,1)S(1)}, f32[4,8,128]{2,1,0:T(8,128)S(1)}, f32[1,128]{1,0:T(1,128)S(1)}) custom-call(f32[2,2048]{1,0:T(2,128)S(1)} %compare_convert_fusion.keep_ref, bf16[2048,128]{1,0:T(8,128)(2,1)S(1)} %bitcast.144, bf16[2048,128]{1,0:T(8,128)(2,1)S(1)} %bitcast.145, f32[4,8,128]{2,1,0:T(8,128)S(1)} %pad_maximum_fusion.3.par_ref, ...), custom_call_target="tpu_custom_call" | custom-call | tf_op jit(solution)/shard_map/pallas_call | solution.py:151
  628.4 12.2 %all_to_all.22 = bf16[8,256,128]{1,2,0:T(8,128)(2,1)S(1)} all-to-all(bf16[8,256,128]{1,2,0:T(8,128)(2,1)S(1)} %copy.98), channel_id=1, replica_groups=mesh['fsdp'=4,'seq'=8] {'seq'}, dimensions={0} | all-to-all | bytes 1048576 | tf_op jit(solution)/shard_map/all_to_all | solution.py:230
  660.4 8.2 convolution_convert_fusion.3
  670.6 9.9 %all-gather = f32[40,8,128]{2,1,0:T(8,128)S(1)} all-gather(f32[5,8,128]{2,1,0:T(8,128)S(1)} %select_maximum_fusion), channel_id=2, replica_groups=mesh['fsdp'=4,'seq'=8] {'seq'}, dimensions={0}, use_global_device_ids=true | all-gather | bytes 184320 | tf_op jit(solution)/shard_map/all_gather | solution.py:367
  688.1 8.4 psum.29
  696.5 39.9 %psum.30 = f32[2,2048]{1,0:T(2,128)S(1)} all-reduce(f32[2,2048]{1,0:T(2,128)S(1)} %pad_maximum_fusion.4), channel_id=1, replica_groups=mesh['fsdp'=4,'seq'=8] {'fsdp','seq'}, use_global_device_ids=true, to_apply=%region_16.17 | all-reduce | flops 4096 | bytes 32768 | tf_op jit(solution)/shard_map/psum | solution.py:362
  736.4 24.0 %psum.31 = f32[3,3,512]{2,1,0:T(4,128)} all-reduce(f32[3,3,512]{2,1,0:T(4,128)S(1)} %reshape.278), channel_id=1, replica_groups=mesh['fsdp'=4,'seq'=8] {'seq'}, use_global_device_ids=true, to_apply=%region_21.22 | all-reduce | flops 4608 | bytes 36864 | tf_op jit(solution)/shard_map/psum | solution.py:363
  768.2 27.0 %reduce-scatter.20.cloned.1.call-done = bf16[256,512]{1,0:T(8,128)(2,1)} async-done(((bf16[2048,512]{1,0:T(8,128)(2,1)}), bf16[256,512]{1,0:T(8,128)(2,1)}) %reduce-scatter.20.cloned.1.call-update) | async-done | bytes 262160 | tf_op jit(solution)/shard_map/reduce_scatter | solution.py:214
  797.2 44.0 %reduce-scatter.12.cloned.1.call-done = bf16[512,512]{1,0:T(8,128)(2,1)} async-done(((bf16[512,2048]{1,0:T(8,128)(2,1)}), bf16[512,512]{1,0:T(8,128)(2,1)}) %reduce-scatter.12.cloned.1.call-update) | async-done | bytes 524304 | tf_op jit(solution)/shard_map/reduce_scatter | solution.py:206
  841.2 45.5 %reduce-scatter.16.cloned.1.call-done = bf16[512,512]{1,0:T(8,128)(2,1)} async-done(((bf16[512,2048]{1,0:T(8,128)(2,1)}), bf16[512,512]{1,0:T(8,128)(2,1)}) %reduce-scatter.16.cloned.1.call-update) | async-done | bytes 524304 | tf_op jit(solution)/shard_map/reduce_scatter | solution.py:206
  889.8 61.3 %reduce-scatter.18.cloned.1.call-done = bf16[256,1536]{1,0:T(8,128)(2,1)} async-done(((bf16[2048,1536]{1,0:T(8,128)(2,1)}), bf16[256,1536]{1,0:T(8,128)(2,1)}) %reduce-scatter.18.cloned.1.call-update) | async-done | bytes 786448 | tf_op jit(solution)/shard_map/reduce_scatter | solution.py:214
  (210 shorter events, 124.3 us)
Async XLA Ops:
  7.2 99.0 %copy-start.23 = (f32[2048]{0:T(1024)S(1)}, f32[2048]{0:T(1024)}, u32[]{:S(2)}) copy-start(f32[2048]{0:T(1024)} %param.21) | copy-start | bytes 24580
  7.2 51.1 %all-gather.11.cloned.1.call-start = ((), (), s32[]{:S(2)}) async-start(), calls=%async_computation.13 | async-start | bytes 2621440 | tf_op jit(solution)/shard_map/all_gather | solution.py:202
  7.9 98.2 %all-gather.13.cloned.1.call-start = ((), (), s32[]{:S(2)}) async-start(), calls=%async_computation.14 | async-start | bytes 7077888 | tf_op jit(solution)/shard_map/all_gather | solution.py:210
  10.3 164.1 %all-gather.15.cloned.1.call-start = ((), (), s32[]{:S(2)}) async-start(), calls=%async_computation.15 | async-start | bytes 2359296 | tf_op jit(solution)/shard_map/all_gather | solution.py:210
  112.4 3.0 collective-permute-start
  119.9 20.5 %all-to-all-start = ((bf16[8,256,128]{1,2,0:T(8,128)(2,1)}), bf16[8,256,128]{1,2,0:T(8,128)(2,1)S(1)}, u32[]{:S(2)}, u32[]{:S(2)}) async-start(bf16[8,256,128]{1,2,0:T(8,128)(2,1)} %bitcast.9), calls=%async_computation | async-start | bytes 1048576 | tf_op jit(solution)/shard_map/all_to_all | solution.py:222
  125.0 97.1 %reduce-scatter.10.cloned.1.call-start = ((), (), s32[]{:S(2)}) async-start(), calls=%async_computation.16 | async-start | bytes 2621440 | tf_op jit(solution)/shard_map/reduce_scatter | solution.py:206
  178.8 43.3 %copy-start.3 = (bf16[2,256,512]{2,1,0:T(8,128)(2,1)S(1)}, bf16[2,256,512]{2,1,0:T(8,128)(2,1)}, u32[]{:S(2)}) copy-start(bf16[2,256,512]{2,1,0:T(8,128)(2,1)} %param.18) | copy-start | bytes 1572868
  178.9 90.1 %all-gather.25.cloned.1.call-start = ((), (), s32[]{:S(2)}) async-start(), calls=%async_computation.22 | async-start | bytes 2621440 | tf_op jit(solution)/shard_map/all_gather | solution.py:202
  179.5 134.5 %all-gather.23.cloned.1.call-start = ((), (), s32[]{:S(2)}) async-start(), calls=%async_computation.20 | async-start | bytes 6488064 | tf_op jit(solution)/shard_map/all_gather | solution.py:210
  180.0 182.1 %all-gather.17.cloned.1.call-start = ((), (), s32[]{:S(2)}) async-start(), calls=%async_computation.17 | async-start | bytes 2621440 | tf_op jit(solution)/shard_map/all_gather | solution.py:202
  224.1 182.1 %all-gather.19.cloned.1.call-start = ((), (), s32[]{:S(2)}) async-start(), calls=%async_computation.18 | async-start | bytes 6488064 | tf_op jit(solution)/shard_map/all_gather | solution.py:210
  224.9 226.7 %all-gather.21.cloned.1.call-start = ((), (), s32[]{:S(2)}) async-start(), calls=%async_computation.19 | async-start | bytes 6488064 | tf_op jit(solution)/shard_map/all_gather | solution.py:210
  225.6 180.6 %copy-start.22 = (f32[2048]{0:T(1024)S(1)}, f32[2048]{0:T(1024)}, u32[]{:S(2)}) copy-start(f32[2048]{0:T(1024)} %param.30) | copy-start | bytes 24580
  225.6 289.3 %reduce-scatter.14.cloned.1.call-start = ((), (), s32[]{:S(2)}) async-start(), calls=%async_computation.23 | async-start | bytes 2621440 | tf_op jit(solution)/shard_map/reduce_scatter | solution.py:206
  406.2 45.4 %copy-start.12 = (bf16[512,2048]{1,0:T(8,128)(2,1)S(1)}, bf16[512,2048]{1,0:T(8,128)(2,1)}, u32[]{:S(2)}) copy-start(bf16[512,2048]{1,0:T(8,128)(2,1)} %all-gather.17.cloned.1.call-done) | copy-start | bytes 6291460
  465.4 49.6 %copy-start.5 = (bf16[512,512]{1,0:T(8,128)(2,1)S(1)}, bf16[512,512]{1,0:T(8,128)(2,1)}, u32[]{:S(2)}) copy-start(bf16[512,512]{1,0:T(8,128)(2,1)} %reduce-scatter.10.cloned.1.call-done) | copy-start | bytes 1572868
  465.4 49.6 %copy-start.7 = (bf16[2,256,512]{2,1,0:T(8,128)(2,1)S(1)}, bf16[2,256,512]{2,1,0:T(8,128)(2,1)}, u32[]{:S(2)}) copy-start(bf16[2,256,512]{2,1,0:T(8,128)(2,1)} %param.19) | copy-start | bytes 1572868
  470.8 91.8 %all-gather.27.cloned.1.call-start = ((), (), s32[]{:S(2)}) async-start(), calls=%async_computation.24 | async-start | bytes 2621440 | tf_op jit(solution)/shard_map/all_gather | solution.py:202
  517.2 243.8 %reduce-scatter.22.cloned.1.call-start = ((), (), s32[]{:S(2)}) async-start(), calls=%async_computation.28 | async-start | bytes 6488064 | tf_op jit(solution)/shard_map/reduce_scatter | solution.py:214
  525.7 237.7 %reduce-scatter.24.cloned.1.call-start = ((), (), s32[]{:S(2)}) async-start(), calls=%async_computation.29 | async-start | bytes 6488064 | tf_op jit(solution)/shard_map/reduce_scatter | solution.py:214
  534.2 231.7 %reduce-scatter.26.cloned.1.call-start = ((), (), s32[]{:S(2)}) async-start(), calls=%async_computation.30 | async-start | bytes 6488064 | tf_op jit(solution)/shard_map/reduce_scatter | solution.py:214
  542.1 20.5 %copy-start.17 = (bf16[512,512]{1,0:T(8,128)(2,1)S(1)}, bf16[512,512]{1,0:T(8,128)(2,1)}, u32[]{:S(2)}) copy-start(bf16[512,512]{1,0:T(8,128)(2,1)} %copy-done.16) | copy-start | bytes 1572868
  542.2 253.0 %reduce-scatter.20.cloned.1.call-start = ((), (), s32[]{:S(2)}) async-start(), calls=%async_computation.27 | async-start | bytes 2359296 | tf_op jit(solution)/shard_map/reduce_scatter | solution.py:214
  566.9 274.3 %reduce-scatter.12.cloned.1.call-start = ((), (), s32[]{:S(2)}) async-start(), calls=%async_computation.21 | async-start | bytes 2621440 | tf_op jit(solution)/shard_map/reduce_scatter | solution.py:206
  575.0 311.7 %reduce-scatter.16.cloned.1.call-start = ((), (), s32[]{:S(2)}) async-start(), calls=%async_computation.25 | async-start | bytes 2621440 | tf_op jit(solution)/shard_map/reduce_scatter | solution.py:206
  650.5 3.4 collective-permute-start.1
  660.3 290.7 %reduce-scatter.18.cloned.1.call-start = ((), (), s32[]{:S(2)}) async-start(), calls=%async_computation.26 | async-start | bytes 7077888 | tf_op jit(solution)/shard_map/reduce_scatter | solution.py:214
  684.4 12.1 %copy-start.19 = (f32[2048]{0:T(1024)S(1)}, f32[2048]{0:T(1024)}, u32[]{:S(2)}) copy-start(f32[2048]{0:T(1024)} %get-tuple-element.105) | copy-start | bytes 24580
  763.4 123.3 %copy-start.6 = (bf16[512,512]{1,0:T(8,128)(2,1)S(1)}, bf16[512,512]{1,0:T(8,128)(2,1)}, u32[]{:S(2)}) copy-start(bf16[512,512]{1,0:T(8,128)(2,1)} %reduce-scatter.10.cloned.1.call-done) | copy-start | bytes 1572868
  763.4 123.3 %copy-start.8 = (bf16[2,256,512]{2,1,0:T(8,128)(2,1)S(1)}, bf16[2,256,512]{2,1,0:T(8,128)(2,1)}, u32[]{:S(2)}) copy-start(bf16[2,256,512]{2,1,0:T(8,128)(2,1)} %param.19) | copy-start | bytes 1572868
  763.4 123.3 %copy-start.15 = (bf16[512,512]{1,0:T(8,128)(2,1)S(1)}, bf16[512,512]{1,0:T(8,128)(2,1)}, u32[]{:S(2)}) copy-start(bf16[512,512]{1,0:T(8,128)(2,1)} %reduce-scatter.14.cloned.1.call-done) | copy-start | bytes 1572868
  (20 other events, 87.9 us)
Sparse Core Ops, SparseCore 0:
  9.6 48.6 all-gather.10
  60.7 45.3 all-gather.12
  108.0 33.0 all-gather.14
  179.0 43.1 reduce-scatter.9
  223.7 45.2 all-gather.24
  270.8 43.0 all-gather.22
  316.1 45.9 all-gather.16
  364.2 42.0 all-gather.18
  408.3 43.3 all-gather.20
  470.9 43.9 reduce-scatter.13
  517.4 45.2 all-gather.26
  565.9 58.7 reduce-scatter.21
  628.6 59.4 reduce-scatter.23
  691.5 58.9 reduce-scatter.25
  754.0 41.1 reduce-scatter.19
  797.3 43.8 reduce-scatter.11
  843.5 43.1 reduce-scatter.15
  889.9 61.0 reduce-scatter.17

commit v2 on v1

--- a/solution.py
+++ b/solution.py
@@ -198,12 +198,54 @@
     return jnp.dot(left, right, preferred_element_type=f32)
 
 
+def along_line(array, pairs):
+    return lax.ppermute(array, "fsdp", pairs)
+
+
+outer_pairs = [(0, 1), (1, 0), (2, 3), (3, 2)]
+inner_pairs = [(1, 2), (2, 1)]
+
+
 def gather_share(share):
-    return lax.all_gather(share, "fsdp", axis=1, tiled=True)
+    own = lax.axis_index("fsdp")
+    next_one = along_line(share, outer_pairs)
+    inner_one = along_line(share, inner_pairs)
+    outer_two = along_line(inner_one, outer_pairs)
+    inner_two = along_line(next_one, inner_pairs)
+    outer_three = along_line(inner_two, outer_pairs)
+    by_offset = (share, next_one, outer_two + inner_two, outer_three + inner_one)
+    blocks = []
+    for place in range(4):
+        offset = own ^ place
+        block = by_offset[3]
+        for k in range(3):
+            block = jnp.where(offset == k, by_offset[k], block)
+        blocks.append(block)
+    return lax.optimization_barrier(jnp.concatenate(blocks, axis=1))
 
 
 def scatter_share(partial_sums):
-    return lax.psum_scatter(partial_sums.astype(bf16), "fsdp", scatter_dimension=1, tiled=True).astype(f32)
+    own = lax.axis_index("fsdp")
+    share = partial_sums.shape[1] // 4
+
+    def part(offset):
+        return lax.dynamic_slice_in_dim(partial_sums, (own ^ offset) * share, share, 1)
+
+    far = along_line(part(3).astype(bf16), outer_pairs)
+    near = along_line(part(2).astype(bf16), outer_pairs)
+    far = along_line((part(2) + far).astype(bf16), inner_pairs)
+    near = along_line((part(3) + near).astype(bf16), inner_pairs)
+    last = along_line((part(1) + far).astype(bf16), outer_pairs)
+    return part(0).astype(f32) + last.astype(f32) + near.astype(f32)
+
+
+def sum_line(array):
+    array = array + along_line(array, outer_pairs)
+    return array + along_line(array, [(i, i ^ 2) for i in range(4)])
+
+
+def swap_seq(array, bit):
+    return lax.ppermute(array, "seq", [(i, i ^ (1 << bit)) for i in range(lax.axis_size("seq"))])
 
 
 def gather_weight(shard):
@@ -211,7 +253,36 @@
 
 
 def scatter_weight(grad):
-    return lax.psum_scatter(grad.astype(bf16), "seq", scatter_dimension=0, tiled=True).astype(f32)
+    count = lax.axis_size("seq")
+    rank = lax.axis_index("seq")
+    bits = count.bit_length() - 1
+    rows = grad.shape[0] // count
+
+    def halve(array, left, bit):
+        dim, mine = left.index(bit), (rank >> bit) & 1
+        keep = lax.dynamic_index_in_dim(array, mine, dim, keepdims=False)
+        give = lax.dynamic_index_in_dim(array, 1 - mine, dim, keepdims=False)
+        got = swap_seq(give.astype(bf16), bit)
+        return keep.astype(f32) + got.astype(f32), [other for other in left if other != bit]
+
+    left = list(range(bits))[::-1]
+    summed, left = halve(grad.reshape((2,) * bits + (rows, grad.shape[1])), left, 0)
+    chip_bits = list(range(1, bits))
+    middle = len(chip_bits) // 2
+    parts = []
+    for half, order in enumerate((chip_bits, chip_bits[middle:] + chip_bits[:middle])):
+        part = lax.slice_in_dim(summed, half * rows // 2, (half + 1) * rows // 2, axis=summed.ndim - 2)
+        rest = left
+        for bit in order:
+            part, rest = halve(part, rest, bit)
+        parts.append(part)
+    return jnp.concatenate(parts, axis=0)
+
+
+def sum_seq(array):
+    for bit in range(lax.axis_size("seq").bit_length() - 1):
+        array = array + swap_seq(array, bit)
+    return array
 
 
 def to_channels(token_side, batches):
@@ -264,10 +335,9 @@
     x_all = gather_share(x_share).astype(f32)
     w_in = gather_weight(in_proj.reshape(d_rows, 3 * share))
     w_out = gather_weight(out_proj.T)
-    w_gate = gather_weight(gate_proj)
-    w_up = gather_weight(up_proj)
+    units = gate_proj.shape[1]
+    w_feed = gather_weight(jnp.concatenate([gate_proj, up_proj], axis=1))
     w_down = gather_weight(down_proj.T)
-    cot_all = gather_share(cot_share)
 
     places = jnp.stack([places_of(doc_lengths[m], total) for m in range(batches)])
     keep = (places > 0).astype(f32)
@@ -289,33 +359,32 @@
     lagged = [extended[:, 2 - lag : 2 - lag + rows] for lag in range(3)]
     conv = sum(taps[lag] * masks[lag] * lagged[lag] for lag in range(3)).reshape(tokens, 3 * share)
     gate_one, gate_two, values = (conv[:, j * share : (j + 1) * share] for j in range(3))
-    channel_in = to_channels((gate_two * values).astype(bf16), batches)
+    product = (gate_two * values).astype(bf16)
+    product, cot_share = lax.optimization_barrier((product, cot_share))
+    cot_all = gather_share(cot_share)
+    channel_in = to_channels(product, batches)
     channel_out = long_conv(channel_in, keep, modes, skips, batches)
     mixed = to_tokens(channel_out, batches).astype(f32)
     gated = (gate_one * mixed).astype(bf16)
-    stream = x_share.astype(f32) + scatter_share(dot_rows(gated, w_out))
+    stream = x_share.astype(f32) + scatter_share(dot_rows(gated, w_out).astype(bf16))
     stream_all = gather_share(stream.astype(bf16)).astype(f32)
     scale_two = lax.rsqrt(jnp.mean(stream_all * stream_all, axis=-1, keepdims=True) + norm_eps)
     unit_two = stream_all * scale_two
     normed_two = (unit_two * feed_gain).astype(bf16)
-    gate_pre = dot(normed_two, w_gate)
-    up_pre = dot(normed_two, w_up)
+    feed_pre = dot(normed_two, w_feed)
+    gate_pre, up_pre = feed_pre[:, :units], feed_pre[:, units:]
     sigmoid = jax.nn.sigmoid(gate_pre)
     activated = gate_pre * sigmoid
     hidden = (activated * up_pre).astype(bf16)
-    block_out = stream + scatter_share(dot_rows(hidden, w_down))
+    down_part = dot_rows(hidden, w_down).astype(bf16)
 
     d_hidden = dot(cot_all, w_down)
-    d_gate = (d_hidden * up_pre * sigmoid * (1.0 + gate_pre * (1.0 - sigmoid))).astype(bf16)
-    d_up = (d_hidden * activated).astype(bf16)
-    grad_down = dot_tokens(cot_all, hidden)
-    grad_gate = dot_tokens(normed_two, d_gate)
-    grad_up = dot_tokens(normed_two, d_up)
-    part_two = dot_rows(d_gate, w_gate) + dot_rows(d_up, w_up)
-    along_two = lax.psum(
-        jnp.sum(d_gate.astype(f32) * gate_pre + d_up.astype(f32) * up_pre, axis=-1, keepdims=True), "fsdp"
-    )
-    feed_gain_part = jnp.sum(unit_two * part_two, axis=0)
+    d_gate = d_hidden * up_pre * sigmoid * (1.0 + gate_pre * (1.0 - sigmoid))
+    d_up = d_hidden * activated
+    d_feed = jnp.concatenate([d_gate.astype(bf16), d_up.astype(bf16)], axis=1)
+    part_two = dot_rows(d_feed, w_feed).astype(bf16)
+    along_two = sum_line(jnp.sum(d_feed.astype(f32) * feed_pre, axis=-1).reshape(-1, 128)).reshape(tokens, 1)
+    feed_gain_part = jnp.sum(unit_two * part_two.astype(f32), axis=0)
 
     def own_features(part):
         return lax.dynamic_slice_in_dim(part, fsdp_rank * share, share, 0)
@@ -326,9 +395,15 @@
         - stream * (scale_two * scale_two * along_two / width)
     )
     d_mix = gather_share(d_stream.astype(bf16))
-
-    grad_out = dot_tokens(d_mix, gated)
+    grad_down = dot_tokens(cot_all, hidden).astype(bf16)
+    grad_feed = dot_tokens(normed_two, d_feed).astype(bf16)
+    down_grad = scatter_weight(grad_down).T
+    feed_grad = scatter_weight(grad_feed)
+
     d_gated = dot(d_mix, w_out)
+    d_gated, down_part = lax.optimization_barrier((d_gated, down_part))
+    block_out = stream + scatter_share(down_part)
+    out_grad = scatter_weight(dot_tokens(d_mix, gated).astype(bf16)).T
     d_gate_one = d_gated * mixed
     back_in = to_channels((d_gated * gate_one).astype(bf16), batches)
     back_out, mode_sums, skip_sums = long_conv_back(channel_in, back_in, keep, modes, skips, batches)
@@ -342,25 +417,20 @@
     returned = shifted(spread[:, :2], "seq", -1)
     d_project = spread[:, 2:] + jnp.pad(returned, ((0, 0), (rows - 2, 0), (0, 0)))
     d_project = d_project.astype(bf16).reshape(tokens, 3 * share)
-    along_one = lax.psum(
-        jnp.sum(d_project.astype(f32) * project.reshape(tokens, 3 * share), axis=-1, keepdims=True), "fsdp"
-    )
-    grad_in = dot_tokens(normed_one, d_project)
-    part_one = dot_rows(d_project, w_in)
-    mixer_gain_part = jnp.sum(unit_one * part_one, axis=0)
+    along_one = jnp.sum(d_project.astype(f32) * project.reshape(tokens, 3 * share), axis=-1)
+    along_one = sum_line(along_one.reshape(-1, 128)).reshape(tokens, 1)
+    part_one = dot_rows(d_project, w_in).astype(bf16)
+    mixer_gain_part = jnp.sum(unit_one * part_one.astype(f32), axis=0)
     d_x = (
         d_stream
         + scale_one * own_features(mixer_gain) * scatter_share(part_one)
         - x_share.astype(f32) * (scale_one * scale_one * along_one / width)
     )
 
-    in_grad = scatter_weight(grad_in).reshape(d_rows, 3, share)
-    out_grad = scatter_weight(grad_out).T
-    gate_grad = scatter_weight(grad_gate)
-    up_grad = scatter_weight(grad_up)
-    down_grad = scatter_weight(grad_down).T
-    gains = lax.psum(jnp.stack([mixer_gain_part, feed_gain_part]), ("fsdp", "seq"))
-    short_grad = lax.psum(short_part, "seq").reshape(3, 3, share)
+    in_grad = scatter_weight(dot_tokens(normed_one, d_project).astype(bf16)).reshape(d_rows, 3, share)
+    gains = sum_seq(sum_line(jnp.concatenate([mixer_gain_part, feed_gain_part]).reshape(-1, 128)))
+    gains = gains.reshape(2, width)
+    short_grad = sum_seq(short_part).reshape(3, 3, share)
     skip_own = jnp.sum(skip_sums.reshape(batches, chan_here), axis=0)
     skip_rows = jnp.zeros((half_modes, 2 * chan_here), f32).at[0, :chan_here].set(skip_own)
     filters = jnp.concatenate([mode_sums, skip_rows[None]], axis=0)
@@ -380,8 +450,8 @@
         by_chan[4, :, 0],
         out_grad,
         gains[1],
-        gate_grad,
-        up_grad,
+        feed_grad[:, :units],
+        feed_grad[:, units:],
         down_grad,
     )
 

time: 969 us -> 703 us (0.73)
  waiting for transfers between devices: 590 us -> 196 us
  starting transfers between devices: 10.2 us -> 172 us
  blocking collectives: 135 us -> 8.34 us
  local copies, waits for them, and re-layouts: 30.6 us -> 94.3 us
  other arithmetic: 37.2 us -> 88.7 us
  matrix products: 98.2 us -> 72.4 us
    reduce_scatter x9 -> x0, waiting for transfers between devices: 252 us -> none  [the longest x4 164 us: scatter_share(): lax.psum_scatter(partial_sums.astype(bf16), 'fsdp', scatter_dimension=1,...]
    all_gather x5 -> x4, waiting for transfers between devices: 170 us -> 2.16 us  [gather_weight(): return lax.all_gather(shard, 'seq', axis=0, tiled=True)]
    ppermute x0 -> x72, waiting for transfers between devices: none -> 162 us  [the longest x46 89.8 us: along_line(): return lax.ppermute(array, 'fsdp', pairs)]
    ppermute x0 -> x72, starting transfers between devices: none -> 150 us  [the longest x46 119 us: along_line(): return lax.ppermute(array, 'fsdp', pairs)]
    all_gather x4 -> x0, waiting for transfers between devices: 148 us -> none  [gather_share(): return lax.all_gather(share, 'fsdp', axis=1, tiled=True)]
    psum x4 -> x0, blocking collectives: 84 us -> none  [the longest x1 39.9 us: on_device(): lax.psum(jnp.stack([mixer_gain_part, feed_gain_part]), ('fsdp', 'seq'))]
    add x0 -> x42, other arithmetic: none -> 44.2 us  [the longest x20 23.4 us: halve(): keep.astype(f32) + got.astype(f32)]
    all_to_all x3 -> x0, blocking collectives: 41.3 us -> none  [the longest x2 24.3 us: to_tokens(): lax.all_to_all(channel_side.reshape(count, rows, width), 'seq', split_axi...]
  transfers between devices with their start and end apart: 21 -> 82, of which waited for: 17 -> 34; matrix products, arithmetic and copies ran while one was open for 14% -> 31% of each run, Pallas kernels for 5% -> 6%
where the time goes in v2:
time: 703 us; the launch traced here: 692 us
  waiting for transfers between devices  196 us (28%)
  starting transfers between devices  172 us (24%)
  local copies, waits for them, and re-layouts  94.3 us (13%)
  other arithmetic  88.7 us (13%)
  matrix products  72.4 us (10%)
  Pallas kernels  45 us (6%)
  between operations  15.7 us (2%)
  blocking collectives  8.34 us (1%)
    ppermute x46, starting transfers between devices, along_line(): return lax.ppermute(array, 'fsdp', pairs)  119 us
    ppermute x46, waiting for transfers between devices, along_line(): return lax.ppermute(array, 'fsdp', pairs)  89.8 us
    ppermute x26, waiting for transfers between devices, swap_seq(): lax.ppermute(array, 'seq', [(i, i ^ 1 << bit) for i in range(lax.axis_siz...  71.9 us
    ppermute x26, starting transfers between devices, swap_seq(): lax.ppermute(array, 'seq', [(i, i ^ 1 << bit) for i in range(lax.axis_siz...  31 us
    pallas_call x1, Pallas kernels, long_conv_back(): pl.pallas_call(functools.partial(back_kernel, count, 16), out_shape=(jax....  29.9 us
    dot_general x4, matrix products, dot(): return jnp.dot(left, right, preferred_element_type=f32)  29.1 us
    unnamed x130, local copies, waits for them, and re-layouts  26 us
    dot_general x4, matrix products, dot_rows(): lax.dot_general(left, right, (((1,), (1,)), ((), ())), preferred_element_...  25.9 us
  transfers between devices with their start and end apart: 82, of which 34 were waited for; matrix products, arithmetic and copies ran while one was open for 31% of the time, Pallas kernels for 6%

profile of v2, /device:TPU:0, one launch (start us, length us, event | category | flops | bytes accessed | tf_op | source)
XLA Modules:
  0.0 692.1 jit_solution(2327852692660329928)
XLA Ops:
  17.1 9.7 %collective-permute-done.2 = bf16[512,512]{1,0:T(8,128)(2,1)S(1)} collective-permute-done((bf16[512,512]{1,0:T(8,128)(2,1)S(1)}, bf16[512,512]{1,0:T(8,128)(2,1)S(1)}, u32[]{:S(2)}, u32[]{:S(2)}) %collective-permute-start.2) | collective-permute-done | bytes 524320 | tf_op jit(solution)/shard_map/ppermute | solution.py:202
  33.0 10.4 %collective-permute-start.4 = (bf16[512,512]{1,0:T(8,128)(2,1)S(1)}, bf16[512,512]{1,0:T(8,128)(2,1)S(1)}, u32[]{:S(2)}, u32[]{:S(2)}) collective-permute-start(bf16[512,512]{1,0:T(8,128)(2,1)S(1)} %collective-permute-done.3), channel_id=1, source_target_pairs={{0,8},{8,0},{16,24},{24,16},{1,9},{9,1},{17,25},{25,17},{2,10},{10... | collective-permute-start | bytes 1572872 | tf_op jit(solution)/shard_map/ppermute | solution.py:202
  45.3 9.8 %collective-permute-done.4 = bf16[512,512]{1,0:T(8,128)(2,1)S(1)} collective-permute-done((bf16[512,512]{1,0:T(8,128)(2,1)S(1)}, bf16[512,512]{1,0:T(8,128)(2,1)S(1)}, u32[]{:S(2)}, u32[]{:S(2)}) %collective-permute-start.4) | collective-permute-done | bytes 524320 | tf_op jit(solution)/shard_map/ppermute | solution.py:202
  59.9 6.3 fusion.29
  79.9 14.3 %all-to-all-done = bf16[8,256,128]{1,2,0:T(8,128)(2,1)S(1)} async-done(((bf16[8,256,128]{1,2,0:T(8,128)(2,1)}), bf16[8,256,128]{1,2,0:T(8,128)(2,1)S(1)}, u32[]{:S(2)}, u32[]{:S(2)}) %all-to-all-start) | async-done | bytes 524320 | tf_op jit(solution)/shard_map/all_to_all | solution.py:293
  94.5 15.1 %shard_map.271 = bf16[2048,128]{1,0:T(8,128)(2,1)S(1)} custom-call(f32[2,2048]{1,0:T(2,128)S(1)} %compare_convert_fusion.keep_ref, bf16[2048,128]{1,0:T(8,128)(2,1)S(1)} %bitcast.234, f32[4,8,128]{2,1,0:T(8,128)S(1)} %pad_maximum_fusion.13.par_ref, f32[1,128]{1,0:T(1,128)S(1)} %broadcast_in_dim_tile.3.skip_ref), custom_call_target="tpu_custom_call" | custom-call | tf_op jit(solution)/shard_map/pallas_call | solution.py:139
  114.1 15.6 %all-to-all-done.1 = bf16[8,256,128]{1,2,0:T(8,128)(2,1)S(1)} async-done(((bf16[8,256,128]{1,2,0:T(8,128)(2,1)}), bf16[8,256,128]{1,2,0:T(8,128)(2,1)S(1)}, u32[]{:S(2)}, u32[]{:S(2)}) %all-to-all-start.1) | async-done | bytes 524320 | tf_op jit(solution)/shard_map/all_to_all | solution.py:301
  142.3 8.7 %collective-permute-done.6 = bf16[512,512]{1,0:T(8,128)(2,1)} collective-permute-done((bf16[512,512]{1,0:T(8,128)(2,1)}, bf16[512,512]{1,0:T(8,128)(2,1)}, u32[]{:S(2)}, u32[]{:S(2)}) %collective-permute-start.6) | collective-permute-done | bytes 524320 | tf_op jit(solution)/shard_map/ppermute | solution.py:202
  159.9 8.6 %collective-permute-done.9 = bf16[512,512]{1,0:T(8,128)(2,1)} collective-permute-done((bf16[512,512]{1,0:T(8,128)(2,1)}, bf16[512,512]{1,0:T(8,128)(2,1)}, u32[]{:S(2)}, u32[]{:S(2)}) %collective-permute-start.9) | collective-permute-done | bytes 524320 | tf_op jit(solution)/shard_map/ppermute | solution.py:202
  195.3 10.8 %collective-permute-start.20 = (bf16[512,512]{1,0:T(8,128)(2,1)}, bf16[512,512]{1,0:T(8,128)(2,1)S(1)}, u32[]{:S(2)}, u32[]{:S(2)}) collective-permute-start(bf16[512,512]{1,0:T(8,128)(2,1)} %collective-permute-done.19), channel_id=1, source_target_pairs={{0,8},{8,0},{16,24},{24,16},{1,9},{9,1},{17,25},{25,17},{2,10},{10... | collective-permute-start | bytes 1572872 | tf_op jit(solution)/shard_map/ppermute | solution.py:202
  213.2 8.5 %collective-permute-done.20 = bf16[512,512]{1,0:T(8,128)(2,1)S(1)} collective-permute-done((bf16[512,512]{1,0:T(8,128)(2,1)}, bf16[512,512]{1,0:T(8,128)(2,1)S(1)}, u32[]{:S(2)}, u32[]{:S(2)}) %collective-permute-start.20) | collective-permute-done | bytes 524320 | tf_op jit(solution)/shard_map/ppermute | solution.py:202
  228.4 7.3 %collective-permute-done.12 = bf16[512,512]{1,0:T(8,128)(2,1)S(1)} collective-permute-done((bf16[512,512]{1,0:T(8,128)(2,1)S(1)}, bf16[512,512]{1,0:T(8,128)(2,1)S(1)}, u32[]{:S(2)}, u32[]{:S(2)}) %collective-permute-start.12) | collective-permute-done | bytes 524320 | tf_op jit(solution)/shard_map/ppermute | solution.py:202
  235.7 5.6 collective-permute-done.15
  242.5 11.2 %fusion.32 = f32[512,2816]{1,0:T(8,128)} fusion(bf16[2048,2816]{1,0:T(8,128)(2,1)} %all-gather.12.cloned.1.call-done, bf16[512,2048]{1,0:T(8,128)(2,1)S(1)} %pad_maximum_fusion.4, f32[2048]{0:T(1024)S(1)} %copy-done.53, f32[512]{0:T(512)S(1)} %add_rsqrt_fusion), kind=kOutput, calls=%fused_computation.112 | convolution fusion | flops 5909774336 | bytes 19408896 | tf_op jit(solution)/shard_map/dot_general | solution.py:198
  253.7 10.4 %multiply_convert_fusion.2 = (bf16[512,1408]{1,0:T(8,128)(2,1)S(1)}, bf16[512,1408]{1,0:T(8,128)(2,1)S(1)}, bf16[512,1408]{1,0:T(8,128)(2,1)}) fusion(f32[512,2816]{1,0:T(8,128)} %fusion.32, bf16[512,2048]{1,0:T(8,128)(2,1)} %pad_maximum_fusion.5, bf16[2048,1408]{0,1:T(8,128)(2,1)} %all-gather.10.cloned.1.call-done), kind=kOutput, calls=%fused_computation.58 | convolution fusion | flops 2963603456 | bytes 17956864 | tf_op jit(solution)/shard_map/dot_general | solution.py:198
  264.0 10.7 %fusion.5 = (f32[2048]{0:T(1024)}, bf16[512,2048]{1,0:T(8,128)(2,1)S(1)}) fusion(bf16[512,2048]{1,0:T(8,128)(2,1)S(1)} %pad_maximum_fusion.4, f32[512]{0:T(512)S(1)} %add_rsqrt_fusion, bf16[2048,2816]{1,0:T(8,128)(2,1)} %all-gather.12.cloned.1.call-done, bf16[512,1408]{1,0:T(8,128)(2,1)S(1)} %get-tuple-element.117, bf16[512,1408]{1,0:T(8,128)(2,1)S(1)} %get-tuple-element.116), kind=kOutput, calls=%fused_computation.23 | convolution fusion | flops 5917636608 | bytes 18622464 | tf_op jit(solution)/shard_map/dot_general | solution.py:190
  284.6 7.0 %collective-permute-done.21 = bf16[512,512]{1,0:T(8,128)(2,1)} collective-permute-done((bf16[512,512]{1,0:T(8,128)(2,1)}, bf16[512,512]{1,0:T(8,128)(2,1)}, u32[]{:S(2)}, u32[]{:S(2)}) %collective-permute-start.21) | collective-permute-done | bytes 524320 | tf_op jit(solution)/shard_map/ppermute | solution.py:202
  324.9 6.7 convolution_convert_fusion
  342.9 7.9 %convolution_convert_fusion.7 = bf16[512,2048]{1,0:T(8,128)(2,1)} fusion(bf16[512,1408]{1,0:T(8,128)(2,1)} %get-tuple-element.126, bf16[2048,1408]{0,1:T(8,128)(2,1)} %all-gather.10.cloned.1.call-done), kind=kOutput, calls=%fused_computation.48 | convolution fusion | flops 2953838592 | bytes 9306112 | tf_op jit(solution)/shard_map/dot_general | solution.py:190
  350.8 7.9 %collective-permute-start.29 = (bf16[512,512]{1,0:T(8,128)(2,1)S(1)}, bf16[512,512]{1,0:T(8,128)(2,1)S(1)}, u32[]{:S(2)}, u32[]{:S(2)}) collective-permute-start(bf16[512,512]{1,0:T(8,128)(2,1)S(1)} %collective-permute-done.28), channel_id=1, source_target_pairs={{0,8},{8,0},{16,24},{24,16},{1,9},{9,1},{17,25},{25,17},{2,10},{10... | collective-permute-start | bytes 1572872 | tf_op jit(solution)/shard_map/ppermute | solution.py:202
  358.7 10.6 %collective-permute-start.32 = (bf16[512,512]{1,0:T(8,128)(2,1)S(1)}, bf16[512,512]{1,0:T(8,128)(2,1)S(1)}, u32[]{:S(2)}, u32[]{:S(2)}) collective-permute-start(bf16[512,512]{1,0:T(8,128)(2,1)S(1)} %collective-permute-done.31), channel_id=1, source_target_pairs={{0,8},{8,0},{16,24},{24,16},{1,9},{9,1},{17,25},{25,17},{2,10},{10... | collective-permute-start | bytes 1572872 | tf_op jit(solution)/shard_map/ppermute | solution.py:202
  395.7 5.7 all-to-all-start.2
  423.9 29.9 %shard_map.272 = (bf16[2048,128]{1,0:T(8,128)(2,1)S(1)}, f32[4,8,128]{2,1,0:T(8,128)S(1)}, f32[1,128]{1,0:T(1,128)S(1)}) custom-call(f32[2,2048]{1,0:T(2,128)S(1)} %compare_convert_fusion.keep_ref, bf16[2048,128]{1,0:T(8,128)(2,1)S(1)} %bitcast.235, bf16[2048,128]{1,0:T(8,128)(2,1)S(1)} %bitcast.236, f32[4,8,128]{2,1,0:T(8,128)S(1)} %pad_maximum_fusion.13.par_ref, ...), custom_call_target="tpu_custom_call" | custom-call | tf_op jit(solution)/shard_map/pallas_call | solution.py:151
  455.1 8.3 %all-gather = f32[40,8,128]{2,1,0:T(8,128)S(1)} all-gather(f32[5,8,128]{2,1,0:T(8,128)S(1)} %select_maximum_fusion), channel_id=2, replica_groups=mesh['fsdp'=4,'seq'=8] {'seq'}, dimensions={0}, use_global_device_ids=true | all-gather | bytes 184320 | tf_op jit(solution)/shard_map/all_gather | solution.py:437
  549.1 6.2 collective-permute-start.35
  571.7 9.8 %convert_add_fusion = f32[2,2,256,2816]{3,2,1,0:T(8,128)} fusion(bf16[2,2,256,2816]{3,2,1,0:T(8,128)(2,1)} %collective-permute-done.64, bf16[2,2,2,256,2816]{4,3,2,1,0:T(8,128)(2,1)} %bitcast.251, s32[]{:T(128)S(6)} %select_n.405), kind=kLoop, calls=%fused_computation | loop fusion | flops 8650752 | bytes 23068676 | tf_op jit(solution)/shard_map/add | solution.py:266
  581.5 7.5 %fusion.61 = (f32[2,2,128,2816]{3,2,1,0:T(8,128)}, f32[2,2,128,2816]{3,2,1,0:T(8,128)S(1)}) fusion(f32[2,2,256,2816]{3,2,1,0:T(8,128)} %convert_add_fusion), kind=kLoop, calls=%fused_computation.222 | loop fusion | bytes 23068672 | tf_op jit(solution)/shard_map/slice | solution.py:274
  612.1 5.7 collective-permute-done.67
  619.0 18.4 %collective-permute-done.65 = bf16[2,128,2816]{2,1,0:T(8,128)(2,1)S(1)} collective-permute-done((bf16[2,128,2816]{2,1,0:T(8,128)(2,1)S(1)}, bf16[2,128,2816]{2,1,0:T(8,128)(2,1)S(1)}, u32[]{:S(2)}, u32[]{:S(2)}) %collective-permute-start.65) | collective-permute-done | bytes 1441824 | tf_op jit(solution)/shard_map/ppermute | solution.py:248
  642.9 10.1 %collective-permute-done.68 = bf16[128,2816]{1,0:T(8,128)(2,1)} collective-permute-done((bf16[128,2816]{1,0:T(8,128)(2,1)S(1)}, bf16[128,2816]{1,0:T(8,128)(2,1)}, u32[]{:S(2)}, u32[]{:S(2)}) %collective-permute-start.68) | collective-permute-done | bytes 720928 | tf_op jit(solution)/shard_map/ppermute | solution.py:248
  658.8 13.3 %collective-permute-done.54 = bf16[2,128,1536]{1,2,0:T(8,128)(2,1)S(1)} collective-permute-done((bf16[2,128,1536]{1,2,0:T(8,128)(2,1)S(1)}, bf16[2,128,1536]{1,2,0:T(8,128)(2,1)S(1)}, u32[]{:S(2)}, u32[]{:S(2)}) %collective-permute-start.54) | collective-permute-done | bytes 786464 | tf_op jit(solution)/shard_map/ppermute | solution.py:248
  674.6 7.2 %collective-permute-done.55 = bf16[128,1536]{0,1:T(8,128)(2,1)S(1)} collective-permute-done((bf16[128,1536]{0,1:T(8,128)(2,1)S(1)}, bf16[128,1536]{0,1:T(8,128)(2,1)S(1)}, u32[]{:S(2)}, u32[]{:S(2)}) %collective-permute-start.55) | collective-permute-done | bytes 393248 | tf_op jit(solution)/shard_map/ppermute | solution.py:248
  (460 shorter events, 351.2 us)
Async XLA Ops:
  7.2 52.7 %all-gather.6.cloned.1.call-start = ((), (), s32[]{:S(2)}) async-start(), calls=%async_computation.4 | async-start | bytes 7077888 | tf_op jit(solution)/shard_map/all_gather | solution.py:252
  9.7 125.8 %all-gather.8.cloned.1.call-start = ((), (), s32[]{:S(2)}) async-start(), calls=%async_computation.5 | async-start | bytes 2359296 | tf_op jit(solution)/shard_map/all_gather | solution.py:252
  10.4 232.0 %all-gather.12.cloned.1.call-start = ((), (), s32[]{:S(2)}) async-start(), calls=%async_computation.7 | async-start | bytes 12976128 | tf_op jit(solution)/shard_map/all_gather | solution.py:252
  11.7 242.0 %all-gather.10.cloned.1.call-start = ((), (), s32[]{:S(2)}) async-start(), calls=%async_computation.6 | async-start | bytes 6488064 | tf_op jit(solution)/shard_map/all_gather | solution.py:252
  33.0 22.1 %collective-permute-start.4 = (bf16[512,512]{1,0:T(8,128)(2,1)S(1)}, bf16[512,512]{1,0:T(8,128)(2,1)S(1)}, u32[]{:S(2)}, u32[]{:S(2)}) collective-permute-start(bf16[512,512]{1,0:T(8,128)(2,1)S(1)} %collective-permute-done.3), channel_id=1, source_target_pairs={{0,8},{8,0},{16,24},{24,16},{1,9},{9,1},{17,25},{25,17},{2,10},{10... | collective-permute-start | bytes 1572872 | tf_op jit(solution)/shard_map/ppermute | solution.py:202
  156.4 23.2 %collective-permute-start.18 = (bf16[512,512]{1,0:T(8,128)(2,1)}, bf16[512,512]{1,0:T(8,128)(2,1)}, u32[]{:S(2)}, u32[]{:S(2)}) collective-permute-start(bf16[512,512]{1,0:T(8,128)(2,1)} %bitcast.8), channel_id=1, source_target_pairs={{0,8},{8,0},{16,24},{24,16},{1,9},{9,1},{17,25},{25,17},{2,10},{10... | collective-permute-start | bytes 1572872 | tf_op jit(solution)/shard_map/ppermute | solution.py:202
  190.9 22.3 %collective-permute-start.17 = (bf16[512,512]{1,0:T(8,128)(2,1)}, bf16[512,512]{1,0:T(8,128)(2,1)S(1)}, u32[]{:S(2)}, u32[]{:S(2)}) collective-permute-start(bf16[512,512]{1,0:T(8,128)(2,1)} %collective-permute-done.16), channel_id=1, source_target_pairs={{0,8},{8,0},{16,24},{24,16},{1,9},{9,1},{17,25},{25,17},{2,10},{10... | collective-permute-start | bytes 1572872 | tf_op jit(solution)/shard_map/ppermute | solution.py:202
  195.3 26.3 %collective-permute-start.20 = (bf16[512,512]{1,0:T(8,128)(2,1)}, bf16[512,512]{1,0:T(8,128)(2,1)S(1)}, u32[]{:S(2)}, u32[]{:S(2)}) collective-permute-start(bf16[512,512]{1,0:T(8,128)(2,1)} %collective-permute-done.19), channel_id=1, source_target_pairs={{0,8},{8,0},{16,24},{24,16},{1,9},{9,1},{17,25},{25,17},{2,10},{10... | collective-permute-start | bytes 1572872 | tf_op jit(solution)/shard_map/ppermute | solution.py:202
  319.2 50.1 %collective-permute-start.69 = (bf16[2,2,256,1408]{2,3,1,0:T(8,128)(2,1)}, bf16[2,2,256,1408]{2,3,1,0:T(8,128)(2,1)}, u32[]{:S(2)}, u32[]{:S(2)}) collective-permute-start(bf16[2,2,256,1408]{2,3,1,0:T(8,128)(2,1)} %bitcast.259), channel_id=1, source_target_pairs={{0,1},{1,0},{2,3},{3,2},{4,5},{5,4},{6,7},{7,6},{8,9},{9,8},{10,11... | collective-permute-start | bytes 8650760 | tf_op jit(solution)/shard_map/ppermute | solution.py:248
  338.3 231.9 %collective-permute-start.64 = (bf16[2,2,256,2816]{3,2,1,0:T(8,128)(2,1)}, bf16[2,2,256,2816]{3,2,1,0:T(8,128)(2,1)}, u32[]{:S(2)}, u32[]{:S(2)}) collective-permute-start(bf16[2,2,256,2816]{3,2,1,0:T(8,128)(2,1)} %dynamic-slice_bitcast_fusion), channel_id=1, source_target_pairs={{0,1},{1,0},{2,3},{3,2},{4,5},{5,4},{6,7},{7,6},{8,9},{9,8},{10,11... | collective-permute-start | bytes 17301512 | tf_op jit(solution)/shard_map/ppermute | solution.py:248
  350.8 28.1 %collective-permute-start.29 = (bf16[512,512]{1,0:T(8,128)(2,1)S(1)}, bf16[512,512]{1,0:T(8,128)(2,1)S(1)}, u32[]{:S(2)}, u32[]{:S(2)}) collective-permute-start(bf16[512,512]{1,0:T(8,128)(2,1)S(1)} %collective-permute-done.28), channel_id=1, source_target_pairs={{0,8},{8,0},{16,24},{24,16},{1,9},{9,1},{17,25},{25,17},{2,10},{10... | collective-permute-start | bytes 1572872 | tf_op jit(solution)/shard_map/ppermute | solution.py:202
  358.7 22.2 %collective-permute-start.32 = (bf16[512,512]{1,0:T(8,128)(2,1)S(1)}, bf16[512,512]{1,0:T(8,128)(2,1)S(1)}, u32[]{:S(2)}, u32[]{:S(2)}) collective-permute-start(bf16[512,512]{1,0:T(8,128)(2,1)S(1)} %collective-permute-done.31), channel_id=1, source_target_pairs={{0,8},{8,0},{16,24},{24,16},{1,9},{9,1},{17,25},{25,17},{2,10},{10... | collective-permute-start | bytes 1572872 | tf_op jit(solution)/shard_map/ppermute | solution.py:202
  373.2 41.2 %collective-permute-start.72 = (bf16[2,128,1408]{1,2,0:T(8,128)(2,1)}, bf16[2,128,1408]{1,2,0:T(8,128)(2,1)}, u32[]{:S(2)}, u32[]{:S(2)}) collective-permute-start(bf16[2,128,1408]{1,2,0:T(8,128)(2,1)} %fusion.27), channel_id=1, source_target_pairs={{0,4},{1,5},{2,6},{3,7},{4,0},{5,1},{6,2},{7,3},{8,12},{9,13},{10,... | collective-permute-start | bytes 2162696 | tf_op jit(solution)/shard_map/ppermute | solution.py:248
  377.0 41.7 %collective-permute-start.70 = (bf16[2,128,1408]{1,2,0:T(8,128)(2,1)}, bf16[2,128,1408]{1,2,0:T(8,128)(2,1)}, u32[]{:S(2)}, u32[]{:S(2)}) collective-permute-start(bf16[2,128,1408]{1,2,0:T(8,128)(2,1)} %fusion.26), channel_id=1, source_target_pairs={{0,2},{1,3},{2,0},{3,1},{4,6},{5,7},{6,4},{7,5},{8,10},{9,11},{10,... | collective-permute-start | bytes 2162696 | tf_op jit(solution)/shard_map/ppermute | solution.py:248
  395.7 26.9 %all-to-all-start.2 = ((bf16[8,256,128]{1,2,0:T(8,128)(2,1)}), bf16[8,256,128]{1,2,0:T(8,128)(2,1)}, u32[]{:S(2)}, u32[]{:S(2)}) async-start(bf16[8,256,128]{1,2,0:T(8,128)(2,1)} %bitcast.265), calls=%async_computation.2 | async-start | bytes 1048576 | tf_op jit(solution)/shard_map/all_to_all | solution.py:293
  403.4 70.0 %collective-permute-start.33 = (bf16[512,512]{1,0:T(8,128)(2,1)}, bf16[512,512]{1,0:T(8,128)(2,1)}, u32[]{:S(2)}, u32[]{:S(2)}) collective-permute-start(bf16[512,512]{1,0:T(8,128)(2,1)} %constant_dynamic-slice_fusion.8), channel_id=1, source_target_pairs={{0,8},{8,0},{16,24},{24,16},{1,9},{9,1},{17,25},{25,17},{2,10},{10... | collective-permute-start | bytes 1572872 | tf_op jit(solution)/shard_map/ppermute | solution.py:202
  411.9 133.0 %collective-permute-start.59 = (bf16[2,2,256,512]{2,3,1,0:T(8,128)(2,1)}, bf16[2,2,256,512]{2,3,1,0:T(8,128)(2,1)}, u32[]{:S(2)}, u32[]{:S(2)}) collective-permute-start(bf16[2,2,256,512]{2,3,1,0:T(8,128)(2,1)} %bitcast.269), channel_id=1, source_target_pairs={{0,1},{1,0},{2,3},{3,2},{4,5},{5,4},{6,7},{7,6},{8,9},{9,8},{10,11... | collective-permute-start | bytes 3145736 | tf_op jit(solution)/shard_map/ppermute | solution.py:248
  416.9 59.1 %collective-permute-start.73 = (bf16[128,1408]{0,1:T(8,128)(2,1)}, bf16[128,1408]{0,1:T(8,128)(2,1)}, u32[]{:S(2)}, u32[]{:S(2)}) collective-permute-start(bf16[128,1408]{0,1:T(8,128)(2,1)} %fusion.37), channel_id=1, source_target_pairs={{0,2},{1,3},{2,0},{3,1},{4,6},{5,7},{6,4},{7,5},{8,10},{9,11},{10,... | collective-permute-start | bytes 1081352 | tf_op jit(solution)/shard_map/ppermute | solution.py:248
  421.1 55.9 %collective-permute-start.71 = (bf16[128,1408]{0,1:T(8,128)(2,1)S(1)}, bf16[128,1408]{0,1:T(8,128)(2,1)S(1)}, u32[]{:S(2)}, u32[]{:S(2)}) collective-permute-start(bf16[128,1408]{0,1:T(8,128)(2,1)S(1)} %fusion.36), channel_id=1, source_target_pairs={{0,4},{1,5},{2,6},{3,7},{4,0},{5,1},{6,2},{7,3},{8,12},{9,13},{10,... | collective-permute-start | bytes 1081352 | tf_op jit(solution)/shard_map/ppermute | solution.py:248
  475.7 65.2 %collective-permute-start.36 = (bf16[512,512]{1,0:T(8,128)(2,1)}, bf16[512,512]{1,0:T(8,128)(2,1)}, u32[]{:S(2)}, u32[]{:S(2)}) collective-permute-start(bf16[512,512]{1,0:T(8,128)(2,1)} %get-tuple-element.95), channel_id=1, source_target_pairs={{0,8},{8,0},{16,24},{24,16},{1,9},{9,1},{17,25},{25,17},{2,10},{10... | collective-permute-start | bytes 1572872 | tf_op jit(solution)/shard_map/ppermute | solution.py:202
  495.9 29.5 %collective-permute-start.44 = (f32[4,128]{1,0:T(4,128)S(1)}, f32[4,128]{1,0:T(4,128)S(1)}, u32[]{:S(2)}, u32[]{:S(2)}) collective-permute-start(f32[4,128]{1,0:T(4,128)S(1)} %bitcast.280), channel_id=1, source_target_pairs={{0,8},{8,0},{16,24},{24,16},{1,9},{9,1},{17,25},{25,17},{2,10},{10... | collective-permute-start | bytes 6152 | tf_op jit(solution)/shard_map/ppermute | solution.py:202
  537.2 30.6 %collective-permute-start.39 = (bf16[512,512]{1,0:T(8,128)(2,1)}, bf16[512,512]{1,0:T(8,128)(2,1)S(1)}, u32[]{:S(2)}, u32[]{:S(2)}) collective-permute-start(bf16[512,512]{1,0:T(8,128)(2,1)} %constant_dynamic-slice_fusion.6), channel_id=1, source_target_pairs={{0,8},{8,0},{16,24},{24,16},{1,9},{9,1},{17,25},{25,17},{2,10},{10... | collective-permute-start | bytes 1572872 | tf_op jit(solution)/shard_map/ppermute | solution.py:202
  543.1 58.8 %collective-permute-start.37 = (bf16[512,512]{1,0:T(8,128)(2,1)}, bf16[512,512]{1,0:T(8,128)(2,1)}, u32[]{:S(2)}, u32[]{:S(2)}) collective-permute-start(bf16[512,512]{1,0:T(8,128)(2,1)} %fusion.93), channel_id=1, source_target_pairs={{8,16},{16,8},{9,17},{17,9},{10,18},{18,10},{11,19},{19,11},{12,20... | collective-permute-start | bytes 1572872 | tf_op jit(solution)/shard_map/ppermute | solution.py:202
  549.1 53.9 %collective-permute-start.35 = (bf16[512,512]{1,0:T(8,128)(2,1)}, bf16[512,512]{1,0:T(8,128)(2,1)}, u32[]{:S(2)}, u32[]{:S(2)}) collective-permute-start(bf16[512,512]{1,0:T(8,128)(2,1)} %dynamic-slice_add_fusion.1), channel_id=1, source_target_pairs={{0,8},{8,0},{16,24},{24,16},{1,9},{9,1},{17,25},{25,17},{2,10},{10... | collective-permute-start | bytes 1572872 | tf_op jit(solution)/shard_map/ppermute | solution.py:202
  566.7 29.6 %collective-permute-start.61 = (bf16[128,512]{0,1:T(8,128)(2,1)S(1)}, bf16[128,512]{0,1:T(8,128)(2,1)}, u32[]{:S(2)}, u32[]{:S(2)}) collective-permute-start(bf16[128,512]{0,1:T(8,128)(2,1)S(1)} %fusion.40), channel_id=1, source_target_pairs={{0,4},{1,5},{2,6},{3,7},{4,0},{5,1},{6,2},{7,3},{8,12},{9,13},{10,... | collective-permute-start | bytes 393224 | tf_op jit(solution)/shard_map/ppermute | solution.py:248
  570.2 24.0 %collective-permute-start.40 = (bf16[512,512]{1,0:T(8,128)(2,1)}, bf16[512,512]{1,0:T(8,128)(2,1)}, u32[]{:S(2)}, u32[]{:S(2)}) collective-permute-start(bf16[512,512]{1,0:T(8,128)(2,1)} %get-tuple-element.92), channel_id=1, source_target_pairs={{8,16},{16,8},{9,17},{17,9},{10,18},{18,10},{11,19},{19,11},{12,20... | collective-permute-start | bytes 1572872 | tf_op jit(solution)/shard_map/ppermute | solution.py:202
  591.2 26.6 %collective-permute-start.67 = (bf16[2,128,2816]{2,1,0:T(8,128)(2,1)S(1)}, bf16[2,128,2816]{2,1,0:T(8,128)(2,1)S(1)}, u32[]{:S(2)}, u32[]{:S(2)}) collective-permute-start(bf16[2,128,2816]{2,1,0:T(8,128)(2,1)S(1)} %fusion.19), channel_id=1, source_target_pairs={{0,4},{1,5},{2,6},{3,7},{4,0},{5,1},{6,2},{7,3},{8,12},{9,13},{10,... | collective-permute-start | bytes 4325384 | tf_op jit(solution)/shard_map/ppermute | solution.py:248
  601.9 37.0 %collective-permute-start.51 = (bf16[2,2,256,1536]{2,3,1,0:T(8,128)(2,1)S(1)}, bf16[2,2,256,1536]{2,3,1,0:T(8,128)(2,1)S(1)}, u32[]{:S(2)}, u32[]{:S(2)}) collective-permute-start(bf16[2,2,256,1536]{2,3,1,0:T(8,128)(2,1)S(1)} %bitcast.257), channel_id=1, source_target_pairs={{0,1},{1,0},{2,3},{3,2},{4,5},{5,4},{6,7},{7,6},{8,9},{9,8},{10,11... | collective-permute-start | bytes 9437192 | tf_op jit(solution)/shard_map/ppermute | solution.py:248
  603.0 34.4 %collective-permute-start.65 = (bf16[2,128,2816]{2,1,0:T(8,128)(2,1)S(1)}, bf16[2,128,2816]{2,1,0:T(8,128)(2,1)S(1)}, u32[]{:S(2)}, u32[]{:S(2)}) collective-permute-start(bf16[2,128,2816]{2,1,0:T(8,128)(2,1)S(1)} %fusion.18), channel_id=1, source_target_pairs={{0,2},{1,3},{2,0},{3,1},{4,6},{5,7},{6,4},{7,5},{8,10},{9,11},{10,... | collective-permute-start | bytes 4325384 | tf_op jit(solution)/shard_map/ppermute | solution.py:248
  618.2 34.8 %collective-permute-start.68 = (bf16[128,2816]{1,0:T(8,128)(2,1)S(1)}, bf16[128,2816]{1,0:T(8,128)(2,1)}, u32[]{:S(2)}, u32[]{:S(2)}) collective-permute-start(bf16[128,2816]{1,0:T(8,128)(2,1)S(1)} %fusion.25), channel_id=1, source_target_pairs={{0,2},{1,3},{2,0},{3,1},{4,6},{5,7},{6,4},{7,5},{8,10},{9,11},{10,... | collective-permute-start | bytes 2162696 | tf_op jit(solution)/shard_map/ppermute | solution.py:248
  640.1 32.0 %collective-permute-start.54 = (bf16[2,128,1536]{1,2,0:T(8,128)(2,1)S(1)}, bf16[2,128,1536]{1,2,0:T(8,128)(2,1)S(1)}, u32[]{:S(2)}, u32[]{:S(2)}) collective-permute-start(bf16[2,128,1536]{1,2,0:T(8,128)(2,1)S(1)} %fusion.23), channel_id=1, source_target_pairs={{0,4},{1,5},{2,6},{3,7},{4,0},{5,1},{6,2},{7,3},{8,12},{9,13},{10,... | collective-permute-start | bytes 2359304 | tf_op jit(solution)/shard_map/ppermute | solution.py:248
  641.3 32.6 %collective-permute-start.52 = (bf16[2,128,1536]{1,2,0:T(8,128)(2,1)S(1)}, bf16[2,128,1536]{1,2,0:T(8,128)(2,1)S(1)}, u32[]{:S(2)}, u32[]{:S(2)}) collective-permute-start(bf16[2,128,1536]{1,2,0:T(8,128)(2,1)S(1)} %fusion.22), channel_id=1, source_target_pairs={{0,2},{1,3},{2,0},{3,1},{4,6},{5,7},{6,4},{7,5},{8,10},{9,11},{10,... | collective-permute-start | bytes 2359304 | tf_op jit(solution)/shard_map/ppermute | solution.py:248
  (112 other events, 1181.8 us)
Sparse Core Ops, SparseCore 0:
  10.5 49.3 all-gather.5
  61.8 33.1 all-gather.7
  97.4 73.7 all-gather.11
  173.0 44.3 all-gather.9

commit v3 on v2

v3 whole, which is shorter than its diff:
```python
import functools

import jax
import jax.numpy as jnp
from jax import lax
from jax.experimental import pallas as pl
from jax.experimental.pallas import tpu as pltpu
from jax.sharding import PartitionSpec as P

norm_eps = 1e-05
half_modes = 8
f32 = jnp.float32
bf16 = jnp.bfloat16


lane_block = 128
step = 8


def times(a_re, a_im, b_re, b_im):
    return a_re * b_re - a_im * b_im, a_re * b_im + a_im * b_re


def each_block(width, body):
    def run(block, carry):
        body(block, pl.ds(pl.multiple_of(block * lane_block, lane_block), lane_block))
        return carry

    lax.fori_loop(0, width // lane_block, run, 0)


def widen(src_ref, dst_ref):
    for block in range(dst_ref.shape[0]):
        dst_ref[block] = src_ref[:, block * lane_block : (block + 1) * lane_block].astype(f32)


def narrow(src_ref, direct_ref, skip_ref, dst_ref):
    for block in range(src_ref.shape[0]):
        lanes = slice(block * lane_block, (block + 1) * lane_block)
        dst_ref[:, lanes] = (src_ref[block] + skip_ref[:, lanes] * direct_ref[block]).astype(bf16)


def load_pairs(ref, index, lanes):
    return [(ref[index, h, :, lanes], ref[index + 1, h, :, lanes]) for h in range(2)]


def edge_kernel(batches, reverse, keep_ref, u_ref, par_ref, edge_ref, u_wide):
    tokens, share = u_ref.shape
    rows = tokens // batches
    widen(u_ref, u_wide)

    def on_lanes(at, lanes):
        turn = load_pairs(par_ref, 0, lanes)

        def body(block, states):
            states = [list(own) for own in states]
            for i in range(step):
                t = block * step + i
                t = rows - 1 - t if reverse else t
                for m in range(batches):
                    keep = keep_ref[m, t]
                    row = u_wide[at, pl.ds(m * rows + t, 1), :]
                    for h in range(2):
                        re, im = states[m][h]
                        turn_re, turn_im = turn[h][0] * keep, turn[h][1] * keep
                        if reverse:
                            states[m][h] = times(turn_re, turn_im, re + row, im)
                        else:
                            re, im = times(turn_re, turn_im, re, im)
                            states[m][h] = (re + row, im)
            return tuple(tuple(own) for own in states)

        zero = jnp.zeros((half_modes, lane_block), f32)
        states = lax.fori_loop(0, rows // step, body, (((zero, zero),) * 2,) * batches)
        for m in range(batches):
            for h in range(2):
                edge_ref[m, 0, h, :, lanes], edge_ref[m, 1, h, :, lanes] = states[m][h]

    each_block(share, on_lanes)


def load_states(ref, batches, lanes):
    return tuple(
        tuple((ref[m, 0, h, :, lanes], ref[m, 1, h, :, lanes]) for h in range(2)) for m in range(batches)
    )


def conv_kernel(batches, keep_ref, u_ref, into_ref, par_ref, skip_ref, y_ref, u_wide, y_wide):
    tokens, share = u_ref.shape
    rows = tokens // batches
    widen(u_ref, u_wide)

    def on_lanes(at, lanes):
        turn, res = (load_pairs(par_ref, 2 * i, lanes) for i in range(2))

        def body(block, states):
            states = [list(own) for own in states]
            for i in range(step):
                t = block * step + i
                for m in range(batches):
                    keep = keep_ref[m, t]
                    row = u_wide[at, pl.ds(m * rows + t, 1), :]
                    out = []
                    for h in range(2):
                        re, im = times(turn[h][0] * keep, turn[h][1] * keep, *states[m][h])
                        re = re + row
                        states[m][h] = (re, im)
                        out.append(res[h][0] * re - res[h][1] * im)
                    y_wide[at, pl.ds(m * rows + t, 1), :] = jnp.sum(out[0] + out[1], axis=0, keepdims=True)
            return tuple(tuple(own) for own in states)

        lax.fori_loop(0, rows // step, body, load_states(into_ref, batches, lanes))

    each_block(share, on_lanes)
    narrow(y_wide, u_wide, skip_ref, y_ref)


def back_kernel(
    batches,
    keep_ref,
    u_ref,
    g_ref,
    into_ref,
    behind_ref,
    par_ref,
    skip_ref,
    d_ref,
    sums_ref,
    skip_sum_ref,
    u_wide,
    g_wide,
    d_wide,
    kept,
):
    tokens, share = u_ref.shape
    rows = tokens // batches
    widen(u_ref, u_wide)
    widen(g_ref, g_wide)

    def on_lanes(at, lanes):
        turn, res = (load_pairs(par_ref, 2 * i, lanes) for i in range(2))

        def ahead(block, states):
            states = [list(own) for own in states]
            for i in range(step):
                t = block * step + i
                for m in range(batches):
                    keep = keep_ref[m, t]
                    row = u_wide[at, pl.ds(m * rows + t, 1), :]
                    for h in range(2):
                        re, im = times(turn[h][0] * keep, turn[h][1] * keep, *states[m][h])
                        kept[t, m, h, 0], kept[t, m, h, 1] = re, im
                        states[m][h] = (re + row, im)
            return tuple(tuple(own) for own in states)

        lax.fori_loop(0, rows // step, ahead, load_states(into_ref, batches, lanes))
        start = load_states(behind_ref, batches, lanes)

        def behind(block, carry):
            states, sums = [list(own) for own in carry[0]], list(carry[1])
            for i in range(step):
                t = rows - 1 - (block * step + i)
                for m in range(batches):
                    keep = keep_ref[m, t]
                    row = g_wide[at, pl.ds(m * rows + t, 1), :]
                    out = []
                    for h in range(2):
                        re, im = states[m][h]
                        re = re + row
                        x_re, x_im = kept[t, m, h, 0], kept[t, m, h, 1]
                        lag_re, lag_im = times(re, im, x_re, x_im)
                        g_re, g_im, w_re, w_im = sums[h]
                        sums[h] = (g_re + row * x_re, g_im + row * x_im, w_re + lag_re, w_im + lag_im)
                        out.append(res[h][0] * re - res[h][1] * im)
                        states[m][h] = times(turn[h][0] * keep, turn[h][1] * keep, re, im)
                    d_wide[at, pl.ds(m * rows + t, 1), :] = jnp.sum(out[0] + out[1], axis=0, keepdims=True)
            return tuple(tuple(own) for own in states), tuple(sums)

        zero = jnp.zeros((half_modes, lane_block), f32)
        skip_sum = jnp.sum(u_wide[at] * g_wide[at], axis=0, keepdims=True)
        skip_sum_ref[:, lanes] = skip_sum
        _, sums = lax.fori_loop(0, rows // step, behind, (start, ((zero,) * 4,) * 2))
        for h in range(2):
            g_re, g_im, w_re, w_im = sums[h]
            lag_re, lag_im = times(*res[h], w_re, w_im)
            sums_ref[0, h, :, lanes] = zero - lag_re
            sums_ref[1, h, :, lanes] = zero - lag_im
            sums_ref[2, h, :, lanes] = g_re + skip_sum
            sums_ref[3, h, :, lanes] = zero - g_im

    each_block(share, on_lanes)
    narrow(d_wide, g_wide, skip_ref, d_ref)


def in_vmem():
    return pl.BlockSpec(memory_space=pltpu.VMEM)


def in_smem():
    return pl.BlockSpec(memory_space=pltpu.SMEM)


def scratch_rows(u):
    return pltpu.VMEM((u.shape[1] // lane_block, u.shape[0], lane_block), f32)


def edge_states(u, keep, params, reverse):
    batches = keep.shape[0]
    return pl.pallas_call(
        functools.partial(edge_kernel, batches, reverse),
        out_shape=jax.ShapeDtypeStruct((batches, 2) + params.shape[1:], f32),
        in_specs=[in_smem(), in_vmem(), in_vmem()],
        out_specs=in_vmem(),
        scratch_shapes=[scratch_rows(u)],
        compiler_params=pltpu.CompilerParams(vmem_limit_bytes=48 << 20),
    )(keep, u, params)


def long_conv(keep, u, into, params, skips):
    return pl.pallas_call(
        functools.partial(conv_kernel, keep.shape[0]),
        out_shape=jax.ShapeDtypeStruct(u.shape, bf16),
        in_specs=[in_smem()] + [in_vmem()] * 4,
        out_specs=in_vmem(),
        scratch_shapes=[scratch_rows(u)] * 2,
        compiler_params=pltpu.CompilerParams(vmem_limit_bytes=48 << 20),
    )(keep, u, into, params, skips)


def long_conv_back(keep, u, g, into, behind, params, skips):
    batches, rows = keep.shape
    return pl.pallas_call(
        functools.partial(back_kernel, batches),
        out_shape=(
            jax.ShapeDtypeStruct(u.shape, bf16),
            jax.ShapeDtypeStruct((4,) + params.shape[1:], f32),
            jax.ShapeDtypeStruct((1, u.shape[1]), f32),
        ),
        in_specs=[in_smem()] + [in_vmem()] * 6,
        out_specs=(in_vmem(),) * 3,
        scratch_shapes=[scratch_rows(u)] * 3 + [pltpu.VMEM((rows, batches, 2, 2, half_modes, lane_block), f32)],
        compiler_params=pltpu.CompilerParams(vmem_limit_bytes=48 << 20),
    )(keep, u, g, into, behind, params, skips)


def shifted(array, axis, by):
    size = lax.axis_size(axis)
    pairs = [(i, i + by) for i in range(size) if 0 <= i + by < size]
    return lax.ppermute(array, axis, pairs)


def places_of(doc_lens, total):
    tokens = jnp.arange(total, dtype=jnp.int32)
    starts = jnp.cumsum(doc_lens, dtype=jnp.int32) - doc_lens
    begins = jnp.max(jnp.where(starts[None, :] <= tokens[:, None], starts[None, :], 0), axis=1)
    return tokens - begins


def dot_rows(left, right):
    return lax.dot_general(left, right, (((1,), (1,)), ((), ())), preferred_element_type=f32)


def dot_tokens(left, right):
    return lax.dot_general(left, right, (((0,), (0,)), ((), ())), preferred_element_type=f32)


def dot(left, right):
    return jnp.dot(left, right, preferred_element_type=f32)


def along_line(array, pairs):
    return lax.ppermute(array, "fsdp", pairs)


outer_pairs = [(0, 1), (1, 0), (2, 3), (3, 2)]
inner_pairs = [(1, 2), (2, 1)]


def after(value, *others):
    return lax.optimization_barrier((value,) + others)[0]


def gather_first(share):
    return along_line(share, outer_pairs), along_line(share, inner_pairs)


def gather_second(first):
    next_one, inner_one = first
    return along_line(inner_one, outer_pairs), along_line(next_one, inner_pairs)


def gather_last(second):
    return along_line(second[1], outer_pairs)


def gathered(share, first, second, last):
    own = lax.axis_index("fsdp")
    by_offset = (share, first[0], second[0] + second[1], last + first[1])
    blocks = []
    for place in range(4):
        offset = own ^ place
        block = by_offset[3]
        for k in range(3):
            block = jnp.where(offset == k, by_offset[k], block)
        blocks.append(block)
    return lax.optimization_barrier(jnp.concatenate(blocks, axis=1))


def gather_share(share):
    first = gather_first(share)
    second = gather_second(first)
    return gathered(share, first, second, gather_last(second))


def part_of(partial_sums, offset):
    share = partial_sums.shape[1] // 4
    return lax.dynamic_slice_in_dim(partial_sums, (lax.axis_index("fsdp") ^ offset) * share, share, 1)


def scatter_first(partial_sums):
    return along_line(part_of(partial_sums, 3), outer_pairs), along_line(part_of(partial_sums, 2), outer_pairs)


def scatter_second(partial_sums, first):
    far, near = first
    return (
        along_line(part_of(partial_sums, 2) + far, inner_pairs),
        along_line(part_of(partial_sums, 3) + near, inner_pairs),
    )


def scatter_last(partial_sums, second):
    return along_line(part_of(partial_sums, 1) + second[0], outer_pairs)


def scattered(partial_sums, second, last):
    return part_of(partial_sums, 0).astype(f32) + last.astype(f32) + second[1].astype(f32)


def scatter_offloaded(partial_sums):
    return lax.psum_scatter(partial_sums, "fsdp", scatter_dimension=1, tiled=True).astype(f32)


def sum_line(array):
    array = array + along_line(array, outer_pairs)
    return array + along_line(array, [(i, i ^ 2) for i in range(4)])


def swap_seq(array, bit):
    return lax.ppermute(array, "seq", [(i, i ^ (1 << bit)) for i in range(lax.axis_size("seq"))])


def gather_weight(shard):
    return lax.all_gather(shard, "seq", axis=0, tiled=True)


def of_core(left, core):
    count = lax.axis_size("seq")
    rows = left.shape[1] // count
    parts = [lax.dynamic_slice_in_dim(left, (2 * chip + core) * rows, rows, 1) for chip in range(count // 2)]
    return lax.optimization_barrier(jnp.concatenate(parts, axis=1))


def core_give(left, right):
    core = lax.axis_index("seq") % 2
    return lax.optimization_barrier(dot_tokens(of_core(left, 1 - core), right).astype(bf16))


def core_sum(left, right, got):
    own = dot_tokens(of_core(left, lax.axis_index("seq") % 2), right)
    return lax.optimization_barrier((own + got.astype(f32)).astype(bf16))


def chip_sums_offloaded(summed):
    count = lax.axis_size("seq")
    groups = [list(range(core, count, 2)) for core in range(2)]
    return lax.psum_scatter(summed, "seq", scatter_dimension=0, axis_index_groups=groups, tiled=True).astype(f32)


def chip_sums(summed):
    count = lax.axis_size("seq")
    rank = lax.axis_index("seq")
    rows, bits = 2 * summed.shape[0] // count, count.bit_length() - 1
    by_bits = summed.reshape((2,) * (bits - 1) + (rows, summed.shape[1]))

    def halve(array, rest, bit):
        dim, mine = rest.index(bit), (rank >> bit) & 1
        keep = lax.dynamic_index_in_dim(array, mine, dim, keepdims=False)
        give = lax.dynamic_index_in_dim(array, 1 - mine, dim, keepdims=False)
        got = swap_seq(give.astype(bf16), bit)
        return keep.astype(f32) + got.astype(f32), [other for other in rest if other != bit]

    chip_bits = list(range(1, bits))
    middle = len(chip_bits) // 2
    parts = []
    for half, order in enumerate((chip_bits, chip_bits[middle:] + chip_bits[:middle])):
        part = lax.slice_in_dim(by_bits, half * rows // 2, (half + 1) * rows // 2, axis=bits - 1)
        rest = chip_bits[::-1]
        for bit in order:
            part, rest = halve(part, rest, bit)
        parts.append(part)
    return lax.optimization_barrier(jnp.concatenate(parts, axis=0))


def passing_factors(whole, power, reverse):
    count = lax.axis_size("seq")
    rank = lax.axis_index("seq")
    if reverse:
        rank, whole = count - 1 - rank, whole[:, ::-1]
    devices = jnp.arange(count)

    def factor(exponent, within):
        kept = jnp.min(jnp.where(within, whole, 1.0), axis=1)[:, None, None, None]
        return jnp.stack([part * kept for part in power(exponent)])

    steps = []
    for bit in range(count.bit_length() - 1):
        size = 1 << bit
        group = rank // size
        later = (group % 2).astype(f32)
        ahead = factor((rank % size).astype(f32), (devices // size == group) & (devices < rank)) * later
        last = factor(float(size), devices // size == (group | 1))
        steps.append((ahead, last))
    return lax.optimization_barrier(steps)


def through(edge, factors, reverse):
    count = lax.axis_size("seq")
    rank = lax.axis_index("seq")
    if reverse:
        rank = count - 1 - rank

    def grown(factor, state):
        re, im = times(factor[0], factor[1], state[:, 0], state[:, 1])
        return jnp.stack([re, im], axis=1)

    into = jnp.zeros_like(edge)
    for bit, (ahead, last) in enumerate(factors):
        later = (rank >> bit) & 1 == 1
        got = swap_seq(edge, bit)
        into = into + grown(ahead, got)
        if bit + 1 < len(factors):
            edge = jnp.where(later, edge, got) + grown(last, jnp.where(later, got, edge))
    return into


def sum_seq(array):
    for bit in range(lax.axis_size("seq").bit_length() - 1):
        array = array + swap_seq(array, bit)
    return array


def on_device(
    hidden_in,
    out_cot,
    doc_lengths,
    mixer_gain,
    in_proj,
    short_filter,
    decay_rate,
    mode_angle,
    residue_re,
    residue_im,
    skip_gain,
    out_proj,
    feed_gain,
    gate_proj,
    up_proj,
    down_proj,
):
    batches, rows, share = hidden_in.shape
    tokens = batches * rows
    width = mixer_gain.shape[0]
    seq_count = lax.axis_size("seq")
    seq_rank = lax.axis_index("seq")
    fsdp_rank = lax.axis_index("fsdp")
    total = rows * seq_count
    d_rows = in_proj.shape[0]

    x_share = hidden_in.reshape(tokens, share)
    cot_share = out_cot.reshape(tokens, share)
    x_all = gather_share(x_share).astype(f32)
    units = gate_proj.shape[1]
    w_in = gather_weight(in_proj.reshape(d_rows, 3 * share))
    w_both = gather_weight(jnp.concatenate([out_proj.T, down_proj.T], axis=1))
    w_out, w_down = w_both[:, :share], w_both[:, share:]
    w_feed = gather_weight(jnp.concatenate([gate_proj, up_proj], axis=1))

    places = jnp.stack([places_of(doc_lengths[m], total) for m in range(batches)])
    keep = (places > 0).astype(f32)
    places_here = lax.dynamic_slice_in_dim(places, seq_rank * rows, rows, 1)
    masks = [(places_here >= lag).astype(f32)[:, :, None] for lag in range(3)]
    taps = short_filter.reshape(3, 3 * share)

    keep_here = lax.dynamic_slice_in_dim(keep, seq_rank * rows, rows, 1)
    whole = jnp.min(keep.reshape(batches, seq_count, rows), axis=2)
    rates, angles, res_re, res_im = (
        part.T.reshape(2, half_modes, share) for part in (decay_rate, mode_angle, residue_re, residue_im)
    )

    def power(devices):
        fading = jnp.exp(-(devices * rows) * rates)
        return fading * jnp.cos((devices * rows) * angles), fading * jnp.sin((devices * rows) * angles)

    fading = jnp.exp(-rates)
    modes = jnp.stack([fading * jnp.cos(angles), fading * jnp.sin(angles), res_re, res_im])
    skips = skip_gain[None]
    factors = passing_factors(whole, power, False)
    back_factors = passing_factors(whole, power, True)

    scale_one = lax.rsqrt(jnp.mean(x_all * x_all, axis=-1, keepdims=True) + norm_eps)
    unit_one = x_all * scale_one
    normed_one = after((unit_one * mixer_gain).astype(bf16), modes, factors, back_factors)
    project = dot(normed_one, w_in).reshape(batches, rows, 3 * share)
    extended = jnp.concatenate([shifted(project[:, -2:], "seq", 1), project], axis=1)
    lagged = [extended[:, 2 - lag : 2 - lag + rows] for lag in range(3)]
    conv = sum(taps[lag] * masks[lag] * lagged[lag] for lag in range(3)).reshape(tokens, 3 * share)
    gate_one, gate_two, values = (conv[:, j * share : (j + 1) * share] for j in range(3))
    product = (gate_two * values).astype(bf16)
    cot_late = after(cot_share, product)
    cot_first = gather_first(cot_late)
    into = through(edge_states(product, keep_here, modes, False), factors, False)
    cot_second = gather_second(cot_first)
    mixed = long_conv(keep_here, product, after(into, *cot_first), modes, skips)
    cot_last = gather_last(cot_second)
    mixed = after(mixed, *cot_second).astype(f32)
    gated = (gate_one * mixed).astype(bf16)
    mix_part = dot_rows(gated, w_out).astype(bf16)
    mix_first = scatter_first(mix_part)
    mix_second = scatter_second(mix_part, mix_first)
    cot_all = gathered(cot_share, cot_first, cot_second, after(cot_last, mix_first[0]))
    d_hidden = lax.optimization_barrier(dot(cot_all, w_down))
    mix_last = scatter_last(mix_part, mix_second)
    stream = x_share.astype(f32) + scattered(mix_part, mix_second, mix_last)
    stream_all = gather_share(stream.astype(bf16)).astype(f32)
    scale_two = lax.rsqrt(jnp.mean(stream_all * stream_all, axis=-1, keepdims=True) + norm_eps)
    unit_two = stream_all * scale_two
    normed_two = lax.optimization_barrier((unit_two * feed_gain).astype(bf16))
    feed_pre = dot(normed_two, w_feed)
    gate_pre, up_pre = feed_pre[:, :units], feed_pre[:, units:]
    sigmoid = jax.nn.sigmoid(gate_pre)
    activated = gate_pre * sigmoid
    hidden = (activated * up_pre).astype(bf16)

    d_gate = d_hidden * up_pre * sigmoid * (1.0 + gate_pre * (1.0 - sigmoid))
    d_up = d_hidden * activated
    d_feed = jnp.concatenate([d_gate.astype(bf16), d_up.astype(bf16)], axis=1)
    part_two = dot_rows(d_feed, w_feed).astype(bf16)
    two_first = scatter_first(part_two)
    along_two = jnp.sum(after(d_feed, part_two).astype(f32) * feed_pre, axis=-1)
    along_two = sum_line(along_two.reshape(-1, 128)).reshape(tokens, 1)
    feed_gain_part = jnp.sum(unit_two * after(part_two, two_first[0]).astype(f32), axis=0)
    down_got = swap_seq(core_give(cot_all, after(hidden, part_two)), 0)
    two_second = scatter_second(part_two, two_first)
    feed_got = swap_seq(core_give(normed_two, after(d_feed, two_first[0])), 0)
    two_last = scatter_last(part_two, two_second)
    down_sum = core_sum(cot_all, hidden, after(down_got, two_second[0]))

    def own_features(part):
        return lax.dynamic_slice_in_dim(part, fsdp_rank * share, share, 0)

    d_stream = (
        cot_share.astype(f32)
        + scale_two * own_features(feed_gain) * scattered(part_two, two_second, two_last)
        - stream * (scale_two * scale_two * along_two / width)
    )
    d_share = d_stream.astype(bf16)
    mix_one = gather_first(d_share)
    mix_two = gather_second(mix_one)
    down_grad = chip_sums_offloaded(down_sum)
    down_part = dot_rows(after(hidden, d_share), w_down).astype(bf16)
    feed_sum = core_sum(normed_two, d_feed, after(feed_got, mix_one[0]))
    feed_grad = chip_sums_offloaded(feed_sum)
    mix_three = gather_last(after(mix_two, feed_sum, down_part, feed_gain_part))
    d_mix = gathered(d_share, mix_one, mix_two, mix_three)

    d_gated = lax.optimization_barrier(dot(d_mix, w_out))
    down_first = scatter_first(after(down_part, d_gated))
    d_gate_one = d_gated * mixed
    d_mixed = (d_gated * gate_one).astype(bf16)
    behind = through(edge_states(d_mixed, keep_here, modes, True), back_factors, True)
    down_second = scatter_second(down_part, down_first)
    out_sum = core_sum(d_mix, gated, swap_seq(core_give(d_mix, after(gated, d_mixed)), 0))
    down_last = scatter_last(down_part, down_second)
    out_grad = chip_sums_offloaded(out_sum)
    d_product, mode_sums, skip_sums = long_conv_back(
        keep_here, product, d_mixed, into, after(behind, *down_second), modes, skips
    )
    d_product = after(d_product, out_sum, down_last)
    block_out = stream + scattered(down_part, down_second, down_last)
    d_product = d_product.astype(f32)
    d_conv = jnp.concatenate([d_gate_one, d_product * values, d_product * gate_two], axis=1)
    d_conv = d_conv.reshape(batches, rows, 3 * share)
    short_part = jnp.stack([jnp.sum(masks[lag] * lagged[lag] * d_conv, axis=(0, 1)) for lag in range(3)])
    spread = sum(
        jnp.pad(taps[lag] * masks[lag] * d_conv, ((0, 0), (2 - lag, lag), (0, 0))) for lag in range(3)
    )
    returned = shifted(spread[:, :2], "seq", -1)
    d_project = spread[:, 2:] + jnp.pad(returned, ((0, 0), (rows - 2, 0), (0, 0)))
    d_project = d_project.astype(bf16).reshape(tokens, 3 * share)
    along_one = jnp.sum(d_project.astype(f32) * project.reshape(tokens, 3 * share), axis=-1)
    along_one = sum_line(along_one.reshape(-1, 128)).reshape(tokens, 1)
    part_one = dot_rows(d_project, w_in).astype(bf16)
    mixer_gain_part = jnp.sum(unit_one * part_one.astype(f32), axis=0)
    one_first = scatter_first(part_one)
    in_got = swap_seq(core_give(normed_one, after(d_project, part_one)), 0)
    one_second = scatter_second(part_one, one_first)
    in_sum = core_sum(normed_one, d_project, in_got)
    one_last = scatter_last(part_one, after(one_second, in_sum))
    d_x = (
        d_stream
        + scale_one * own_features(mixer_gain) * scattered(part_one, one_second, one_last)
        - x_share.astype(f32) * (scale_one * scale_one * along_one / width)
    )

    in_grad = chip_sums_offloaded(in_sum).reshape(d_rows, 3, share)
    small = [mixer_gain_part, feed_gain_part, short_part, mode_sums, skip_sums]
    small = sum_seq(jnp.concatenate([part.reshape(-1, 128) for part in small]))
    gains = sum_line(small[: 2 * width // 128]).reshape(2, width)
    small = small[2 * width // 128 :].reshape(-1, share)
    short_grad = small[:9].reshape(3, 3, share)
    filters = small[9:]
    by_chan = filters[:-1].reshape(4, 2 * half_modes, share).transpose(0, 2, 1)
    return (
        block_out.astype(bf16).reshape(hidden_in.shape),
        d_x.reshape(hidden_in.shape),
        gains[0],
        in_grad,
        short_grad,
        by_chan[0],
        by_chan[1],
        by_chan[2],
        by_chan[3],
        filters[-1],
        out_grad.T,
        gains[1],
        feed_grad[:, :units],
        feed_grad[:, units:],
        down_grad.T,
    )


def solution(mesh):
    tokens = P(None, "seq", "fsdp")
    chan_rows = P("fsdp", None)
    d_rows = P("seq", "fsdp")
    d_cols = P("fsdp", "seq")
    in_specs = (
        tokens,
        tokens,
        P(),
        P(),
        P("seq", None, "fsdp"),
        P(None, None, "fsdp"),
        chan_rows,
        chan_rows,
        chan_rows,
        chan_rows,
        P("fsdp"),
        d_cols,
        P(),
        d_rows,
        d_rows,
        d_cols,
    )
    out_specs = (
        tokens,
        tokens,
        P(),
        P("seq", None, "fsdp"),
        P(None, None, "fsdp"),
        chan_rows,
        chan_rows,
        chan_rows,
        chan_rows,
        P("fsdp"),
        d_cols,
        P(),
        d_rows,
        d_rows,
        d_cols,
    )
    return jax.shard_map(on_device, mesh=mesh, in_specs=in_specs, out_specs=out_specs, check_vma=False)
```

time: 703 us -> 577 us (0.82)
  waiting for transfers between devices: 196 us -> 141 us
  local copies, waits for them, and re-layouts: 94.3 us -> 42.9 us
  starting transfers between devices: 172 us -> 158 us
  blocking collectives: 8.34 us -> 0 us
    ppermute x26 -> x13, waiting for transfers between devices: 71.9 us -> 19.4 us  [swap_seq(): lax.ppermute(array, 'seq', [(i, i ^ 1 << bit) for i in range(lax.axis_siz...]
    add x32 -> x17, other arithmetic: 44.1 us -> 12.2 us  [the longest x4 4.83 us: scatter_last(): return along_line(part_of(partial_sums, 1) + second[0], outer_pairs)]
    ppermute x46, waiting for transfers between devices: 89.8 us -> 121 us  [along_line(): return lax.ppermute(array, 'fsdp', pairs)]
    all_to_all x4 -> x0, waiting for transfers between devices: 29.9 us -> none  [the longest x2 15.6 us: to_tokens(): lax.all_to_all(channel_side.reshape(count, rows, width), 'seq', split_axi...]
    ppermute x46, starting transfers between devices: 119 us -> 147 us  [along_line(): return lax.ppermute(array, 'fsdp', pairs)]
    ppermute x26 -> x13, starting transfers between devices: 31 us -> 6.48 us  [swap_seq(): lax.ppermute(array, 'seq', [(i, i ^ 1 << bit) for i in range(lax.axis_siz...]
    all_to_all x4 -> x0, starting transfers between devices: 18 us -> none  [the longest x2 10.8 us: to_channels(): lax.all_to_all(pieces.reshape(count, rows, batches * part), 'seq', split_...]
    convert_element_type x21 -> x0, local copies, waits for them, and re-layouts: 17.7 us -> none  [the longest x2 6.03 us: on_device(): d_product = to_tokens(back_out, batches).astype(f32)]
  transfers between devices with their start and end apart: 82 -> 68, of which waited for: 34 -> 25; matrix products, arithmetic and copies ran while one was open for 31% -> 28% of each run, Pallas kernels for 6% -> 9%
where the time goes in v3:
time: 577 us; the launch traced here: 567 us
  starting transfers between devices  158 us (27%)
  waiting for transfers between devices  141 us (24%)
  other arithmetic  84 us (15%)
  matrix products  74.4 us (13%)
  Pallas kernels  49.3 us (9%)
  local copies, waits for them, and re-layouts  42.9 us (7%)
  between operations  16.6 us (3%)
    ppermute x46, starting transfers between devices, along_line(): return lax.ppermute(array, 'fsdp', pairs)  147 us
    ppermute x46, waiting for transfers between devices, along_line(): return lax.ppermute(array, 'fsdp', pairs)  121 us
    dot_general x4, matrix products, dot(): return jnp.dot(left, right, preferred_element_type=f32)  27.2 us
    dot_general x4, matrix products, dot_rows(): lax.dot_general(left, right, (((1,), (1,)), ((), ())), preferred_element_...  24.6 us
    pallas_call x1, Pallas kernels, long_conv_back(): pl.pallas_call(functools.partial(back_kernel, batches), out_shape=(jax.Sh...  24.1 us
    dot_general x8, matrix products, dot_tokens(): lax.dot_general(left, right, (((0,), (0,)), ((), ())), preferred_element_...  22.6 us
    ppermute x13, waiting for transfers between devices, swap_seq(): lax.ppermute(array, 'seq', [(i, i ^ 1 << bit) for i in range(lax.axis_siz...  19.4 us
    unnamed x189, local copies, waits for them, and re-layouts  18.5 us
  transfers between devices with their start and end apart: 68, of which 25 were waited for; matrix products, arithmetic and copies ran while one was open for 28% of the time, Pallas kernels for 9%

profile of v3, /device:TPU:0, one launch (start us, length us, event | category | flops | bytes accessed | tf_op | source)
XLA Modules:
  0.0 566.8 jit_solution(8738662760562631609)
XLA Ops:
  33.6 11.2 %collective-permute-start.4 = (bf16[512,512]{1,0:T(8,128)(2,1)S(1)}, bf16[512,512]{1,0:T(8,128)(2,1)S(1)}, u32[]{:S(2)}, u32[]{:S(2)}) collective-permute-start(bf16[512,512]{1,0:T(8,128)(2,1)S(1)} %collective-permute-done.3), channel_id=1, source_target_pairs={{0,8},{8,0},{16,24},{24,16},{1,9},{9,1},{17,25},{25,17},{2,10},{10... | collective-permute-start | bytes 1572872 | tf_op jit(solution)/shard_map/ppermute | solution.py:272
  48.3 7.4 %collective-permute-done.4 = bf16[512,512]{1,0:T(8,128)(2,1)S(1)} collective-permute-done((bf16[512,512]{1,0:T(8,128)(2,1)S(1)}, bf16[512,512]{1,0:T(8,128)(2,1)S(1)}, u32[]{:S(2)}, u32[]{:S(2)}) %collective-permute-start.4) | collective-permute-done | bytes 524320 | tf_op jit(solution)/shard_map/ppermute | solution.py:272
  59.9 6.2 %fusion.67 = f32[512,1536]{1,0:T(8,128)S(1)} fusion(bf16[512,2048]{1,0:T(8,128)(2,1)} %fusion.10, bf16[2048,1536]{0,1:T(8,128)(2,1)} %all-gather.4.cloned.1.call-done), kind=kOutput, calls=%fused_computation.359 | convolution fusion | flops 3221225472 | bytes 11534336 | tf_op jit(solution)/shard_map/dot_general | solution.py:268
  77.5 6.9 %shard_map.271 = f32[2,2,2,8,512]{4,3,2,1,0:T(8,128)S(1)} custom-call(f32[2,256]{1,0:T(2,128)S(1)} %get-tuple-element.284.keep_ref, bf16[512,512]{1,0:T(8,128)(2,1)S(1)} %multiply_convert_fusion.4.u_ref, f32[4,2,8,512]{3,2,1,0:T(8,128)S(1)} %pad_maximum_fusion.17.par_ref), custom_call_target="tpu_custom_call" | custom-call | tf_op jit(solution)/shard_map/pallas_call | solution.py:209
  91.6 7.3 %collective-permute-done.7 = f32[2,2,2,8,512]{4,3,2,0,1:T(8,128)S(1)} collective-permute-done((f32[2,2,2,8,512]{4,3,2,0,1:T(8,128)S(1)}, f32[2,2,2,8,512]{4,3,2,0,1:T(8,128)S(1)}, u32[]{:S(2)}, u32[]{:S(2)}) %collective-permute-start.7) | collective-permute-done | bytes 131104 | tf_op jit(solution)/shard_map/ppermute | solution.py:350
  107.5 11.4 %shard_map.272 = bf16[512,512]{1,0:T(8,128)(2,1)S(1)} custom-call(f32[2,256]{1,0:T(2,128)S(1)} %get-tuple-element.284.keep_ref, bf16[512,512]{1,0:T(8,128)(2,1)S(1)} %multiply_convert_fusion.4.u_ref, f32[2,2,2,8,512]{4,3,2,1,0:T(8,128)S(1)} %copy.75.into_ref, f32[4,2,8,512]{3,2,1,0:T(8,128)S(1)} %pad_maximum_fusion.17.par_ref, f32[1,512]{1,0:T(1,128)S(1)} %bitcast.339), custom_call_target="tpu_custom_call" | custom-call | tf_op jit(solution)/shard_map/pallas_call | solution.py:220
  126.3 11.6 %collective-permute-done.13 = bf16[512,512]{1,0:T(8,128)(2,1)} collective-permute-done((bf16[512,512]{1,0:T(8,128)(2,1)S(1)}, bf16[512,512]{1,0:T(8,128)(2,1)}, u32[]{:S(2)}, u32[]{:S(2)}) %collective-permute-start.13) | collective-permute-done | bytes 524320 | tf_op jit(solution)/shard_map/ppermute | solution.py:272
  145.8 11.1 %collective-permute-start.15 = (bf16[512,512]{1,0:T(8,128)(2,1)}, bf16[512,512]{1,0:T(8,128)(2,1)S(1)}, u32[]{:S(2)}, u32[]{:S(2)}) collective-permute-start(bf16[512,512]{1,0:T(8,128)(2,1)} %dynamic-slice_add_fusion.5), channel_id=1, source_target_pairs={{0,8},{8,0},{16,24},{24,16},{1,9},{9,1},{17,25},{25,17},{2,10},{10... | collective-permute-start | bytes 1572872 | tf_op jit(solution)/shard_map/ppermute | solution.py:272
  163.0 7.0 %collective-permute-done.15 = bf16[512,512]{1,0:T(8,128)(2,1)S(1)} collective-permute-done((bf16[512,512]{1,0:T(8,128)(2,1)}, bf16[512,512]{1,0:T(8,128)(2,1)S(1)}, u32[]{:S(2)}, u32[]{:S(2)}) %collective-permute-start.15) | collective-permute-done | bytes 524320 | tf_op jit(solution)/shard_map/ppermute | solution.py:272
  190.9 9.0 %collective-permute-start.19 = (bf16[512,512]{1,0:T(8,128)(2,1)S(1)}, bf16[512,512]{1,0:T(8,128)(2,1)S(1)}, u32[]{:S(2)}, u32[]{:S(2)}) collective-permute-start(bf16[512,512]{1,0:T(8,128)(2,1)S(1)} %collective-permute-done.18), channel_id=1, source_target_pairs={{0,8},{8,0},{16,24},{24,16},{1,9},{9,1},{17,25},{25,17},{2,10},{10... | collective-permute-start | bytes 1572872 | tf_op jit(solution)/shard_map/ppermute | solution.py:272
  199.9 7.8 %collective-permute-start.22 = (bf16[512,512]{1,0:T(8,128)(2,1)S(1)}, bf16[512,512]{1,0:T(8,128)(2,1)S(1)}, u32[]{:S(2)}, u32[]{:S(2)}) collective-permute-start(bf16[512,512]{1,0:T(8,128)(2,1)S(1)} %collective-permute-done.21), channel_id=1, source_target_pairs={{0,8},{8,0},{16,24},{24,16},{1,9},{9,1},{17,25},{25,17},{2,10},{10... | collective-permute-start | bytes 1572872 | tf_op jit(solution)/shard_map/ppermute | solution.py:272
  207.7 7.7 %fusion.2 = f32[512,1408]{1,0:T(8,128)} fusion(bf16[512,2048]{1,0:T(8,128)(2,1)S(1)} %pad_maximum_fusion.5, bf16[2048,1920]{0,1:T(8,128)(2,1)} %all-gather.6.cloned.1.call-done), kind=kOutput, calls=%fused_computation.11 | convolution fusion | flops 2952790016 | bytes 10747904 | tf_op jit(solution)/shard_map/dot_general | solution.py:268
  226.2 10.3 %fusion.68 = f32[512,2816]{1,0:T(8,128)S(1)} fusion(bf16[512,2048]{1,0:T(8,128)(2,1)} %copy-done.12, bf16[2048,2816]{1,0:T(8,128)(2,1)} %all-gather.8.cloned.1.call-done), kind=kOutput, calls=%fused_computation.360 | convolution fusion | flops 5905580032 | bytes 19398656 | tf_op jit(solution)/shard_map/dot_general | solution.py:268
  238.4 9.6 %convolution_convert_fusion.4 = bf16[512,2048]{1,0:T(8,128)(2,1)S(1)} fusion(bf16[2048,2816]{1,0:T(8,128)(2,1)} %all-gather.8.cloned.1.call-done, bf16[512,1408]{1,0:T(8,128)(2,1)S(1)} %get-tuple-element.161, bf16[512,1408]{1,0:T(8,128)(2,1)S(1)} %get-tuple-element.160), kind=kOutput, calls=%fused_computation.48 | convolution fusion | flops 5912395776 | bytes 16515072 | tf_op jit(solution)/shard_map/dot_general | solution.py:260
  250.6 9.5 %collective-permute-done.24 = bf16[512,512]{1,0:T(8,128)(2,1)S(1)} collective-permute-done((bf16[512,512]{1,0:T(8,128)(2,1)S(1)}, bf16[512,512]{1,0:T(8,128)(2,1)S(1)}, u32[]{:S(2)}, u32[]{:S(2)}) %collective-permute-start.24) | collective-permute-done | bytes 524320 | tf_op jit(solution)/shard_map/ppermute | solution.py:272
  270.8 6.1 %fusion.58 = f32[1024,2816]{1,0:T(8,128)} fusion(bf16[512,1024]{1,0:T(8,128)(2,1)S(1)} %pad_maximum_fusion.8, bf16[512,1408]{1,0:T(8,128)(2,1)S(1)} %get-tuple-element.161, bf16[512,1408]{1,0:T(8,128)(2,1)S(1)} %get-tuple-element.160), kind=kOutput, calls=%fused_computation.351 | convolution fusion | flops 2958557184 | bytes 15466496 | tf_op jit(solution)/shard_map/dot_general | solution.py:264
  277.1 11.7 %collective-permute-start.25 = (bf16[512,512]{1,0:T(8,128)(2,1)S(1)}, bf16[512,512]{1,0:T(8,128)(2,1)S(1)}, u32[]{:S(2)}, u32[]{:S(2)}) collective-permute-start(bf16[512,512]{1,0:T(8,128)(2,1)S(1)} %get-tuple-element.147), channel_id=1, source_target_pairs={{8,16},{16,8},{9,17},{17,9},{10,18},{18,10},{11,19},{19,11},{12,20... | collective-permute-start | bytes 1572872 | tf_op jit(solution)/shard_map/ppermute | solution.py:272
  296.1 7.8 %collective-permute-done.27 = bf16[512,512]{1,0:T(8,128)(2,1)S(1)} collective-permute-done((bf16[512,512]{1,0:T(8,128)(2,1)S(1)}, bf16[512,512]{1,0:T(8,128)(2,1)S(1)}, u32[]{:S(2)}, u32[]{:S(2)}) %collective-permute-start.27) | collective-permute-done | bytes 524320 | tf_op jit(solution)/shard_map/ppermute | solution.py:272
  306.3 8.2 %collective-permute-done.26 = bf16[512,512]{1,0:T(8,128)(2,1)S(1)} collective-permute-done((bf16[512,512]{1,0:T(8,128)(2,1)S(1)}, bf16[512,512]{1,0:T(8,128)(2,1)S(1)}, u32[]{:S(2)}, u32[]{:S(2)}) %collective-permute-start.26) | collective-permute-done | bytes 524320 | tf_op jit(solution)/shard_map/ppermute | solution.py:272
  327.9 7.4 %fusion.21 = bf16[512,2048]{1,0:T(8,128)(2,1)} fusion(bf16[512,1408]{1,0:T(8,128)(2,1)S(1)} %copy-done.16, bf16[2048,1920]{0,1:T(8,128)(2,1)} %all-gather.6.cloned.1.call-done), kind=kOutput, calls=%fused_computation.50 | convolution fusion | flops 2953838592 | bytes 9306112 | tf_op jit(solution)/shard_map/dot_general | solution.py:260
  337.6 10.2 %add_convert_fusion = bf16[1024,2816]{1,0:T(8,128)(2,1)} fusion(f32[1024,2816]{1,0:T(8,128)} %fusion.58, bf16[1024,2816]{1,0:T(8,128)(2,1)} %collective-permute-done.35), kind=kLoop, calls=%fused_computation | loop fusion | flops 8650752 | bytes 23068672 | tf_op jit(solution)/shard_map/convert_element_type | solution.py:371
  350.5 8.5 %collective-permute-done.36 = bf16[512,512]{1,0:T(8,128)(2,1)S(1)} collective-permute-done((bf16[512,512]{1,0:T(8,128)(2,1)S(1)}, bf16[512,512]{1,0:T(8,128)(2,1)S(1)}, u32[]{:S(2)}, u32[]{:S(2)}) %collective-permute-start.36) | collective-permute-done | bytes 524320 | tf_op jit(solution)/shard_map/ppermute | solution.py:272
  377.4 6.9 %shard_map.273 = f32[2,2,2,8,512]{4,3,2,1,0:T(8,128)S(1)} custom-call(f32[2,256]{1,0:T(2,128)S(1)} %get-tuple-element.284.keep_ref, bf16[512,512]{1,0:T(8,128)(2,1)S(1)} %get-tuple-element.219.u_ref.g_ref, f32[4,2,8,512]{3,2,1,0:T(8,128)S(1)} %pad_maximum_fusion.17.par_ref), custom_call_target="tpu_custom_call" | custom-call | tf_op jit(solution)/shard_map/pallas_call | solution.py:209
  387.7 11.7 %collective-permute-done.37 = bf16[512,512]{1,0:T(8,128)(2,1)S(1)} collective-permute-done((bf16[512,512]{1,0:T(8,128)(2,1)S(1)}, bf16[512,512]{1,0:T(8,128)(2,1)S(1)}, u32[]{:S(2)}, u32[]{:S(2)}) %collective-permute-start.37) | collective-permute-done | bytes 524320 | tf_op jit(solution)/shard_map/ppermute | solution.py:272
  400.5 9.8 %collective-permute-done.40 = bf16[512,512]{1,0:T(8,128)(2,1)S(1)} collective-permute-done((bf16[512,512]{1,0:T(8,128)(2,1)S(1)}, bf16[512,512]{1,0:T(8,128)(2,1)S(1)}, u32[]{:S(2)}, u32[]{:S(2)}) %collective-permute-start.40) | collective-permute-done | bytes 524320 | tf_op jit(solution)/shard_map/ppermute | solution.py:272
  412.1 7.1 %collective-permute-start.39 = (bf16[512,512]{1,0:T(8,128)(2,1)S(1)}, bf16[512,512]{1,0:T(8,128)(2,1)S(1)}, u32[]{:S(2)}, u32[]{:S(2)}) collective-permute-start(bf16[512,512]{1,0:T(8,128)(2,1)S(1)} %get-tuple-element.192), channel_id=1, source_target_pairs={{0,8},{8,0},{16,24},{24,16},{1,9},{9,1},{17,25},{25,17},{2,10},{10... | collective-permute-start | bytes 1572872 | tf_op jit(solution)/shard_map/ppermute | solution.py:272
  419.4 24.1 %shard_map.274 = (bf16[512,512]{1,0:T(8,128)(2,1)S(1)}, f32[4,2,8,512]{3,2,1,0:T(8,128)S(1)}, f32[1,512]{1,0:T(1,128)S(1)}) custom-call(f32[2,256]{1,0:T(2,128)S(1)} %get-tuple-element.284.keep_ref, bf16[512,512]{1,0:T(8,128)(2,1)S(1)} %multiply_convert_fusion.4.u_ref, bf16[512,512]{1,0:T(8,128)(2,1)S(1)} %get-tuple-element.219.u_ref.g_ref, ...), custom_call_target="tpu_custom_call" | custom-call | tf_op jit(solution)/shard_map/pallas_call | solution.py:232
  470.6 11.6 %collective-permute-start.47 = (bf16[512,512]{1,0:T(8,128)(2,1)}, bf16[512,512]{1,0:T(8,128)(2,1)S(1)}, u32[]{:S(2)}, u32[]{:S(2)}) collective-permute-start(bf16[512,512]{1,0:T(8,128)(2,1)} %constant_dynamic-slice_fusion.16), channel_id=1, source_target_pairs={{0,8},{8,0},{16,24},{24,16},{1,9},{9,1},{17,25},{25,17},{2,10},{10... | collective-permute-start | bytes 1572872 | tf_op jit(solution)/shard_map/ppermute | solution.py:272
  486.2 8.7 %collective-permute-done.47 = bf16[512,512]{1,0:T(8,128)(2,1)S(1)} collective-permute-done((bf16[512,512]{1,0:T(8,128)(2,1)}, bf16[512,512]{1,0:T(8,128)(2,1)S(1)}, u32[]{:S(2)}, u32[]{:S(2)}) %collective-permute-start.47) | collective-permute-done | bytes 524320 | tf_op jit(solution)/shard_map/ppermute | solution.py:272
  500.3 8.6 %collective-permute-done.54 = f32[4,128]{1,0:T(4,128)S(1)} collective-permute-done((f32[4,128]{1,0:T(4,128)S(1)}, f32[4,128]{1,0:T(4,128)S(1)}, u32[]{:S(2)}, u32[]{:S(2)}) %collective-permute-start.54) | collective-permute-done | bytes 2080 | tf_op jit(solution)/shard_map/ppermute | solution.py:272
  531.9 7.9 %collective-permute-start.52 = (bf16[512,512]{1,0:T(8,128)(2,1)}, bf16[512,512]{1,0:T(8,128)(2,1)}, u32[]{:S(2)}, u32[]{:S(2)}) collective-permute-start(bf16[512,512]{1,0:T(8,128)(2,1)} %dynamic-slice_add_fusion), channel_id=1, source_target_pairs={{0,8},{8,0},{16,24},{24,16},{1,9},{9,1},{17,25},{25,17},{2,10},{10... | collective-permute-start | bytes 1572872 | tf_op jit(solution)/shard_map/ppermute | solution.py:272
  543.6 5.9 %collective-permute-done.52 = bf16[512,512]{1,0:T(8,128)(2,1)} collective-permute-done((bf16[512,512]{1,0:T(8,128)(2,1)}, bf16[512,512]{1,0:T(8,128)(2,1)}, u32[]{:S(2)}, u32[]{:S(2)}) %collective-permute-start.52) | collective-permute-done | bytes 524320 | tf_op jit(solution)/shard_map/ppermute | solution.py:272
  (487 shorter events, 253.9 us)
Async XLA Ops:
  7.2 52.7 %all-gather.4.cloned.1.call-start = ((), (), s32[]{:S(2)}) async-start(), calls=%async_computation.4 | async-start | bytes 7077888 | tf_op jit(solution)/shard_map/all_gather | solution.py:354
  9.7 111.4 %all-gather.6.cloned.1.call-start = ((), (), s32[]{:S(2)}) async-start(), calls=%async_computation.5 | async-start | bytes 8847360 | tf_op jit(solution)/shard_map/all_gather | solution.py:354
  11.9 214.2 %all-gather.8.cloned.1.call-start = ((), (), s32[]{:S(2)}) async-start(), calls=%async_computation.6 | async-start | bytes 12976128 | tf_op jit(solution)/shard_map/all_gather | solution.py:354
  13.2 500.8 %reduce-scatter.11.cloned.1.call-start = ((), (), s32[]{:S(2)}) async-start(), calls=%async_computation.10 | async-start | bytes 3604480 | tf_op jit(solution)/shard_map/reduce_scatter | solution.py:377
  29.0 19.3 %collective-permute-start.1 = (bf16[512,512]{1,0:T(8,128)(2,1)S(1)}, bf16[512,512]{1,0:T(8,128)(2,1)S(1)}, u32[]{:S(2)}, u32[]{:S(2)}) collective-permute-start(bf16[512,512]{1,0:T(8,128)(2,1)S(1)} %collective-permute-done), channel_id=1, source_target_pairs={{0,8},{8,0},{16,24},{24,16},{1,9},{9,1},{17,25},{25,17},{2,10},{10... | collective-permute-start | bytes 1572872 | tf_op jit(solution)/shard_map/ppermute | solution.py:272
  33.6 22.1 %collective-permute-start.4 = (bf16[512,512]{1,0:T(8,128)(2,1)S(1)}, bf16[512,512]{1,0:T(8,128)(2,1)S(1)}, u32[]{:S(2)}, u32[]{:S(2)}) collective-permute-start(bf16[512,512]{1,0:T(8,128)(2,1)S(1)} %collective-permute-done.3), channel_id=1, source_target_pairs={{0,8},{8,0},{16,24},{24,16},{1,9},{9,1},{17,25},{25,17},{2,10},{10... | collective-permute-start | bytes 1572872 | tf_op jit(solution)/shard_map/ppermute | solution.py:272
  85.9 16.7 %collective-permute-start.9 = (bf16[512,512]{1,0:T(8,128)(2,1)S(1)}, bf16[512,512]{1,0:T(8,128)(2,1)S(1)}, u32[]{:S(2)}, u32[]{:S(2)}) collective-permute-start(bf16[512,512]{1,0:T(8,128)(2,1)S(1)} %bitcast.356), channel_id=1, source_target_pairs={{0,8},{8,0},{16,24},{24,16},{1,9},{9,1},{17,25},{25,17},{2,10},{10... | collective-permute-start | bytes 1572872 | tf_op jit(solution)/shard_map/ppermute | solution.py:272
  100.3 18.6 %collective-permute-start.11 = (bf16[512,512]{1,0:T(8,128)(2,1)S(1)}, bf16[512,512]{1,0:T(8,128)(2,1)S(1)}, u32[]{:S(2)}, u32[]{:S(2)}) collective-permute-start(bf16[512,512]{1,0:T(8,128)(2,1)S(1)} %collective-permute-done.10), channel_id=1, source_target_pairs={{0,8},{8,0},{16,24},{24,16},{1,9},{9,1},{17,25},{25,17},{2,10},{10... | collective-permute-start | bytes 1572872 | tf_op jit(solution)/shard_map/ppermute | solution.py:272
  102.6 16.3 %collective-permute-start.12 = (bf16[512,512]{1,0:T(8,128)(2,1)S(1)}, bf16[512,512]{1,0:T(8,128)(2,1)}, u32[]{:S(2)}, u32[]{:S(2)}) collective-permute-start(bf16[512,512]{1,0:T(8,128)(2,1)S(1)} %collective-permute-done.9), channel_id=1, source_target_pairs={{8,16},{16,8},{9,17},{17,9},{10,18},{18,10},{11,19},{19,11},{12,20... | collective-permute-start | bytes 1572872 | tf_op jit(solution)/shard_map/ppermute | solution.py:272
  140.7 16.2 %collective-permute-start.16 = (bf16[512,512]{1,0:T(8,128)(2,1)S(1)}, bf16[512,512]{1,0:T(8,128)(2,1)}, u32[]{:S(2)}, u32[]{:S(2)}) collective-permute-start(bf16[512,512]{1,0:T(8,128)(2,1)S(1)} %get-tuple-element.156), channel_id=1, source_target_pairs={{0,8},{8,0},{16,24},{24,16},{1,9},{9,1},{17,25},{25,17},{2,10},{10... | collective-permute-start | bytes 1572872 | tf_op jit(solution)/shard_map/ppermute | solution.py:272
  145.8 24.2 %collective-permute-start.15 = (bf16[512,512]{1,0:T(8,128)(2,1)}, bf16[512,512]{1,0:T(8,128)(2,1)S(1)}, u32[]{:S(2)}, u32[]{:S(2)}) collective-permute-start(bf16[512,512]{1,0:T(8,128)(2,1)} %dynamic-slice_add_fusion.5), channel_id=1, source_target_pairs={{0,8},{8,0},{16,24},{24,16},{1,9},{9,1},{17,25},{25,17},{2,10},{10... | collective-permute-start | bytes 1572872 | tf_op jit(solution)/shard_map/ppermute | solution.py:272
  159.7 21.6 %collective-permute-start.23 = (bf16[512,512]{1,0:T(8,128)(2,1)}, bf16[512,512]{1,0:T(8,128)(2,1)}, u32[]{:S(2)}, u32[]{:S(2)}) collective-permute-start(bf16[512,512]{1,0:T(8,128)(2,1)} %collective-permute-done.12), channel_id=1, source_target_pairs={{0,8},{8,0},{16,24},{24,16},{1,9},{9,1},{17,25},{25,17},{2,10},{10... | collective-permute-start | bytes 1572872 | tf_op jit(solution)/shard_map/ppermute | solution.py:272
  172.5 16.9 %collective-permute-start.20 = (bf16[512,512]{1,0:T(8,128)(2,1)}, bf16[512,512]{1,0:T(8,128)(2,1)}, u32[]{:S(2)}, u32[]{:S(2)}) collective-permute-start(bf16[512,512]{1,0:T(8,128)(2,1)} %fusion.57), channel_id=1, source_target_pairs={{0,8},{8,0},{16,24},{24,16},{1,9},{9,1},{17,25},{25,17},{2,10},{10... | collective-permute-start | bytes 1572872 | tf_op jit(solution)/shard_map/ppermute | solution.py:272
  190.9 25.9 %collective-permute-start.19 = (bf16[512,512]{1,0:T(8,128)(2,1)S(1)}, bf16[512,512]{1,0:T(8,128)(2,1)S(1)}, u32[]{:S(2)}, u32[]{:S(2)}) collective-permute-start(bf16[512,512]{1,0:T(8,128)(2,1)S(1)} %collective-permute-done.18), channel_id=1, source_target_pairs={{0,8},{8,0},{16,24},{24,16},{1,9},{9,1},{17,25},{25,17},{2,10},{10... | collective-permute-start | bytes 1572872 | tf_op jit(solution)/shard_map/ppermute | solution.py:272
  199.9 18.4 %collective-permute-start.22 = (bf16[512,512]{1,0:T(8,128)(2,1)S(1)}, bf16[512,512]{1,0:T(8,128)(2,1)S(1)}, u32[]{:S(2)}, u32[]{:S(2)}) collective-permute-start(bf16[512,512]{1,0:T(8,128)(2,1)S(1)} %collective-permute-done.21), channel_id=1, source_target_pairs={{0,8},{8,0},{16,24},{24,16},{1,9},{9,1},{17,25},{25,17},{2,10},{10... | collective-permute-start | bytes 1572872 | tf_op jit(solution)/shard_map/ppermute | solution.py:272
  265.1 72.5 %collective-permute-start.35 = (bf16[1024,2816]{1,0:T(8,128)(2,1)}, bf16[1024,2816]{1,0:T(8,128)(2,1)}, u32[]{:S(2)}, u32[]{:S(2)}) collective-permute-start(bf16[1024,2816]{1,0:T(8,128)(2,1)} %convolution_convert_fusion), channel_id=1, source_target_pairs={{0,1},{1,0},{2,3},{3,2},{4,5},{5,4},{6,7},{7,6},{8,9},{9,8},{10,11... | collective-permute-start | bytes 17301512 | tf_op jit(solution)/shard_map/ppermute | solution.py:350
  268.2 55.9 %collective-permute-start.60 = (bf16[1024,1408]{1,0:T(8,128)(2,1)S(1)}, bf16[1024,1408]{1,0:T(8,128)(2,1)S(1)}, u32[]{:S(2)}, u32[]{:S(2)}) collective-permute-start(bf16[1024,1408]{1,0:T(8,128)(2,1)S(1)} %convolution_convert_fusion.1), channel_id=1, source_target_pairs={{0,1},{1,0},{2,3},{3,2},{4,5},{5,4},{6,7},{7,6},{8,9},{9,8},{10,11... | collective-permute-start | bytes 8650760 | tf_op jit(solution)/shard_map/ppermute | solution.py:350
  269.0 24.1 %collective-permute-start.29 = (f32[4,128]{1,0:T(4,128)S(1)}, f32[4,128]{1,0:T(4,128)S(1)}, u32[]{:S(2)}, u32[]{:S(2)}) collective-permute-start(f32[4,128]{1,0:T(4,128)S(1)} %bitcast.368), channel_id=1, source_target_pairs={{0,8},{8,0},{16,24},{24,16},{1,9},{9,1},{17,25},{25,17},{2,10},{10... | collective-permute-start | bytes 6152 | tf_op jit(solution)/shard_map/ppermute | solution.py:272
  277.1 16.7 %collective-permute-start.25 = (bf16[512,512]{1,0:T(8,128)(2,1)S(1)}, bf16[512,512]{1,0:T(8,128)(2,1)S(1)}, u32[]{:S(2)}, u32[]{:S(2)}) collective-permute-start(bf16[512,512]{1,0:T(8,128)(2,1)S(1)} %get-tuple-element.147), channel_id=1, source_target_pairs={{8,16},{16,8},{9,17},{17,9},{10,18},{18,10},{11,19},{19,11},{12,20... | collective-permute-start | bytes 1572872 | tf_op jit(solution)/shard_map/ppermute | solution.py:272
  288.8 15.2 %collective-permute-start.27 = (bf16[512,512]{1,0:T(8,128)(2,1)S(1)}, bf16[512,512]{1,0:T(8,128)(2,1)S(1)}, u32[]{:S(2)}, u32[]{:S(2)}) collective-permute-start(bf16[512,512]{1,0:T(8,128)(2,1)S(1)} %get-tuple-element.148), channel_id=1, source_target_pairs={{0,8},{8,0},{16,24},{24,16},{1,9},{9,1},{17,25},{25,17},{2,10},{10... | collective-permute-start | bytes 1572872 | tf_op jit(solution)/shard_map/ppermute | solution.py:272
  294.0 20.5 %collective-permute-start.26 = (bf16[512,512]{1,0:T(8,128)(2,1)S(1)}, bf16[512,512]{1,0:T(8,128)(2,1)S(1)}, u32[]{:S(2)}, u32[]{:S(2)}) collective-permute-start(bf16[512,512]{1,0:T(8,128)(2,1)S(1)} %dynamic-slice_add_fusion.4), channel_id=1, source_target_pairs={{0,8},{8,0},{16,24},{24,16},{1,9},{9,1},{17,25},{25,17},{2,10},{10... | collective-permute-start | bytes 1572872 | tf_op jit(solution)/shard_map/ppermute | solution.py:272
  317.2 19.7 %collective-permute-start.33 = (bf16[512,512]{1,0:T(8,128)(2,1)S(1)}, bf16[512,512]{1,0:T(8,128)(2,1)}, u32[]{:S(2)}, u32[]{:S(2)}) collective-permute-start(bf16[512,512]{1,0:T(8,128)(2,1)S(1)} %get-tuple-element.145), channel_id=1, source_target_pairs={{0,8},{8,0},{16,24},{24,16},{1,9},{9,1},{17,25},{25,17},{2,10},{10... | collective-permute-start | bytes 1572872 | tf_op jit(solution)/shard_map/ppermute | solution.py:272
  326.5 215.0 %reduce-scatter.7.cloned.1.call-start = ((), (), s32[]{:S(2)}) async-start(), calls=%async_computation.8 | async-start | bytes 1310720 | tf_op jit(solution)/shard_map/reduce_scatter | solution.py:377
  372.9 180.6 %reduce-scatter.9.cloned.1.call-start = ((), (), s32[]{:S(2)}) async-start(), calls=%async_computation.9 | async-start | bytes 7208960 | tf_op jit(solution)/shard_map/reduce_scatter | solution.py:377
  373.5 183.1 %reduce-scatter.5.cloned.1.call-start = ((), (), s32[]{:S(2)}) async-start(), calls=%async_computation.7 | async-start | bytes 3932160 | tf_op jit(solution)/shard_map/reduce_scatter | solution.py:377
  386.5 23.7 %collective-permute-start.40 = (bf16[512,512]{1,0:T(8,128)(2,1)S(1)}, bf16[512,512]{1,0:T(8,128)(2,1)S(1)}, u32[]{:S(2)}, u32[]{:S(2)}) collective-permute-start(bf16[512,512]{1,0:T(8,128)(2,1)S(1)} %get-tuple-element.195), channel_id=1, source_target_pairs={{0,8},{8,0},{16,24},{24,16},{1,9},{9,1},{17,25},{25,17},{2,10},{10... | collective-permute-start | bytes 1572872 | tf_op jit(solution)/shard_map/ppermute | solution.py:272
  400.4 18.9 %collective-permute-start.44 = (f32[2,2,2,8,512]{4,3,2,1,0:T(8,128)S(1)}, f32[2,2,2,8,512]{4,3,2,1,0:T(8,128)S(1)}, u32[]{:S(2)}, u32[]{:S(2)}) collective-permute-start(f32[2,2,2,8,512]{4,3,2,1,0:T(8,128)S(1)} %maximum_add_fusion.5), channel_id=1, source_target_pairs={{0,4},{1,5},{2,6},{3,7},{4,0},{5,1},{6,2},{7,3},{8,12},{9,13},{10,... | collective-permute-start | bytes 393224 | tf_op jit(solution)/shard_map/ppermute | solution.py:350
  412.1 31.5 %collective-permute-start.39 = (bf16[512,512]{1,0:T(8,128)(2,1)S(1)}, bf16[512,512]{1,0:T(8,128)(2,1)S(1)}, u32[]{:S(2)}, u32[]{:S(2)}) collective-permute-start(bf16[512,512]{1,0:T(8,128)(2,1)S(1)} %get-tuple-element.192), channel_id=1, source_target_pairs={{0,8},{8,0},{16,24},{24,16},{1,9},{9,1},{17,25},{25,17},{2,10},{10... | collective-permute-start | bytes 1572872 | tf_op jit(solution)/shard_map/ppermute | solution.py:272
  470.6 24.2 %collective-permute-start.47 = (bf16[512,512]{1,0:T(8,128)(2,1)}, bf16[512,512]{1,0:T(8,128)(2,1)S(1)}, u32[]{:S(2)}, u32[]{:S(2)}) collective-permute-start(bf16[512,512]{1,0:T(8,128)(2,1)} %constant_dynamic-slice_fusion.16), channel_id=1, source_target_pairs={{0,8},{8,0},{16,24},{24,16},{1,9},{9,1},{17,25},{25,17},{2,10},{10... | collective-permute-start | bytes 1572872 | tf_op jit(solution)/shard_map/ppermute | solution.py:272
  509.1 20.6 %collective-permute-start.48 = (bf16[512,512]{1,0:T(8,128)(2,1)S(1)}, bf16[512,512]{1,0:T(8,128)(2,1)}, u32[]{:S(2)}, u32[]{:S(2)}) collective-permute-start(bf16[512,512]{1,0:T(8,128)(2,1)S(1)} %get-tuple-element.140), channel_id=1, source_target_pairs={{8,16},{16,8},{9,17},{17,9},{10,18},{18,10},{11,19},{19,11},{12,20... | collective-permute-start | bytes 1572872 | tf_op jit(solution)/shard_map/ppermute | solution.py:272
  512.6 17.1 %collective-permute-start.50 = (bf16[512,512]{1,0:T(8,128)(2,1)}, bf16[512,512]{1,0:T(8,128)(2,1)}, u32[]{:S(2)}, u32[]{:S(2)}) collective-permute-start(bf16[512,512]{1,0:T(8,128)(2,1)} %fusion.96), channel_id=1, source_target_pairs={{8,16},{16,8},{9,17},{17,9},{10,18},{18,10},{11,19},{19,11},{12,20... | collective-permute-start | bytes 1572872 | tf_op jit(solution)/shard_map/ppermute | solution.py:272
  531.9 17.6 %collective-permute-start.52 = (bf16[512,512]{1,0:T(8,128)(2,1)}, bf16[512,512]{1,0:T(8,128)(2,1)}, u32[]{:S(2)}, u32[]{:S(2)}) collective-permute-start(bf16[512,512]{1,0:T(8,128)(2,1)} %dynamic-slice_add_fusion), channel_id=1, source_target_pairs={{0,8},{8,0},{16,24},{24,16},{1,9},{9,1},{17,25},{25,17},{2,10},{10... | collective-permute-start | bytes 1572872 | tf_op jit(solution)/shard_map/ppermute | solution.py:272
  (128 other events, 1531.0 us)
Sparse Core Ops, SparseCore 0:
  10.5 49.3 all-gather.3
  62.4 56.4 all-gather.5
  121.3 67.6 all-gather.7
  326.7 39.8 reduce-scatter.10
  373.0 25.5 reduce-scatter.6
  401.8 65.9 reduce-scatter.8
  471.0 52.6 reduce-scatter.4

commit v4 on v3

--- a/solution.py
+++ b/solution.py
@@ -5,6 +5,7 @@
 from jax import lax
 from jax.experimental import pallas as pl
 from jax.experimental.pallas import tpu as pltpu
+from jax.experimental.layout import Layout, with_layout_constraint
 from jax.sharding import PartitionSpec as P
 
 norm_eps = 1e-05
@@ -14,7 +15,7 @@
 
 
 lane_block = 128
-step = 8
+step = 16
 
 
 def times(a_re, a_im, b_re, b_im):
@@ -368,16 +369,16 @@
 
 def core_sum(left, right, got):
     own = dot_tokens(of_core(left, lax.axis_index("seq") % 2), right)
-    return lax.optimization_barrier((own + got.astype(f32)).astype(bf16))
+    return with_layout_constraint((own + got.astype(f32)).astype(bf16), Layout(major_to_minor=(0, 1)))
 
 
 def chip_sums_offloaded(summed):
     count = lax.axis_size("seq")
     groups = [list(range(core, count, 2)) for core in range(2)]
-    return lax.psum_scatter(summed, "seq", scatter_dimension=0, axis_index_groups=groups, tiled=True).astype(f32)
-
-
-def chip_sums(summed):
+    return lax.psum_scatter(summed, "seq", scatter_dimension=0, axis_index_groups=groups, tiled=True)
+
+
+def chip_sums(summed, *before_last):
     count = lax.axis_size("seq")
     rank = lax.axis_index("seq")
     rows, bits = 2 * summed.shape[0] // count, count.bit_length() - 1
@@ -396,10 +397,11 @@
     for half, order in enumerate((chip_bits, chip_bits[middle:] + chip_bits[:middle])):
         part = lax.slice_in_dim(by_bits, half * rows // 2, (half + 1) * rows // 2, axis=bits - 1)
         rest = chip_bits[::-1]
-        for bit in order:
+        for bit in order[:-1]:
             part, rest = halve(part, rest, bit)
-        parts.append(part)
-    return lax.optimization_barrier(jnp.concatenate(parts, axis=0))
+        part, rest = halve(after(part.astype(bf16), *before_last), rest, order[-1])
+        parts.append(with_layout_constraint(part, Layout(major_to_minor=(0, 1))))
+    return parts
 
 
 def passing_factors(whole, power, reverse):
@@ -479,9 +481,10 @@
 
     x_share = hidden_in.reshape(tokens, share)
     cot_share = out_cot.reshape(tokens, share)
-    x_all = gather_share(x_share).astype(f32)
+    x_rows = gather_share(x_share)
+    x_all = x_rows.astype(f32)
     units = gate_proj.shape[1]
-    w_in = gather_weight(in_proj.reshape(d_rows, 3 * share))
+    w_in = gather_weight(jnp.concatenate([in_proj[:, j] for j in range(3)], axis=1))
     w_both = gather_weight(jnp.concatenate([out_proj.T, down_proj.T], axis=1))
     w_out, w_down = w_both[:, :share], w_both[:, share:]
     w_feed = gather_weight(jnp.concatenate([gate_proj, up_proj], axis=1))
@@ -505,16 +508,17 @@
     fading = jnp.exp(-rates)
     modes = jnp.stack([fading * jnp.cos(angles), fading * jnp.sin(angles), res_re, res_im])
     skips = skip_gain[None]
+    masked_taps = lax.optimization_barrier([taps[lag] * masks[lag] for lag in range(3)])
     factors = passing_factors(whole, power, False)
     back_factors = passing_factors(whole, power, True)
 
     scale_one = lax.rsqrt(jnp.mean(x_all * x_all, axis=-1, keepdims=True) + norm_eps)
     unit_one = x_all * scale_one
-    normed_one = after((unit_one * mixer_gain).astype(bf16), modes, factors, back_factors)
+    normed_one = after((unit_one * mixer_gain).astype(bf16), modes, masked_taps, factors, back_factors)
     project = dot(normed_one, w_in).reshape(batches, rows, 3 * share)
     extended = jnp.concatenate([shifted(project[:, -2:], "seq", 1), project], axis=1)
     lagged = [extended[:, 2 - lag : 2 - lag + rows] for lag in range(3)]
-    conv = sum(taps[lag] * masks[lag] * lagged[lag] for lag in range(3)).reshape(tokens, 3 * share)
+    conv = sum(masked_taps[lag] * lagged[lag] for lag in range(3)).reshape(tokens, 3 * share)
     gate_one, gate_two, values = (conv[:, j * share : (j + 1) * share] for j in range(3))
     product = (gate_two * values).astype(bf16)
     cot_late = after(cot_share, product)
@@ -545,34 +549,30 @@
     d_gate = d_hidden * up_pre * sigmoid * (1.0 + gate_pre * (1.0 - sigmoid))
     d_up = d_hidden * activated
     d_feed = jnp.concatenate([d_gate.astype(bf16), d_up.astype(bf16)], axis=1)
+    along_two = jnp.sum(d_gate * gate_pre + d_up * up_pre, axis=-1)
+    along_two = sum_line(along_two.reshape(-1, 128))
     part_two = dot_rows(d_feed, w_feed).astype(bf16)
-    two_first = scatter_first(part_two)
-    along_two = jnp.sum(after(d_feed, part_two).astype(f32) * feed_pre, axis=-1)
-    along_two = sum_line(along_two.reshape(-1, 128)).reshape(tokens, 1)
-    feed_gain_part = jnp.sum(unit_two * after(part_two, two_first[0]).astype(f32), axis=0)
+    along_two = along_two.reshape(tokens, 1)
+    dn_two = lax.psum_scatter(part_two, "fsdp", scatter_dimension=1, tiled=True)
+    feed_got = swap_seq(core_give(normed_two, after(d_feed, part_two)), 0)
     down_got = swap_seq(core_give(cot_all, after(hidden, part_two)), 0)
-    two_second = scatter_second(part_two, two_first)
-    feed_got = swap_seq(core_give(normed_two, after(d_feed, two_first[0])), 0)
-    two_last = scatter_last(part_two, two_second)
-    down_sum = core_sum(cot_all, hidden, after(down_got, two_second[0]))
+    feed_sum = core_sum(normed_two, d_feed, feed_got)
+    down_sum = core_sum(cot_all, hidden, down_got)
 
     def own_features(part):
         return lax.dynamic_slice_in_dim(part, fsdp_rank * share, share, 0)
 
     d_stream = (
         cot_share.astype(f32)
-        + scale_two * own_features(feed_gain) * scattered(part_two, two_second, two_last)
+        + scale_two * own_features(feed_gain) * dn_two.astype(f32)
         - stream * (scale_two * scale_two * along_two / width)
     )
     d_share = d_stream.astype(bf16)
-    mix_one = gather_first(d_share)
-    mix_two = gather_second(mix_one)
-    down_grad = chip_sums_offloaded(down_sum)
+    d_mix = lax.all_gather(d_share, "fsdp", axis=1, tiled=True)
     down_part = dot_rows(after(hidden, d_share), w_down).astype(bf16)
-    feed_sum = core_sum(normed_two, d_feed, after(feed_got, mix_one[0]))
-    feed_grad = chip_sums_offloaded(feed_sum)
-    mix_three = gather_last(after(mix_two, feed_sum, down_part, feed_gain_part))
-    d_mix = gathered(d_share, mix_one, mix_two, mix_three)
+    feed_sums = lax.optimization_barrier(jnp.concatenate([feed_sum, down_sum], axis=1))
+    d_mix = after(d_mix, feed_sums, down_part)
+    feed_own = chip_sums_offloaded(after(feed_sums, d_mix))
 
     d_gated = lax.optimization_barrier(dot(d_mix, w_out))
     down_first = scatter_first(after(down_part, d_gated))
@@ -580,46 +580,57 @@
     d_mixed = (d_gated * gate_one).astype(bf16)
     behind = through(edge_states(d_mixed, keep_here, modes, True), back_factors, True)
     down_second = scatter_second(down_part, down_first)
-    out_sum = core_sum(d_mix, gated, swap_seq(core_give(d_mix, after(gated, d_mixed)), 0))
+    d_mix_late = after(d_mix, d_mixed)
+    out_sum = core_sum(d_mix_late, gated, swap_seq(core_give(d_mix_late, gated), 0))
     down_last = scatter_last(down_part, down_second)
-    out_grad = chip_sums_offloaded(out_sum)
+    feed_gain_part = jnp.sum(unit_two * after(part_two, d_mixed).astype(f32), axis=0)
     d_product, mode_sums, skip_sums = long_conv_back(
-        keep_here, product, d_mixed, into, after(behind, *down_second), modes, skips
-    )
-    d_product = after(d_product, out_sum, down_last)
+        keep_here, product, d_mixed, into, after(behind, *down_first), modes, skips
+    )
+    d_product = after(d_product, out_sum, feed_gain_part, *down_second)
     block_out = stream + scattered(down_part, down_second, down_last)
     d_product = d_product.astype(f32)
     d_conv = jnp.concatenate([d_gate_one, d_product * values, d_product * gate_two], axis=1)
     d_conv = d_conv.reshape(batches, rows, 3 * share)
-    short_part = jnp.stack([jnp.sum(masks[lag] * lagged[lag] * d_conv, axis=(0, 1)) for lag in range(3)])
     spread = sum(
         jnp.pad(taps[lag] * masks[lag] * d_conv, ((0, 0), (2 - lag, lag), (0, 0))) for lag in range(3)
     )
     returned = shifted(spread[:, :2], "seq", -1)
     d_project = spread[:, 2:] + jnp.pad(returned, ((0, 0), (rows - 2, 0), (0, 0)))
     d_project = d_project.astype(bf16).reshape(tokens, 3 * share)
-    along_one = jnp.sum(d_project.astype(f32) * project.reshape(tokens, 3 * share), axis=-1)
-    along_one = sum_line(along_one.reshape(-1, 128)).reshape(tokens, 1)
     part_one = dot_rows(d_project, w_in).astype(bf16)
-    mixer_gain_part = jnp.sum(unit_one * part_one.astype(f32), axis=0)
-    one_first = scatter_first(part_one)
-    in_got = swap_seq(core_give(normed_one, after(d_project, part_one)), 0)
-    one_second = scatter_second(part_one, one_first)
-    in_sum = core_sum(normed_one, d_project, in_got)
-    one_last = scatter_last(part_one, after(one_second, in_sum))
+    dn_one = lax.psum_scatter(after(part_one, feed_own), "fsdp", scatter_dimension=1, tiled=True)
+    in_give = core_give(normed_one, after(d_project, part_one, feed_own))
+    in_got = swap_seq(in_give, 0)
+    d_conv, late_project, late_part = lax.optimization_barrier((d_conv, d_project, part_one, in_give))[:3]
+    short_part = jnp.stack([jnp.sum(masks[lag] * lagged[lag] * d_conv, axis=(0, 1)) for lag in range(3)])
+    mixer_gain_part = jnp.sum(unit_one * late_part.astype(f32), axis=0)
+    in_sum = core_sum(normed_one, d_project, after(in_got, mixer_gain_part))
+    small = after((mixer_gain_part, feed_gain_part, short_part, mode_sums, skip_sums), in_sum)
+    small = jnp.concatenate([part.reshape(-1, share) for part in small])
+    for bit in range(1, seq_count.bit_length() - 1):
+        small = small + swap_seq(small, bit)
+    in_out = jnp.concatenate([in_sum, out_sum], axis=1)
+    feed_own = after(feed_own, in_sum)
+    gate_grad, up_grad, down_grad = (
+        feed_own[:, i * units : (i + 1) * units].astype(f32) for i in range(3)
+    )
+    in_out = chip_sums(after(in_out, small), dn_one)
+    small = small + swap_seq(small, 0)
+    gain_rows = 2 * width // share
+    along_one = jnp.sum(late_project.astype(f32) * project.reshape(tokens, 3 * share), axis=-1)
+    lined = sum_line(jnp.concatenate([small[:gain_rows], along_one.reshape(-1, share)]))
+    gains, along_one = lined[:gain_rows].reshape(2, width), lined[gain_rows:].reshape(tokens, 1)
     d_x = (
         d_stream
-        + scale_one * own_features(mixer_gain) * scattered(part_one, one_second, one_last)
+        + scale_one * own_features(mixer_gain) * dn_one.astype(f32)
         - x_share.astype(f32) * (scale_one * scale_one * along_one / width)
     )
 
-    in_grad = chip_sums_offloaded(in_sum).reshape(d_rows, 3, share)
-    small = [mixer_gain_part, feed_gain_part, short_part, mode_sums, skip_sums]
-    small = sum_seq(jnp.concatenate([part.reshape(-1, 128) for part in small]))
-    gains = sum_line(small[: 2 * width // 128]).reshape(2, width)
-    small = small[2 * width // 128 :].reshape(-1, share)
-    short_grad = small[:9].reshape(3, 3, share)
-    filters = small[9:]
+    branches = [jnp.concatenate([half[:, j * share : (j + 1) * share] for half in in_out]) for j in range(4)]
+    in_grad, out_grad = jnp.stack(branches[:3]).transpose(1, 0, 2), branches[3]
+    short_grad = small[gain_rows : gain_rows + 9].reshape(3, 3, share)
+    filters = small[gain_rows + 9 :]
     by_chan = filters[:-1].reshape(4, 2 * half_modes, share).transpose(0, 2, 1)
     return (
         block_out.astype(bf16).reshape(hidden_in.shape),
@@ -634,8 +645,8 @@
         filters[-1],
         out_grad.T,
         gains[1],
-        feed_grad[:, :units],
-        feed_grad[:, units:],
+        gate_grad,
+        up_grad,
         down_grad.T,
     )
 

time: 577 us -> 541 us (0.938)
  starting transfers between devices: 158 us -> 91.4 us
  waiting for transfers between devices: 141 us -> 178 us
  local copies, waits for them, and re-layouts: 42.9 us -> 30.1 us
  matrix products: 74.4 us -> 80.7 us
    ppermute x46 -> x29, starting transfers between devices: 147 us -> 69.1 us  [along_line(): return lax.ppermute(array, 'fsdp', pairs)]
    ppermute x46 -> x29, waiting for transfers between devices: 121 us -> 76.8 us  [along_line(): return lax.ppermute(array, 'fsdp', pairs)]
    reduce_scatter x0 -> x2, waiting for transfers between devices: none -> 24.8 us  [the longest x1 20.1 us: on_device(): dn_two = lax.psum_scatter(part_two, 'fsdp', scatter_dimension=1, tiled=True)]
    all_gather x0 -> x1, waiting for transfers between devices: none -> 24.6 us  [on_device(): d_mix = lax.all_gather(d_share, 'fsdp', axis=1, tiled=True)]
    reduce_scatter x4 -> x1, waiting for transfers between devices: 0.01 us -> 16 us  [chip_sums_offloaded(): lax.psum_scatter(summed, 'seq', scatter_dimension=0, axis_index_groups=gr...]
    ppermute x13 -> x17, waiting for transfers between devices: 19.4 us -> 34.6 us  [swap_seq(): lax.ppermute(array, 'seq', [(i, i ^ 1 << bit) for i in range(lax.axis_siz...]
    ppermute x13 -> x17, starting transfers between devices: 6.48 us -> 18.9 us  [swap_seq(): lax.ppermute(array, 'seq', [(i, i ^ 1 << bit) for i in range(lax.axis_siz...]
    dot_general x8, matrix products: 22.6 us -> 32.9 us  [dot_tokens(): lax.dot_general(left, right, (((0,), (0,)), ((), ())), preferred_element_...]
  transfers between devices with their start and end apart: 68 -> 55, of which waited for: 25 -> 27; matrix products, arithmetic and copies ran while one was open for 28% -> 29% of each run, Pallas kernels for 9% -> 9%
where the time goes in v4:
time: 541 us; the launch traced here: 532 us
  waiting for transfers between devices  178 us (33%)
  starting transfers between devices  91.4 us (17%)
  other arithmetic  89.4 us (17%)
  matrix products  80.7 us (15%)
  Pallas kernels  45.6 us (8%)
  local copies, waits for them, and re-layouts  30.1 us (6%)
  between operations  16.6 us (3%)
    ppermute x29, waiting for transfers between devices, along_line(): return lax.ppermute(array, 'fsdp', pairs)  76.8 us
    ppermute x29, starting transfers between devices, along_line(): return lax.ppermute(array, 'fsdp', pairs)  69.1 us
    ppermute x17, waiting for transfers between devices, swap_seq(): lax.ppermute(array, 'seq', [(i, i ^ 1 << bit) for i in range(lax.axis_siz...  34.6 us
    dot_general x8, matrix products, dot_tokens(): lax.dot_general(left, right, (((0,), (0,)), ((), ())), preferred_element_...  32.9 us
    dot_general x4, matrix products, dot(): return jnp.dot(left, right, preferred_element_type=f32)  27.9 us
    all_gather x1, waiting for transfers between devices, on_device(): d_mix = lax.all_gather(d_share, 'fsdp', axis=1, tiled=True)  24.6 us
    pallas_call x1, Pallas kernels, long_conv_back(): pl.pallas_call(functools.partial(back_kernel, batches), out_shape=(jax.Sh...  22.7 us
    reduce_scatter x1, waiting for transfers between devices, on_device(): dn_two = lax.psum_scatter(part_two, 'fsdp', scatter_dimension=1, tiled=True)  20.1 us
  transfers between devices with their start and end apart: 55, of which 27 were waited for; matrix products, arithmetic and copies ran while one was open for 29% of the time, Pallas kernels for 9%

profile of v4, /device:TPU:0, one launch (start us, length us, event | category | flops | bytes accessed | tf_op | source)
XLA Modules:
  0.0 532.2 jit_solution(5041540808703019368)
XLA Ops:
  32.6 4.9 collective-permute-start.1
  37.5 9.5 %collective-permute-start.4 = (bf16[512,512]{1,0:T(8,128)(2,1)S(1)}, bf16[512,512]{1,0:T(8,128)(2,1)S(1)}, u32[]{:S(2)}, u32[]{:S(2)}) collective-permute-start(bf16[512,512]{1,0:T(8,128)(2,1)S(1)} %collective-permute-done.3), channel_id=1, source_target_pairs={{0,8},{8,0},{16,24},{24,16},{1,9},{9,1},{17,25},{25,17},{2,10},{10... | collective-permute-start | bytes 1572872 | tf_op jit(solution)/shard_map/ppermute | solution.py:273
  50.6 9.8 %collective-permute-done.4 = bf16[512,512]{1,0:T(8,128)(2,1)S(1)} collective-permute-done((bf16[512,512]{1,0:T(8,128)(2,1)S(1)}, bf16[512,512]{1,0:T(8,128)(2,1)S(1)}, u32[]{:S(2)}, u32[]{:S(2)}) %collective-permute-start.4) | collective-permute-done | bytes 524320 | tf_op jit(solution)/shard_map/ppermute | solution.py:273
  66.7 6.9 %fusion.67 = f32[512,1536]{1,0:T(8,128)S(1)} fusion(bf16[512,2048]{1,0:T(8,128)(2,1)} %fusion.10, bf16[2048,1536]{1,0:T(8,128)(2,1)} %all-gather.5.cloned.1.call-done), kind=kOutput, calls=%fused_computation.365 | convolution fusion | flops 3221225472 | bytes 11534336 | tf_op jit(solution)/shard_map/dot_general | solution.py:269
  79.2 6.4 %shard_map.271 = f32[2,2,2,8,512]{4,3,2,1,0:T(8,128)S(1)} custom-call(f32[2,256]{1,0:T(2,128)S(1)} %get-tuple-element.299.keep_ref, bf16[512,512]{1,0:T(8,128)(2,1)S(1)} %multiply_convert_fusion.3.u_ref, f32[4,2,8,512]{3,2,1,0:T(8,128)S(1)} %pad_maximum_fusion.19.par_ref), custom_call_target="tpu_custom_call" | custom-call | tf_op jit(solution)/shard_map/pallas_call | solution.py:210
  93.6 6.9 %collective-permute-done.7 = f32[2,2,2,8,512]{4,3,2,0,1:T(8,128)S(1)} collective-permute-done((f32[2,2,2,8,512]{4,3,2,0,1:T(8,128)S(1)}, f32[2,2,2,8,512]{4,3,2,0,1:T(8,128)S(1)}, u32[]{:S(2)}, u32[]{:S(2)}) %collective-permute-start.7) | collective-permute-done | bytes 131104 | tf_op jit(solution)/shard_map/ppermute | solution.py:351
  110.3 10.2 %shard_map.272 = bf16[512,512]{1,0:T(8,128)(2,1)S(1)} custom-call(f32[2,256]{1,0:T(2,128)S(1)} %get-tuple-element.299.keep_ref, bf16[512,512]{1,0:T(8,128)(2,1)S(1)} %multiply_convert_fusion.3.u_ref, f32[2,2,2,8,512]{4,3,2,1,0:T(8,128)S(1)} %copy.52.into_ref, f32[4,2,8,512]{3,2,1,0:T(8,128)S(1)} %pad_maximum_fusion.19.par_ref, f32[1,512]{1,0:T(1,128)S(1)} %bitcast.357), custom_call_target="tpu_custom_call" | custom-call | tf_op jit(solution)/shard_map/pallas_call | solution.py:221
  130.6 11.1 %collective-permute-done.13 = bf16[512,512]{1,0:T(8,128)(2,1)} collective-permute-done((bf16[512,512]{1,0:T(8,128)(2,1)S(1)}, bf16[512,512]{1,0:T(8,128)(2,1)}, u32[]{:S(2)}, u32[]{:S(2)}) %collective-permute-start.13) | collective-permute-done | bytes 524320 | tf_op jit(solution)/shard_map/ppermute | solution.py:273
  146.3 9.0 %collective-permute-done.16 = bf16[512,512]{1,0:T(8,128)(2,1)} collective-permute-done((bf16[512,512]{1,0:T(8,128)(2,1)S(1)}, bf16[512,512]{1,0:T(8,128)(2,1)}, u32[]{:S(2)}, u32[]{:S(2)}) %collective-permute-start.16) | collective-permute-done | bytes 524320 | tf_op jit(solution)/shard_map/ppermute | solution.py:273
  162.4 12.9 %collective-permute-done.15 = bf16[512,512]{1,0:T(8,128)(2,1)} collective-permute-done((bf16[512,512]{1,0:T(8,128)(2,1)S(1)}, bf16[512,512]{1,0:T(8,128)(2,1)}, u32[]{:S(2)}, u32[]{:S(2)}) %collective-permute-start.15) | collective-permute-done | bytes 524320 | tf_op jit(solution)/shard_map/ppermute | solution.py:273
  180.1 6.4 %collective-permute-done.23 = bf16[512,512]{1,0:T(8,128)(2,1)} collective-permute-done((bf16[512,512]{1,0:T(8,128)(2,1)}, bf16[512,512]{1,0:T(8,128)(2,1)}, u32[]{:S(2)}, u32[]{:S(2)}) %collective-permute-start.23) | collective-permute-done | bytes 524320 | tf_op jit(solution)/shard_map/ppermute | solution.py:273
  189.0 5.0 collective-permute-done.20
  195.2 11.5 %collective-permute-start.19 = (bf16[512,512]{1,0:T(8,128)(2,1)S(1)}, bf16[512,512]{1,0:T(8,128)(2,1)S(1)}, u32[]{:S(2)}, u32[]{:S(2)}) collective-permute-start(bf16[512,512]{1,0:T(8,128)(2,1)S(1)} %collective-permute-done.18), channel_id=1, source_target_pairs={{0,8},{8,0},{16,24},{24,16},{1,9},{9,1},{17,25},{25,17},{2,10},{10... | collective-permute-start | bytes 1572872 | tf_op jit(solution)/shard_map/ppermute | solution.py:273
  206.7 5.9 %collective-permute-start.22 = (bf16[512,512]{1,0:T(8,128)(2,1)S(1)}, bf16[512,512]{1,0:T(8,128)(2,1)S(1)}, u32[]{:S(2)}, u32[]{:S(2)}) collective-permute-start(bf16[512,512]{1,0:T(8,128)(2,1)S(1)} %collective-permute-done.21), channel_id=1, source_target_pairs={{0,8},{8,0},{16,24},{24,16},{1,9},{9,1},{17,25},{25,17},{2,10},{10... | collective-permute-start | bytes 1572872 | tf_op jit(solution)/shard_map/ppermute | solution.py:273
  212.6 7.7 %fusion.2 = f32[512,1408]{1,0:T(8,128)} fusion(bf16[512,2048]{1,0:T(8,128)(2,1)S(1)} %pad_maximum_fusion.7, bf16[2048,1920]{0,1:T(8,128)(2,1)} %all-gather.7.cloned.1.call-done), kind=kOutput, calls=%fused_computation.11 | convolution fusion | flops 2952790016 | bytes 10747904 | tf_op jit(solution)/shard_map/dot_general | solution.py:269
  220.3 4.8 collective-permute-done.22
  230.9 10.3 %fusion.68 = f32[512,2816]{1,0:T(8,128)S(1)} fusion(bf16[512,2048]{1,0:T(8,128)(2,1)} %copy-done.15, bf16[2048,2816]{1,0:T(8,128)(2,1)} %all-gather.9.cloned.1.call-done), kind=kOutput, calls=%fused_computation.366 | convolution fusion | flops 5905580032 | bytes 19398656 | tf_op jit(solution)/shard_map/dot_general | solution.py:269
  247.6 7.4 %convolution_convert_fusion.4 = bf16[512,2048]{1,0:T(8,128)(2,1)} fusion(bf16[2048,2816]{1,0:T(8,128)(2,1)S(1)} %copy-done.85, bf16[512,1408]{1,0:T(8,128)(2,1)S(1)} %get-tuple-element.167, bf16[512,1408]{1,0:T(8,128)(2,1)S(1)} %get-tuple-element.165), kind=kOutput, calls=%fused_computation.40 | convolution fusion | flops 5912395776 | bytes 16515072 | tf_op jit(solution)/shard_map/dot_general | solution.py:261
  255.2 7.9 %convolution_convert_fusion = bf16[1024,2816]{1,0:T(8,128)(2,1)} fusion(bf16[512,1024]{1,0:T(8,128)(2,1)} %pad_maximum_fusion.10, bf16[512,2816]{1,0:T(8,128)(2,1)} %pad_maximum_fusion.4), kind=kOutput, calls=%fused_computation.4 | convolution fusion | flops 2955673600 | bytes 9699328 | tf_op jit(solution)/shard_map/dot_general | solution.py:265
  277.6 20.1 %reduce-scatter.4.cloned.1.call-done = bf16[512,512]{1,0:T(8,128)(2,1)} async-done(((bf16[512,2048]{1,0:T(8,128)(2,1)}), bf16[512,512]{1,0:T(8,128)(2,1)}) %reduce-scatter.4.cloned.1.call-update) | async-done | bytes 524304 | tf_op jit(solution)/shard_map/reduce_scatter | solution.py:556
  312.0 5.3 %add_convert_fusion = bf16[1024,2816]{1,0:T(8,128)(2,1)S(1)} fusion(bf16[1024,2816]{1,0:T(8,128)(2,1)} %collective-permute-done.26, bf16[512,1024]{1,0:T(8,128)(2,1)S(1)} %pad_maximum_fusion.9, bf16[512,1408]{1,0:T(8,128)(2,1)S(1)} %copy-done.24, bf16[512,1408]{1,0:T(8,128)(2,1)S(1)} %copy-done.22), kind=kOutput, calls=%fused_computation | convolution fusion | flops 2967207936 | bytes 15466496 | tf_op jit(solution)/shard_map/dot_general | solution.py:265
  321.1 24.6 %all-gather.11.cloned.1.call-done = bf16[512,2048]{1,0:T(8,128)(2,1)} async-done(((bf16[512,512]{1,0:T(8,128)(2,1)}), bf16[512,2048]{1,0:T(8,128)(2,1)}) %all-gather.11.cloned.1.call-update) | async-done | bytes 2097168 | tf_op jit(solution)/shard_map/all_gather | solution.py:571
  353.2 6.3 %shard_map.273 = f32[2,2,2,8,512]{4,3,2,1,0:T(8,128)S(1)} custom-call(f32[2,256]{1,0:T(2,128)S(1)} %get-tuple-element.299.keep_ref, bf16[512,512]{1,0:T(8,128)(2,1)S(1)} %get-tuple-element.235.u_ref.g_ref, f32[4,2,8,512]{3,2,1,0:T(8,128)S(1)} %pad_maximum_fusion.19.par_ref), custom_call_target="tpu_custom_call" | custom-call | tf_op jit(solution)/shard_map/pallas_call | solution.py:210
  367.2 7.5 %collective-permute-done.34 = f32[2,2,2,8,512]{4,3,2,0,1:T(8,128)S(1)} collective-permute-done((f32[2,2,2,8,512]{4,3,2,0,1:T(8,128)S(1)}, f32[2,2,2,8,512]{4,3,2,0,1:T(8,128)S(1)}, u32[]{:S(2)}, u32[]{:S(2)}) %collective-permute-start.34) | collective-permute-done | bytes 131104 | tf_op jit(solution)/shard_map/ppermute | solution.py:351
  377.3 8.1 %collective-permute-done.31 = bf16[512,512]{1,0:T(8,128)(2,1)S(1)} collective-permute-done((bf16[512,512]{1,0:T(8,128)(2,1)S(1)}, bf16[512,512]{1,0:T(8,128)(2,1)S(1)}, u32[]{:S(2)}, u32[]{:S(2)}) %collective-permute-start.31) | collective-permute-done | bytes 524320 | tf_op jit(solution)/shard_map/ppermute | solution.py:273
  387.3 22.7 %shard_map.274 = (bf16[512,512]{1,0:T(8,128)(2,1)S(1)}, f32[4,2,8,512]{3,2,1,0:T(8,128)S(1)}, f32[1,512]{1,0:T(1,128)S(1)}) custom-call(f32[2,256]{1,0:T(2,128)S(1)} %get-tuple-element.299.keep_ref, bf16[512,512]{1,0:T(8,128)(2,1)S(1)} %multiply_convert_fusion.3.u_ref, bf16[512,512]{1,0:T(8,128)(2,1)S(1)} %get-tuple-element.235.u_ref.g_ref, ...), custom_call_target="tpu_custom_call" | custom-call | tf_op jit(solution)/shard_map/pallas_call | solution.py:233
  418.2 5.0 convolution_convert_fusion.3
  423.2 16.0 %reduce-scatter.6.cloned.1.call-done = bf16[256,4224]{1,0:T(8,128)(2,1)} async-done(((bf16[1024,4224]{1,0:T(8,128)(2,1)}), bf16[256,4224]{1,0:T(8,128)(2,1)}) %reduce-scatter.6.cloned.1.call-update) | async-done | bytes 2162704 | tf_op jit(solution)/shard_map/reduce_scatter | solution.py:378
  447.2 6.6 %multiply_reduce_fusion.2 = (f32[1536]{0:T(1024)S(1)}, f32[1536]{0:T(1024)S(1)}, f32[1536]{0:T(1024)S(1)}) fusion(f32[2,256,1536]{2,1,0:T(8,128)} %bitcast.367, f32[2,256]{1,0:T(2,128)S(1)} %copy-done.69, f32[2,256,1536]{2,1,0:T(8,128)} %bitcast.361, f32[2,2,1536]{2,1,0:T(2,128)S(1)} %copy-done.55, f32[2,256]{1,0:T(2,128)S(1)} %copy-done.73, ...), kind=kLoop, calls=%fused_computation.36 | loop fusion | flops 8646144 | bytes 9486336 | tf_op jit(solution)/shard_map/reduce_sum | solution.py:606
  456.8 5.4 %add_convert_fusion.1 = bf16[1024,1536]{1,0:T(8,128)(2,1)} fusion(bf16[1024,1536]{1,0:T(8,128)(2,1)} %collective-permute-done.38, bf16[512,1024]{1,0:T(8,128)(2,1)S(1)} %copy-done.32, bf16[512,1536]{1,0:T(8,128)(2,1)S(1)} %bitcast.374), kind=kOutput, calls=%fused_computation.2 | convolution fusion | flops 1615331328 | bytes 8912896 | tf_op jit(solution)/shard_map/dot_general | solution.py:265
  492.3 4.7 reduce-scatter.8.cloned.1.call-done
  509.7 9.8 %collective-permute-done.47 = bf16[128,2048]{1,0:T(8,128)(2,1)S(1)} collective-permute-done((bf16[128,2048]{1,0:T(8,128)(2,1)S(1)}, bf16[128,2048]{1,0:T(8,128)(2,1)S(1)}, u32[]{:S(2)}, u32[]{:S(2)}) %collective-permute-start.47) | collective-permute-done | bytes 524320 | tf_op jit(solution)/shard_map/ppermute | solution.py:351
  (467 shorter events, 219.4 us)
Async XLA Ops:
  7.2 59.5 %all-gather.5.cloned.1.call-start = ((), (), s32[]{:S(2)}) async-start(), calls=%async_computation.3 | async-start | bytes 7077888 | tf_op jit(solution)/shard_map/all_gather | solution.py:355
  9.5 113.3 %all-gather.7.cloned.1.call-start = ((), (), s32[]{:S(2)}) async-start(), calls=%async_computation.4 | async-start | bytes 8847360 | tf_op jit(solution)/shard_map/all_gather | solution.py:355
  10.6 220.3 %all-gather.9.cloned.1.call-start = ((), (), s32[]{:S(2)}) async-start(), calls=%async_computation.5 | async-start | bytes 12976128 | tf_op jit(solution)/shard_map/all_gather | solution.py:355
  10.6 17.5 %collective-permute-start.2 = (bf16[512,512]{1,0:T(8,128)(2,1)}, bf16[512,512]{1,0:T(8,128)(2,1)}, u32[]{:S(2)}, u32[]{:S(2)}) collective-permute-start(bf16[512,512]{1,0:T(8,128)(2,1)} %bitcast), channel_id=1, source_target_pairs={{0,8},{8,0},{16,24},{24,16},{1,9},{9,1},{17,25},{25,17},{2,10},{10... | collective-permute-start | bytes 1572872 | tf_op jit(solution)/shard_map/ppermute | solution.py:273
  13.7 18.9 %collective-permute-start = (bf16[512,512]{1,0:T(8,128)(2,1)}, bf16[512,512]{1,0:T(8,128)(2,1)}, u32[]{:S(2)}, u32[]{:S(2)}) collective-permute-start(bf16[512,512]{1,0:T(8,128)(2,1)} %bitcast), channel_id=1, source_target_pairs={{8,16},{16,8},{9,17},{17,9},{10,18},{18,10},{11,19},{19,11},{12,20... | collective-permute-start | bytes 1572872 | tf_op jit(solution)/shard_map/ppermute | solution.py:273
  16.4 281.2 %reduce-scatter.4.cloned.1.call-start = ((), (), s32[]{:S(2)}) async-start(), calls=%async_computation.6 | async-start | bytes 2621440 | tf_op jit(solution)/shard_map/reduce_scatter | solution.py:556
  32.6 17.9 %collective-permute-start.1 = (bf16[512,512]{1,0:T(8,128)(2,1)}, bf16[512,512]{1,0:T(8,128)(2,1)S(1)}, u32[]{:S(2)}, u32[]{:S(2)}) collective-permute-start(bf16[512,512]{1,0:T(8,128)(2,1)} %collective-permute-done), channel_id=1, source_target_pairs={{0,8},{8,0},{16,24},{24,16},{1,9},{9,1},{17,25},{25,17},{2,10},{10... | collective-permute-start | bytes 1572872 | tf_op jit(solution)/shard_map/ppermute | solution.py:273
  37.5 22.8 %collective-permute-start.4 = (bf16[512,512]{1,0:T(8,128)(2,1)S(1)}, bf16[512,512]{1,0:T(8,128)(2,1)S(1)}, u32[]{:S(2)}, u32[]{:S(2)}) collective-permute-start(bf16[512,512]{1,0:T(8,128)(2,1)S(1)} %collective-permute-done.3), channel_id=1, source_target_pairs={{0,8},{8,0},{16,24},{24,16},{1,9},{9,1},{17,25},{25,17},{2,10},{10... | collective-permute-start | bytes 1572872 | tf_op jit(solution)/shard_map/ppermute | solution.py:273
  88.3 18.1 %collective-permute-start.9 = (bf16[512,512]{1,0:T(8,128)(2,1)S(1)}, bf16[512,512]{1,0:T(8,128)(2,1)S(1)}, u32[]{:S(2)}, u32[]{:S(2)}) collective-permute-start(bf16[512,512]{1,0:T(8,128)(2,1)S(1)} %bitcast.369), channel_id=1, source_target_pairs={{0,8},{8,0},{16,24},{24,16},{1,9},{9,1},{17,25},{25,17},{2,10},{10... | collective-permute-start | bytes 1572872 | tf_op jit(solution)/shard_map/ppermute | solution.py:273
  103.6 17.0 %collective-permute-start.11 = (bf16[512,512]{1,0:T(8,128)(2,1)S(1)}, bf16[512,512]{1,0:T(8,128)(2,1)S(1)}, u32[]{:S(2)}, u32[]{:S(2)}) collective-permute-start(bf16[512,512]{1,0:T(8,128)(2,1)S(1)} %collective-permute-done.10), channel_id=1, source_target_pairs={{0,8},{8,0},{16,24},{24,16},{1,9},{9,1},{17,25},{25,17},{2,10},{10... | collective-permute-start | bytes 1572872 | tf_op jit(solution)/shard_map/ppermute | solution.py:273
  106.4 14.2 %collective-permute-start.12 = (bf16[512,512]{1,0:T(8,128)(2,1)S(1)}, bf16[512,512]{1,0:T(8,128)(2,1)}, u32[]{:S(2)}, u32[]{:S(2)}) collective-permute-start(bf16[512,512]{1,0:T(8,128)(2,1)S(1)} %collective-permute-done.9), channel_id=1, source_target_pairs={{8,16},{16,8},{9,17},{17,9},{10,18},{18,10},{11,19},{19,11},{12,20... | collective-permute-start | bytes 1572872 | tf_op jit(solution)/shard_map/ppermute | solution.py:273
  127.8 13.9 %collective-permute-start.13 = (bf16[512,512]{1,0:T(8,128)(2,1)S(1)}, bf16[512,512]{1,0:T(8,128)(2,1)}, u32[]{:S(2)}, u32[]{:S(2)}) collective-permute-start(bf16[512,512]{1,0:T(8,128)(2,1)S(1)} %constant_dynamic-slice_fusion.34), channel_id=1, source_target_pairs={{0,8},{8,0},{16,24},{24,16},{1,9},{9,1},{17,25},{25,17},{2,10},{10... | collective-permute-start | bytes 1572872 | tf_op jit(solution)/shard_map/ppermute | solution.py:273
  144.9 13.7 %collective-permute-start.14 = (bf16[512,512]{1,0:T(8,128)(2,1)S(1)}, bf16[512,512]{1,0:T(8,128)(2,1)}, u32[]{:S(2)}, u32[]{:S(2)}) collective-permute-start(bf16[512,512]{1,0:T(8,128)(2,1)S(1)} %get-tuple-element.158), channel_id=1, source_target_pairs={{8,16},{16,8},{9,17},{17,9},{10,18},{18,10},{11,19},{19,11},{12,20... | collective-permute-start | bytes 1572872 | tf_op jit(solution)/shard_map/ppermute | solution.py:273
  160.0 15.3 %collective-permute-start.15 = (bf16[512,512]{1,0:T(8,128)(2,1)S(1)}, bf16[512,512]{1,0:T(8,128)(2,1)}, u32[]{:S(2)}, u32[]{:S(2)}) collective-permute-start(bf16[512,512]{1,0:T(8,128)(2,1)S(1)} %dynamic-slice_add_fusion.3), channel_id=1, source_target_pairs={{0,8},{8,0},{16,24},{24,16},{1,9},{9,1},{17,25},{25,17},{2,10},{10... | collective-permute-start | bytes 1572872 | tf_op jit(solution)/shard_map/ppermute | solution.py:273
  162.3 24.2 %collective-permute-start.23 = (bf16[512,512]{1,0:T(8,128)(2,1)}, bf16[512,512]{1,0:T(8,128)(2,1)}, u32[]{:S(2)}, u32[]{:S(2)}) collective-permute-start(bf16[512,512]{1,0:T(8,128)(2,1)} %collective-permute-done.12), channel_id=1, source_target_pairs={{0,8},{8,0},{16,24},{24,16},{1,9},{9,1},{17,25},{25,17},{2,10},{10... | collective-permute-start | bytes 1572872 | tf_op jit(solution)/shard_map/ppermute | solution.py:273
  178.1 15.9 %collective-permute-start.20 = (bf16[512,512]{1,0:T(8,128)(2,1)S(1)}, bf16[512,512]{1,0:T(8,128)(2,1)S(1)}, u32[]{:S(2)}, u32[]{:S(2)}) collective-permute-start(bf16[512,512]{1,0:T(8,128)(2,1)S(1)} %get-tuple-element.156), channel_id=1, source_target_pairs={{0,8},{8,0},{16,24},{24,16},{1,9},{9,1},{17,25},{25,17},{2,10},{10... | collective-permute-start | bytes 1572872 | tf_op jit(solution)/shard_map/ppermute | solution.py:273
  195.2 25.0 %collective-permute-start.19 = (bf16[512,512]{1,0:T(8,128)(2,1)S(1)}, bf16[512,512]{1,0:T(8,128)(2,1)S(1)}, u32[]{:S(2)}, u32[]{:S(2)}) collective-permute-start(bf16[512,512]{1,0:T(8,128)(2,1)S(1)} %collective-permute-done.18), channel_id=1, source_target_pairs={{0,8},{8,0},{16,24},{24,16},{1,9},{9,1},{17,25},{25,17},{2,10},{10... | collective-permute-start | bytes 1572872 | tf_op jit(solution)/shard_map/ppermute | solution.py:273
  206.7 18.3 %collective-permute-start.22 = (bf16[512,512]{1,0:T(8,128)(2,1)S(1)}, bf16[512,512]{1,0:T(8,128)(2,1)S(1)}, u32[]{:S(2)}, u32[]{:S(2)}) collective-permute-start(bf16[512,512]{1,0:T(8,128)(2,1)S(1)} %collective-permute-done.21), channel_id=1, source_target_pairs={{0,8},{8,0},{16,24},{24,16},{1,9},{9,1},{17,25},{25,17},{2,10},{10... | collective-permute-start | bytes 1572872 | tf_op jit(solution)/shard_map/ppermute | solution.py:273
  254.9 90.7 %all-gather.11.cloned.1.call-start = ((), (), s32[]{:S(2)}) async-start(), calls=%async_computation.7 | async-start | bytes 2621440 | tf_op jit(solution)/shard_map/all_gather | solution.py:571
  263.1 48.9 %collective-permute-start.26 = (bf16[1024,2816]{1,0:T(8,128)(2,1)}, bf16[1024,2816]{1,0:T(8,128)(2,1)}, u32[]{:S(2)}, u32[]{:S(2)}) collective-permute-start(bf16[1024,2816]{1,0:T(8,128)(2,1)} %convolution_convert_fusion), channel_id=1, source_target_pairs={{0,1},{1,0},{2,3},{3,2},{4,5},{5,4},{6,7},{7,6},{8,9},{9,8},{10,11... | collective-permute-start | bytes 17301512 | tf_op jit(solution)/shard_map/ppermute | solution.py:351
  268.3 35.1 %collective-permute-start.27 = (bf16[1024,1408]{1,0:T(8,128)(2,1)}, bf16[1024,1408]{1,0:T(8,128)(2,1)}, u32[]{:S(2)}, u32[]{:S(2)}) collective-permute-start(bf16[1024,1408]{1,0:T(8,128)(2,1)} %convolution_convert_fusion.2), channel_id=1, source_target_pairs={{0,1},{1,0},{2,3},{3,2},{4,5},{5,4},{6,7},{7,6},{8,9},{9,8},{10,11... | collective-permute-start | bytes 8650760 | tf_op jit(solution)/shard_map/ppermute | solution.py:351
  300.3 138.9 %reduce-scatter.6.cloned.1.call-start = ((), (), s32[]{:S(2)}) async-start(), calls=%async_computation.8 | async-start | bytes 10813440 | tf_op jit(solution)/shard_map/reduce_scatter | solution.py:378
  345.7 151.4 %reduce-scatter.8.cloned.1.call-start = ((), (), s32[]{:S(2)}) async-start(), calls=%async_computation.9 | async-start | bytes 2621440 | tf_op jit(solution)/shard_map/reduce_scatter | solution.py:602
  359.7 15.0 %collective-permute-start.28 = (bf16[512,512]{1,0:T(8,128)(2,1)S(1)}, bf16[512,512]{1,0:T(8,128)(2,1)S(1)}, u32[]{:S(2)}, u32[]{:S(2)}) collective-permute-start(bf16[512,512]{1,0:T(8,128)(2,1)S(1)} %get-tuple-element.197), channel_id=1, source_target_pairs={{0,8},{8,0},{16,24},{24,16},{1,9},{9,1},{17,25},{25,17},{2,10},{10... | collective-permute-start | bytes 1572872 | tf_op jit(solution)/shard_map/ppermute | solution.py:273
  359.8 25.5 %collective-permute-start.31 = (bf16[512,512]{1,0:T(8,128)(2,1)S(1)}, bf16[512,512]{1,0:T(8,128)(2,1)S(1)}, u32[]{:S(2)}, u32[]{:S(2)}) collective-permute-start(bf16[512,512]{1,0:T(8,128)(2,1)S(1)} %get-tuple-element.198), channel_id=1, source_target_pairs={{0,8},{8,0},{16,24},{24,16},{1,9},{9,1},{17,25},{25,17},{2,10},{10... | collective-permute-start | bytes 1572872 | tf_op jit(solution)/shard_map/ppermute | solution.py:273
  364.0 46.0 %collective-permute-start.36 = (bf16[1024,512]{1,0:T(8,128)(2,1)}, bf16[1024,512]{1,0:T(8,128)(2,1)S(1)}, u32[]{:S(2)}, u32[]{:S(2)}) collective-permute-start(bf16[1024,512]{1,0:T(8,128)(2,1)} %convolution_convert_fusion.6), channel_id=1, source_target_pairs={{0,1},{1,0},{2,3},{3,2},{4,5},{5,4},{6,7},{7,6},{8,9},{9,8},{10,11... | collective-permute-start | bytes 3145736 | tf_op jit(solution)/shard_map/ppermute | solution.py:351
  386.5 25.3 %collective-permute-start.32 = (bf16[512,512]{1,0:T(8,128)(2,1)S(1)}, bf16[512,512]{1,0:T(8,128)(2,1)S(1)}, u32[]{:S(2)}, u32[]{:S(2)}) collective-permute-start(bf16[512,512]{1,0:T(8,128)(2,1)S(1)} %get-tuple-element.196), channel_id=1, source_target_pairs={{8,16},{16,8},{9,17},{17,9},{10,18},{18,10},{11,19},{19,11},{12,20... | collective-permute-start | bytes 1572872 | tf_op jit(solution)/shard_map/ppermute | solution.py:273
  442.7 14.1 %collective-permute-start.38 = (bf16[1024,1536]{1,0:T(8,128)(2,1)}, bf16[1024,1536]{1,0:T(8,128)(2,1)}, u32[]{:S(2)}, u32[]{:S(2)}) collective-permute-start(bf16[1024,1536]{1,0:T(8,128)(2,1)} %convolution_convert_fusion.1), channel_id=1, source_target_pairs={{0,1},{1,0},{2,3},{3,2},{4,5},{5,4},{6,7},{7,6},{8,9},{9,8},{10,11... | collective-permute-start | bytes 9437192 | tf_op jit(solution)/shard_map/ppermute | solution.py:351
  445.7 46.7 %collective-permute-start.30 = (bf16[512,512]{1,0:T(8,128)(2,1)}, bf16[512,512]{1,0:T(8,128)(2,1)}, u32[]{:S(2)}, u32[]{:S(2)}) collective-permute-start(bf16[512,512]{1,0:T(8,128)(2,1)} %get-tuple-element.195), channel_id=1, source_target_pairs={{0,8},{8,0},{16,24},{24,16},{1,9},{9,1},{17,25},{25,17},{2,10},{10... | collective-permute-start | bytes 1572872 | tf_op jit(solution)/shard_map/ppermute | solution.py:273
  478.4 25.9 %collective-permute-start.46 = (bf16[2,128,2048]{2,1,0:T(8,128)(2,1)}, bf16[2,128,2048]{2,1,0:T(8,128)(2,1)}, u32[]{:S(2)}, u32[]{:S(2)}) collective-permute-start(bf16[2,128,2048]{2,1,0:T(8,128)(2,1)} %dynamic-slice_bitcast_fusion), channel_id=1, source_target_pairs={{0,4},{1,5},{2,6},{3,7},{4,0},{5,1},{6,2},{7,3},{8,12},{9,13},{10,... | collective-permute-start | bytes 3145736 | tf_op jit(solution)/shard_map/ppermute | solution.py:351
  481.3 25.9 %collective-permute-start.44 = (bf16[2,128,2048]{2,1,0:T(8,128)(2,1)}, bf16[2,128,2048]{2,1,0:T(8,128)(2,1)}, u32[]{:S(2)}, u32[]{:S(2)}) collective-permute-start(bf16[2,128,2048]{2,1,0:T(8,128)(2,1)} %dynamic-slice_bitcast_fusion.1), channel_id=1, source_target_pairs={{0,2},{1,3},{2,0},{3,1},{4,6},{5,7},{6,4},{7,5},{8,10},{9,11},{10,... | collective-permute-start | bytes 3145736 | tf_op jit(solution)/shard_map/ppermute | solution.py:351
  505.9 13.6 %collective-permute-start.47 = (bf16[128,2048]{1,0:T(8,128)(2,1)S(1)}, bf16[128,2048]{1,0:T(8,128)(2,1)S(1)}, u32[]{:S(2)}, u32[]{:S(2)}) collective-permute-start(bf16[128,2048]{1,0:T(8,128)(2,1)S(1)} %dynamic-slice_bitcast_fusion.2), channel_id=1, source_target_pairs={{0,2},{1,3},{2,0},{3,1},{4,6},{5,7},{6,4},{7,5},{8,10},{9,11},{10,... | collective-permute-start | bytes 1572872 | tf_op jit(solution)/shard_map/ppermute | solution.py:351
  (113 other events, 835.2 us)
Sparse Core Ops, SparseCore 0:
  10.5 48.2 all-gather.4
  61.2 56.4 all-gather.6
  120.2 67.6 all-gather.8
  255.1 42.5 reduce-scatter.3
  300.4 45.2 all-gather.10
  349.0 90.2 reduce-scatter.5
  447.3 49.7 reduce-scatter.7

commit v5 on v4

--- a/solution.py
+++ b/solution.py
@@ -399,7 +399,7 @@
         rest = chip_bits[::-1]
         for bit in order[:-1]:
             part, rest = halve(part, rest, bit)
-        part, rest = halve(after(part.astype(bf16), *before_last), rest, order[-1])
+        part, rest = halve(after(part.astype(bf16), *before_last) if before_last else part, rest, order[-1])
         parts.append(with_layout_constraint(part, Layout(major_to_minor=(0, 1))))
     return parts
 
@@ -600,22 +600,22 @@
     d_project = d_project.astype(bf16).reshape(tokens, 3 * share)
     part_one = dot_rows(d_project, w_in).astype(bf16)
     dn_one = lax.psum_scatter(after(part_one, feed_own), "fsdp", scatter_dimension=1, tiled=True)
-    in_give = core_give(normed_one, after(d_project, part_one, feed_own))
+    in_give = core_give(normed_one, after(d_project, part_one))
     in_got = swap_seq(in_give, 0)
-    d_conv, late_project, late_part = lax.optimization_barrier((d_conv, d_project, part_one, in_give))[:3]
+    in_sum = core_sum(normed_one, d_project, in_got)
+    in_out = chip_sums(jnp.concatenate([in_sum, out_sum], axis=1), dn_one)
+    d_conv, late_project, late_part = lax.optimization_barrier((d_conv, d_project, part_one, in_sum, feed_own))[:3]
     short_part = jnp.stack([jnp.sum(masks[lag] * lagged[lag] * d_conv, axis=(0, 1)) for lag in range(3)])
     mixer_gain_part = jnp.sum(unit_one * late_part.astype(f32), axis=0)
-    in_sum = core_sum(normed_one, d_project, after(in_got, mixer_gain_part))
-    small = after((mixer_gain_part, feed_gain_part, short_part, mode_sums, skip_sums), in_sum)
+    small = [mixer_gain_part, feed_gain_part, short_part, mode_sums, skip_sums]
     small = jnp.concatenate([part.reshape(-1, share) for part in small])
     for bit in range(1, seq_count.bit_length() - 1):
         small = small + swap_seq(small, bit)
-    in_out = jnp.concatenate([in_sum, out_sum], axis=1)
     feed_own = after(feed_own, in_sum)
     gate_grad, up_grad, down_grad = (
         feed_own[:, i * units : (i + 1) * units].astype(f32) for i in range(3)
     )
-    in_out = chip_sums(after(in_out, small), dn_one)
+    small = small
     small = small + swap_seq(small, 0)
     gain_rows = 2 * width // share
     along_one = jnp.sum(late_project.astype(f32) * project.reshape(tokens, 3 * share), axis=-1)

time: 541 us -> 539 us (level)
  waiting for transfers between devices: 178 us -> 161 us
  starting transfers between devices: 91.4 us -> 102 us
  local copies, waits for them, and re-layouts: 30.1 us -> 36.6 us
    reduce_scatter x1, waiting for transfers between devices: 16 us -> 0.01 us  [chip_sums_offloaded(): lax.psum_scatter(summed, 'seq', scatter_dimension=0, axis_index_groups=gr...]
    ppermute x29, starting transfers between devices: 69.1 us -> 77.7 us  [along_line(): return lax.ppermute(array, 'fsdp', pairs)]
    ppermute x17, waiting for transfers between devices: 34.6 us -> 43.1 us  [swap_seq(): lax.ppermute(array, 'seq', [(i, i ^ 1 << bit) for i in range(lax.axis_siz...]
    unnamed x185 -> x201, local copies, waits for them, and re-layouts: 16.2 us -> 14.6 us
  transfers between devices with their start and end apart: 55 -> 55, of which waited for: 27 -> 25; matrix products, arithmetic and copies ran while one was open for 29% -> 31% of each run, Pallas kernels for 9% -> 9%
where the time goes in v5:
time: 539 us; the launch traced here: 529 us
  waiting for transfers between devices  161 us (30%)
  starting transfers between devices  102 us (19%)
  other arithmetic  88.4 us (16%)
  matrix products  78.7 us (15%)
  Pallas kernels  45.6 us (8%)
  local copies, waits for them, and re-layouts  36.6 us (7%)
  between operations  16.4 us (3%)
    ppermute x29, starting transfers between devices, along_line(): return lax.ppermute(array, 'fsdp', pairs)  77.7 us
    ppermute x29, waiting for transfers between devices, along_line(): return lax.ppermute(array, 'fsdp', pairs)  72 us
    ppermute x17, waiting for transfers between devices, swap_seq(): lax.ppermute(array, 'seq', [(i, i ^ 1 << bit) for i in range(lax.axis_siz...  43.1 us
    dot_general x8, matrix products, dot_tokens(): lax.dot_general(left, right, (((0,), (0,)), ((), ())), preferred_element_...  31.2 us
    dot_general x4, matrix products, dot(): return jnp.dot(left, right, preferred_element_type=f32)  27.9 us
    all_gather x1, waiting for transfers between devices, on_device(): d_mix = lax.all_gather(d_share, 'fsdp', axis=1, tiled=True)  24.6 us
    pallas_call x1, Pallas kernels, long_conv_back(): pl.pallas_call(functools.partial(back_kernel, batches), out_shape=(jax.Sh...  22.7 us
    ppermute x17, starting transfers between devices, swap_seq(): lax.ppermute(array, 'seq', [(i, i ^ 1 << bit) for i in range(lax.axis_siz...  20.3 us
  transfers between devices with their start and end apart: 55, of which 25 were waited for; matrix products, arithmetic and copies ran while one was open for 31% of the time, Pallas kernels for 9%

profile of v5, /device:TPU:0, one launch (start us, length us, event | category | flops | bytes accessed | tf_op | source)
XLA Modules:
  0.0 528.8 jit_solution(14360076139250646637)
XLA Ops:
  32.6 4.9 collective-permute-start.1
  37.5 9.5 %collective-permute-start.4 = (bf16[512,512]{1,0:T(8,128)(2,1)S(1)}, bf16[512,512]{1,0:T(8,128)(2,1)S(1)}, u32[]{:S(2)}, u32[]{:S(2)}) collective-permute-start(bf16[512,512]{1,0:T(8,128)(2,1)S(1)} %collective-permute-done.3), channel_id=1, source_target_pairs={{0,8},{8,0},{16,24},{24,16},{1,9},{9,1},{17,25},{25,17},{2,10},{10... | collective-permute-start | bytes 1572872 | tf_op jit(solution)/shard_map/ppermute | solution.py:273
  50.5 9.8 %collective-permute-done.4 = bf16[512,512]{1,0:T(8,128)(2,1)S(1)} collective-permute-done((bf16[512,512]{1,0:T(8,128)(2,1)S(1)}, bf16[512,512]{1,0:T(8,128)(2,1)S(1)}, u32[]{:S(2)}, u32[]{:S(2)}) %collective-permute-start.4) | collective-permute-done | bytes 524320 | tf_op jit(solution)/shard_map/ppermute | solution.py:273
  66.6 6.9 %fusion.67 = f32[512,1536]{1,0:T(8,128)S(1)} fusion(bf16[512,2048]{1,0:T(8,128)(2,1)} %fusion.10, bf16[2048,1536]{1,0:T(8,128)(2,1)} %all-gather.5.cloned.1.call-done), kind=kOutput, calls=%fused_computation.365 | convolution fusion | flops 3221225472 | bytes 11534336 | tf_op jit(solution)/shard_map/dot_general | solution.py:269
  79.2 6.4 %shard_map.271 = f32[2,2,2,8,512]{4,3,2,1,0:T(8,128)S(1)} custom-call(f32[2,256]{1,0:T(2,128)S(1)} %get-tuple-element.285.keep_ref, bf16[512,512]{1,0:T(8,128)(2,1)S(1)} %multiply_convert_fusion.3.u_ref, f32[4,2,8,512]{3,2,1,0:T(8,128)S(1)} %pad_maximum_fusion.19.par_ref), custom_call_target="tpu_custom_call" | custom-call | tf_op jit(solution)/shard_map/pallas_call | solution.py:210
  93.6 6.9 %collective-permute-done.7 = f32[2,2,2,8,512]{4,3,2,0,1:T(8,128)S(1)} collective-permute-done((f32[2,2,2,8,512]{4,3,2,0,1:T(8,128)S(1)}, f32[2,2,2,8,512]{4,3,2,0,1:T(8,128)S(1)}, u32[]{:S(2)}, u32[]{:S(2)}) %collective-permute-start.7) | collective-permute-done | bytes 131104 | tf_op jit(solution)/shard_map/ppermute | solution.py:351
  110.3 10.2 %shard_map.272 = bf16[512,512]{1,0:T(8,128)(2,1)S(1)} custom-call(f32[2,256]{1,0:T(2,128)S(1)} %get-tuple-element.285.keep_ref, bf16[512,512]{1,0:T(8,128)(2,1)S(1)} %multiply_convert_fusion.3.u_ref, f32[2,2,2,8,512]{4,3,2,1,0:T(8,128)S(1)} %copy.52.into_ref, f32[4,2,8,512]{3,2,1,0:T(8,128)S(1)} %pad_maximum_fusion.19.par_ref, f32[1,512]{1,0:T(1,128)S(1)} %bitcast.357), custom_call_target="tpu_custom_call" | custom-call | tf_op jit(solution)/shard_map/pallas_call | solution.py:221
  130.6 11.1 %collective-permute-done.13 = bf16[512,512]{1,0:T(8,128)(2,1)} collective-permute-done((bf16[512,512]{1,0:T(8,128)(2,1)S(1)}, bf16[512,512]{1,0:T(8,128)(2,1)}, u32[]{:S(2)}, u32[]{:S(2)}) %collective-permute-start.13) | collective-permute-done | bytes 524320 | tf_op jit(solution)/shard_map/ppermute | solution.py:273
  146.3 9.0 %collective-permute-done.16 = bf16[512,512]{1,0:T(8,128)(2,1)} collective-permute-done((bf16[512,512]{1,0:T(8,128)(2,1)S(1)}, bf16[512,512]{1,0:T(8,128)(2,1)}, u32[]{:S(2)}, u32[]{:S(2)}) %collective-permute-start.16) | collective-permute-done | bytes 524320 | tf_op jit(solution)/shard_map/ppermute | solution.py:273
  162.2 12.9 %collective-permute-done.15 = bf16[512,512]{1,0:T(8,128)(2,1)} collective-permute-done((bf16[512,512]{1,0:T(8,128)(2,1)S(1)}, bf16[512,512]{1,0:T(8,128)(2,1)}, u32[]{:S(2)}, u32[]{:S(2)}) %collective-permute-start.15) | collective-permute-done | bytes 524320 | tf_op jit(solution)/shard_map/ppermute | solution.py:273
  179.9 6.4 %collective-permute-done.23 = bf16[512,512]{1,0:T(8,128)(2,1)} collective-permute-done((bf16[512,512]{1,0:T(8,128)(2,1)}, bf16[512,512]{1,0:T(8,128)(2,1)}, u32[]{:S(2)}, u32[]{:S(2)}) %collective-permute-start.23) | collective-permute-done | bytes 524320 | tf_op jit(solution)/shard_map/ppermute | solution.py:273
  188.8 4.9 collective-permute-done.20
  194.9 11.8 %collective-permute-start.19 = (bf16[512,512]{1,0:T(8,128)(2,1)S(1)}, bf16[512,512]{1,0:T(8,128)(2,1)S(1)}, u32[]{:S(2)}, u32[]{:S(2)}) collective-permute-start(bf16[512,512]{1,0:T(8,128)(2,1)S(1)} %collective-permute-done.18), channel_id=1, source_target_pairs={{0,8},{8,0},{16,24},{24,16},{1,9},{9,1},{17,25},{25,17},{2,10},{10... | collective-permute-start | bytes 1572872 | tf_op jit(solution)/shard_map/ppermute | solution.py:273
  206.7 5.7 %collective-permute-start.22 = (bf16[512,512]{1,0:T(8,128)(2,1)S(1)}, bf16[512,512]{1,0:T(8,128)(2,1)S(1)}, u32[]{:S(2)}, u32[]{:S(2)}) collective-permute-start(bf16[512,512]{1,0:T(8,128)(2,1)S(1)} %collective-permute-done.21), channel_id=1, source_target_pairs={{0,8},{8,0},{16,24},{24,16},{1,9},{9,1},{17,25},{25,17},{2,10},{10... | collective-permute-start | bytes 1572872 | tf_op jit(solution)/shard_map/ppermute | solution.py:273
  212.4 7.7 %fusion.2 = f32[512,1408]{1,0:T(8,128)} fusion(bf16[512,2048]{1,0:T(8,128)(2,1)S(1)} %pad_maximum_fusion.7, bf16[2048,1920]{0,1:T(8,128)(2,1)} %all-gather.7.cloned.1.call-done), kind=kOutput, calls=%fused_computation.11 | convolution fusion | flops 2952790016 | bytes 10747904 | tf_op jit(solution)/shard_map/dot_general | solution.py:269
  220.0 4.6 collective-permute-done.22
  230.5 10.3 %fusion.68 = f32[512,2816]{1,0:T(8,128)S(1)} fusion(bf16[512,2048]{1,0:T(8,128)(2,1)} %copy-done.15, bf16[2048,2816]{1,0:T(8,128)(2,1)} %all-gather.9.cloned.1.call-done), kind=kOutput, calls=%fused_computation.366 | convolution fusion | flops 5905580032 | bytes 19398656 | tf_op jit(solution)/shard_map/dot_general | solution.py:269
  247.2 7.4 %convolution_convert_fusion.4 = bf16[512,2048]{1,0:T(8,128)(2,1)} fusion(bf16[2048,2816]{1,0:T(8,128)(2,1)S(1)} %copy-done.93, bf16[512,1408]{1,0:T(8,128)(2,1)S(1)} %get-tuple-element.153, bf16[512,1408]{1,0:T(8,128)(2,1)S(1)} %get-tuple-element.151), kind=kOutput, calls=%fused_computation.40 | convolution fusion | flops 5912395776 | bytes 16515072 | tf_op jit(solution)/shard_map/dot_general | solution.py:261
  254.8 7.9 %convolution_convert_fusion = bf16[1024,2816]{1,0:T(8,128)(2,1)} fusion(bf16[512,1024]{1,0:T(8,128)(2,1)} %pad_maximum_fusion.10, bf16[512,2816]{1,0:T(8,128)(2,1)} %pad_maximum_fusion.4), kind=kOutput, calls=%fused_computation.4 | convolution fusion | flops 2955673600 | bytes 9699328 | tf_op jit(solution)/shard_map/dot_general | solution.py:265
  277.3 20.0 %reduce-scatter.4.cloned.1.call-done = bf16[512,512]{1,0:T(8,128)(2,1)} async-done(((bf16[512,2048]{1,0:T(8,128)(2,1)}), bf16[512,512]{1,0:T(8,128)(2,1)}) %reduce-scatter.4.cloned.1.call-update) | async-done | bytes 524304 | tf_op jit(solution)/shard_map/reduce_scatter | solution.py:556
  306.9 4.7 fusion.16
  311.6 5.3 %add_convert_fusion = bf16[1024,2816]{1,0:T(8,128)(2,1)S(1)} fusion(bf16[1024,2816]{1,0:T(8,128)(2,1)} %collective-permute-done.26, bf16[512,1024]{1,0:T(8,128)(2,1)S(1)} %pad_maximum_fusion.9, bf16[512,1408]{1,0:T(8,128)(2,1)S(1)} %copy-done.25, bf16[512,1408]{1,0:T(8,128)(2,1)S(1)} %copy-done.23), kind=kOutput, calls=%fused_computation | convolution fusion | flops 2967207936 | bytes 15466496 | tf_op jit(solution)/shard_map/dot_general | solution.py:265
  320.8 24.6 %all-gather.11.cloned.1.call-done = bf16[512,2048]{1,0:T(8,128)(2,1)} async-done(((bf16[512,512]{1,0:T(8,128)(2,1)}), bf16[512,2048]{1,0:T(8,128)(2,1)}) %all-gather.11.cloned.1.call-update) | async-done | bytes 2097168 | tf_op jit(solution)/shard_map/all_gather | solution.py:571
  353.2 6.3 %shard_map.273 = f32[2,2,2,8,512]{4,3,2,1,0:T(8,128)S(1)} custom-call(f32[2,256]{1,0:T(2,128)S(1)} %get-tuple-element.285.keep_ref, bf16[512,512]{1,0:T(8,128)(2,1)S(1)} %get-tuple-element.221.u_ref.g_ref, f32[4,2,8,512]{3,2,1,0:T(8,128)S(1)} %pad_maximum_fusion.19.par_ref), custom_call_target="tpu_custom_call" | custom-call | tf_op jit(solution)/shard_map/pallas_call | solution.py:210
  367.2 7.5 %collective-permute-done.34 = f32[2,2,2,8,512]{4,3,2,0,1:T(8,128)S(1)} collective-permute-done((f32[2,2,2,8,512]{4,3,2,0,1:T(8,128)S(1)}, f32[2,2,2,8,512]{4,3,2,0,1:T(8,128)S(1)}, u32[]{:S(2)}, u32[]{:S(2)}) %collective-permute-start.34) | collective-permute-done | bytes 131104 | tf_op jit(solution)/shard_map/ppermute | solution.py:351
  377.2 8.1 %collective-permute-done.31 = bf16[512,512]{1,0:T(8,128)(2,1)S(1)} collective-permute-done((bf16[512,512]{1,0:T(8,128)(2,1)S(1)}, bf16[512,512]{1,0:T(8,128)(2,1)S(1)}, u32[]{:S(2)}, u32[]{:S(2)}) %collective-permute-start.31) | collective-permute-done | bytes 524320 | tf_op jit(solution)/shard_map/ppermute | solution.py:273
  387.3 22.7 %shard_map.274 = (bf16[512,512]{1,0:T(8,128)(2,1)S(1)}, f32[4,2,8,512]{3,2,1,0:T(8,128)S(1)}, f32[1,512]{1,0:T(1,128)S(1)}) custom-call(f32[2,256]{1,0:T(2,128)S(1)} %get-tuple-element.285.keep_ref, bf16[512,512]{1,0:T(8,128)(2,1)S(1)} %multiply_convert_fusion.3.u_ref, bf16[512,512]{1,0:T(8,128)(2,1)S(1)} %get-tuple-element.221.u_ref.g_ref, ...), custom_call_target="tpu_custom_call" | custom-call | tf_op jit(solution)/shard_map/pallas_call | solution.py:233
  418.1 4.8 convolution_convert_fusion.3
  431.9 7.9 %collective-permute-start.30 = (bf16[512,512]{1,0:T(8,128)(2,1)}, bf16[512,512]{1,0:T(8,128)(2,1)}, u32[]{:S(2)}, u32[]{:S(2)}) collective-permute-start(bf16[512,512]{1,0:T(8,128)(2,1)} %get-tuple-element.181), channel_id=1, source_target_pairs={{0,8},{8,0},{16,24},{24,16},{1,9},{9,1},{17,25},{25,17},{2,10},{10... | collective-permute-start | bytes 1572872 | tf_op jit(solution)/shard_map/ppermute | solution.py:273
  453.0 6.7 %multiply_reduce_fusion.2 = (f32[1536]{0:T(1024)S(1)}, f32[1536]{0:T(1024)S(1)}, f32[1536]{0:T(1024)S(1)}) fusion(f32[2,256,1536]{2,1,0:T(8,128)} %bitcast.367, f32[2,256]{1,0:T(2,128)S(1)} %copy-done.76, f32[2,256,1536]{2,1,0:T(8,128)} %bitcast.361, f32[2,2,1536]{2,1,0:T(2,128)S(1)} %copy-done.62, f32[2,256]{1,0:T(2,128)S(1)} %copy-done.80, ...), kind=kLoop, calls=%fused_computation.36 | loop fusion | flops 8646144 | bytes 9486336 | tf_op jit(solution)/shard_map/reduce_sum | solution.py:608
  462.4 10.9 %collective-permute-done.46 = bf16[2,128,2048]{2,1,0:T(8,128)(2,1)} collective-permute-done((bf16[2,128,2048]{2,1,0:T(8,128)(2,1)}, bf16[2,128,2048]{2,1,0:T(8,128)(2,1)}, u32[]{:S(2)}, u32[]{:S(2)}) %collective-permute-start.46) | collective-permute-done | bytes 1048608 | tf_op jit(solution)/shard_map/ppermute | solution.py:351
  511.3 6.3 %collective-permute-done.47 = bf16[128,2048]{1,0:T(8,128)(2,1)S(1)} collective-permute-done((bf16[128,2048]{1,0:T(8,128)(2,1)S(1)}, bf16[128,2048]{1,0:T(8,128)(2,1)S(1)}, u32[]{:S(2)}, u32[]{:S(2)}) %collective-permute-start.47) | collective-permute-done | bytes 524320 | tf_op jit(solution)/shard_map/ppermute | solution.py:351
  (483 shorter events, 222.5 us)
Async XLA Ops:
  7.2 59.4 %all-gather.5.cloned.1.call-start = ((), (), s32[]{:S(2)}) async-start(), calls=%async_computation.3 | async-start | bytes 7077888 | tf_op jit(solution)/shard_map/all_gather | solution.py:355
  9.5 113.3 %all-gather.7.cloned.1.call-start = ((), (), s32[]{:S(2)}) async-start(), calls=%async_computation.4 | async-start | bytes 8847360 | tf_op jit(solution)/shard_map/all_gather | solution.py:355
  10.6 219.9 %all-gather.9.cloned.1.call-start = ((), (), s32[]{:S(2)}) async-start(), calls=%async_computation.5 | async-start | bytes 12976128 | tf_op jit(solution)/shard_map/all_gather | solution.py:355
  10.6 17.5 %collective-permute-start.2 = (bf16[512,512]{1,0:T(8,128)(2,1)}, bf16[512,512]{1,0:T(8,128)(2,1)}, u32[]{:S(2)}, u32[]{:S(2)}) collective-permute-start(bf16[512,512]{1,0:T(8,128)(2,1)} %bitcast), channel_id=1, source_target_pairs={{0,8},{8,0},{16,24},{24,16},{1,9},{9,1},{17,25},{25,17},{2,10},{10... | collective-permute-start | bytes 1572872 | tf_op jit(solution)/shard_map/ppermute | solution.py:273
  13.7 18.9 %collective-permute-start = (bf16[512,512]{1,0:T(8,128)(2,1)}, bf16[512,512]{1,0:T(8,128)(2,1)}, u32[]{:S(2)}, u32[]{:S(2)}) collective-permute-start(bf16[512,512]{1,0:T(8,128)(2,1)} %bitcast), channel_id=1, source_target_pairs={{8,16},{16,8},{9,17},{17,9},{10,18},{18,10},{11,19},{19,11},{12,20... | collective-permute-start | bytes 1572872 | tf_op jit(solution)/shard_map/ppermute | solution.py:273
  16.4 280.9 %reduce-scatter.4.cloned.1.call-start = ((), (), s32[]{:S(2)}) async-start(), calls=%async_computation.6 | async-start | bytes 2621440 | tf_op jit(solution)/shard_map/reduce_scatter | solution.py:556
  32.6 18.0 %collective-permute-start.1 = (bf16[512,512]{1,0:T(8,128)(2,1)}, bf16[512,512]{1,0:T(8,128)(2,1)S(1)}, u32[]{:S(2)}, u32[]{:S(2)}) collective-permute-start(bf16[512,512]{1,0:T(8,128)(2,1)} %collective-permute-done), channel_id=1, source_target_pairs={{0,8},{8,0},{16,24},{24,16},{1,9},{9,1},{17,25},{25,17},{2,10},{10... | collective-permute-start | bytes 1572872 | tf_op jit(solution)/shard_map/ppermute | solution.py:273
  37.5 22.8 %collective-permute-start.4 = (bf16[512,512]{1,0:T(8,128)(2,1)S(1)}, bf16[512,512]{1,0:T(8,128)(2,1)S(1)}, u32[]{:S(2)}, u32[]{:S(2)}) collective-permute-start(bf16[512,512]{1,0:T(8,128)(2,1)S(1)} %collective-permute-done.3), channel_id=1, source_target_pairs={{0,8},{8,0},{16,24},{24,16},{1,9},{9,1},{17,25},{25,17},{2,10},{10... | collective-permute-start | bytes 1572872 | tf_op jit(solution)/shard_map/ppermute | solution.py:273
  88.2 18.1 %collective-permute-start.9 = (bf16[512,512]{1,0:T(8,128)(2,1)S(1)}, bf16[512,512]{1,0:T(8,128)(2,1)S(1)}, u32[]{:S(2)}, u32[]{:S(2)}) collective-permute-start(bf16[512,512]{1,0:T(8,128)(2,1)S(1)} %bitcast.369), channel_id=1, source_target_pairs={{0,8},{8,0},{16,24},{24,16},{1,9},{9,1},{17,25},{25,17},{2,10},{10... | collective-permute-start | bytes 1572872 | tf_op jit(solution)/shard_map/ppermute | solution.py:273
  103.5 17.0 %collective-permute-start.11 = (bf16[512,512]{1,0:T(8,128)(2,1)S(1)}, bf16[512,512]{1,0:T(8,128)(2,1)S(1)}, u32[]{:S(2)}, u32[]{:S(2)}) collective-permute-start(bf16[512,512]{1,0:T(8,128)(2,1)S(1)} %collective-permute-done.10), channel_id=1, source_target_pairs={{0,8},{8,0},{16,24},{24,16},{1,9},{9,1},{17,25},{25,17},{2,10},{10... | collective-permute-start | bytes 1572872 | tf_op jit(solution)/shard_map/ppermute | solution.py:273
  106.3 14.2 %collective-permute-start.12 = (bf16[512,512]{1,0:T(8,128)(2,1)S(1)}, bf16[512,512]{1,0:T(8,128)(2,1)}, u32[]{:S(2)}, u32[]{:S(2)}) collective-permute-start(bf16[512,512]{1,0:T(8,128)(2,1)S(1)} %collective-permute-done.9), channel_id=1, source_target_pairs={{8,16},{16,8},{9,17},{17,9},{10,18},{18,10},{11,19},{19,11},{12,20... | collective-permute-start | bytes 1572872 | tf_op jit(solution)/shard_map/ppermute | solution.py:273
  127.8 13.9 %collective-permute-start.13 = (bf16[512,512]{1,0:T(8,128)(2,1)S(1)}, bf16[512,512]{1,0:T(8,128)(2,1)}, u32[]{:S(2)}, u32[]{:S(2)}) collective-permute-start(bf16[512,512]{1,0:T(8,128)(2,1)S(1)} %constant_dynamic-slice_fusion.34), channel_id=1, source_target_pairs={{0,8},{8,0},{16,24},{24,16},{1,9},{9,1},{17,25},{25,17},{2,10},{10... | collective-permute-start | bytes 1572872 | tf_op jit(solution)/shard_map/ppermute | solution.py:273
  144.9 13.4 %collective-permute-start.14 = (bf16[512,512]{1,0:T(8,128)(2,1)S(1)}, bf16[512,512]{1,0:T(8,128)(2,1)}, u32[]{:S(2)}, u32[]{:S(2)}) collective-permute-start(bf16[512,512]{1,0:T(8,128)(2,1)S(1)} %get-tuple-element.144), channel_id=1, source_target_pairs={{8,16},{16,8},{9,17},{17,9},{10,18},{18,10},{11,19},{19,11},{12,20... | collective-permute-start | bytes 1572872 | tf_op jit(solution)/shard_map/ppermute | solution.py:273
  159.6 15.5 %collective-permute-start.15 = (bf16[512,512]{1,0:T(8,128)(2,1)S(1)}, bf16[512,512]{1,0:T(8,128)(2,1)}, u32[]{:S(2)}, u32[]{:S(2)}) collective-permute-start(bf16[512,512]{1,0:T(8,128)(2,1)S(1)} %dynamic-slice_add_fusion.3), channel_id=1, source_target_pairs={{0,8},{8,0},{16,24},{24,16},{1,9},{9,1},{17,25},{25,17},{2,10},{10... | collective-permute-start | bytes 1572872 | tf_op jit(solution)/shard_map/ppermute | solution.py:273
  162.1 24.2 %collective-permute-start.23 = (bf16[512,512]{1,0:T(8,128)(2,1)}, bf16[512,512]{1,0:T(8,128)(2,1)}, u32[]{:S(2)}, u32[]{:S(2)}) collective-permute-start(bf16[512,512]{1,0:T(8,128)(2,1)} %collective-permute-done.12), channel_id=1, source_target_pairs={{0,8},{8,0},{16,24},{24,16},{1,9},{9,1},{17,25},{25,17},{2,10},{10... | collective-permute-start | bytes 1572872 | tf_op jit(solution)/shard_map/ppermute | solution.py:273
  177.8 15.8 %collective-permute-start.20 = (bf16[512,512]{1,0:T(8,128)(2,1)S(1)}, bf16[512,512]{1,0:T(8,128)(2,1)S(1)}, u32[]{:S(2)}, u32[]{:S(2)}) collective-permute-start(bf16[512,512]{1,0:T(8,128)(2,1)S(1)} %get-tuple-element.142), channel_id=1, source_target_pairs={{0,8},{8,0},{16,24},{24,16},{1,9},{9,1},{17,25},{25,17},{2,10},{10... | collective-permute-start | bytes 1572872 | tf_op jit(solution)/shard_map/ppermute | solution.py:273
  194.9 25.2 %collective-permute-start.19 = (bf16[512,512]{1,0:T(8,128)(2,1)S(1)}, bf16[512,512]{1,0:T(8,128)(2,1)S(1)}, u32[]{:S(2)}, u32[]{:S(2)}) collective-permute-start(bf16[512,512]{1,0:T(8,128)(2,1)S(1)} %collective-permute-done.18), channel_id=1, source_target_pairs={{0,8},{8,0},{16,24},{24,16},{1,9},{9,1},{17,25},{25,17},{2,10},{10... | collective-permute-start | bytes 1572872 | tf_op jit(solution)/shard_map/ppermute | solution.py:273
  206.7 17.9 %collective-permute-start.22 = (bf16[512,512]{1,0:T(8,128)(2,1)S(1)}, bf16[512,512]{1,0:T(8,128)(2,1)S(1)}, u32[]{:S(2)}, u32[]{:S(2)}) collective-permute-start(bf16[512,512]{1,0:T(8,128)(2,1)S(1)} %collective-permute-done.21), channel_id=1, source_target_pairs={{0,8},{8,0},{16,24},{24,16},{1,9},{9,1},{17,25},{25,17},{2,10},{10... | collective-permute-start | bytes 1572872 | tf_op jit(solution)/shard_map/ppermute | solution.py:273
  254.5 90.9 %all-gather.11.cloned.1.call-start = ((), (), s32[]{:S(2)}) async-start(), calls=%async_computation.7 | async-start | bytes 2621440 | tf_op jit(solution)/shard_map/all_gather | solution.py:571
  262.7 48.9 %collective-permute-start.26 = (bf16[1024,2816]{1,0:T(8,128)(2,1)}, bf16[1024,2816]{1,0:T(8,128)(2,1)}, u32[]{:S(2)}, u32[]{:S(2)}) collective-permute-start(bf16[1024,2816]{1,0:T(8,128)(2,1)} %convolution_convert_fusion), channel_id=1, source_target_pairs={{0,1},{1,0},{2,3},{3,2},{4,5},{5,4},{6,7},{7,6},{8,9},{9,8},{10,11... | collective-permute-start | bytes 17301512 | tf_op jit(solution)/shard_map/ppermute | solution.py:351
  267.9 35.1 %collective-permute-start.27 = (bf16[1024,1408]{1,0:T(8,128)(2,1)}, bf16[1024,1408]{1,0:T(8,128)(2,1)}, u32[]{:S(2)}, u32[]{:S(2)}) collective-permute-start(bf16[1024,1408]{1,0:T(8,128)(2,1)} %convolution_convert_fusion.2), channel_id=1, source_target_pairs={{0,1},{1,0},{2,3},{3,2},{4,5},{5,4},{6,7},{7,6},{8,9},{9,8},{10,11... | collective-permute-start | bytes 8650760 | tf_op jit(solution)/shard_map/ppermute | solution.py:351
  300.0 149.7 %reduce-scatter.6.cloned.1.call-start = ((), (), s32[]{:S(2)}) async-start(), calls=%async_computation.8 | async-start | bytes 10813440 | tf_op jit(solution)/shard_map/reduce_scatter | solution.py:378
  345.5 158.4 %reduce-scatter.8.cloned.1.call-start = ((), (), s32[]{:S(2)}) async-start(), calls=%async_computation.9 | async-start | bytes 2621440 | tf_op jit(solution)/shard_map/reduce_scatter | solution.py:602
  359.7 15.0 %collective-permute-start.28 = (bf16[512,512]{1,0:T(8,128)(2,1)S(1)}, bf16[512,512]{1,0:T(8,128)(2,1)S(1)}, u32[]{:S(2)}, u32[]{:S(2)}) collective-permute-start(bf16[512,512]{1,0:T(8,128)(2,1)S(1)} %get-tuple-element.183), channel_id=1, source_target_pairs={{0,8},{8,0},{16,24},{24,16},{1,9},{9,1},{17,25},{25,17},{2,10},{10... | collective-permute-start | bytes 1572872 | tf_op jit(solution)/shard_map/ppermute | solution.py:273
  359.8 25.5 %collective-permute-start.31 = (bf16[512,512]{1,0:T(8,128)(2,1)S(1)}, bf16[512,512]{1,0:T(8,128)(2,1)S(1)}, u32[]{:S(2)}, u32[]{:S(2)}) collective-permute-start(bf16[512,512]{1,0:T(8,128)(2,1)S(1)} %get-tuple-element.184), channel_id=1, source_target_pairs={{0,8},{8,0},{16,24},{24,16},{1,9},{9,1},{17,25},{25,17},{2,10},{10... | collective-permute-start | bytes 1572872 | tf_op jit(solution)/shard_map/ppermute | solution.py:273
  364.0 46.0 %collective-permute-start.36 = (bf16[1024,512]{1,0:T(8,128)(2,1)}, bf16[1024,512]{1,0:T(8,128)(2,1)S(1)}, u32[]{:S(2)}, u32[]{:S(2)}) collective-permute-start(bf16[1024,512]{1,0:T(8,128)(2,1)} %convolution_convert_fusion.6), channel_id=1, source_target_pairs={{0,1},{1,0},{2,3},{3,2},{4,5},{5,4},{6,7},{7,6},{8,9},{9,8},{10,11... | collective-permute-start | bytes 3145736 | tf_op jit(solution)/shard_map/ppermute | solution.py:351
  386.5 25.2 %collective-permute-start.32 = (bf16[512,512]{1,0:T(8,128)(2,1)S(1)}, bf16[512,512]{1,0:T(8,128)(2,1)S(1)}, u32[]{:S(2)}, u32[]{:S(2)}) collective-permute-start(bf16[512,512]{1,0:T(8,128)(2,1)S(1)} %get-tuple-element.182), channel_id=1, source_target_pairs={{8,16},{16,8},{9,17},{17,9},{10,18},{18,10},{11,19},{19,11},{12,20... | collective-permute-start | bytes 1572872 | tf_op jit(solution)/shard_map/ppermute | solution.py:273
  426.4 13.4 %collective-permute-start.38 = (bf16[1024,1536]{1,0:T(8,128)(2,1)}, bf16[1024,1536]{1,0:T(8,128)(2,1)}, u32[]{:S(2)}, u32[]{:S(2)}) collective-permute-start(bf16[1024,1536]{1,0:T(8,128)(2,1)} %convolution_convert_fusion.1), channel_id=1, source_target_pairs={{0,1},{1,0},{2,3},{3,2},{4,5},{5,4},{6,7},{7,6},{8,9},{9,8},{10,11... | collective-permute-start | bytes 9437192 | tf_op jit(solution)/shard_map/ppermute | solution.py:351
  431.9 75.9 %collective-permute-start.30 = (bf16[512,512]{1,0:T(8,128)(2,1)}, bf16[512,512]{1,0:T(8,128)(2,1)}, u32[]{:S(2)}, u32[]{:S(2)}) collective-permute-start(bf16[512,512]{1,0:T(8,128)(2,1)} %get-tuple-element.181), channel_id=1, source_target_pairs={{0,8},{8,0},{16,24},{24,16},{1,9},{9,1},{17,25},{25,17},{2,10},{10... | collective-permute-start | bytes 1572872 | tf_op jit(solution)/shard_map/ppermute | solution.py:273
  448.2 25.1 %collective-permute-start.46 = (bf16[2,128,2048]{2,1,0:T(8,128)(2,1)}, bf16[2,128,2048]{2,1,0:T(8,128)(2,1)}, u32[]{:S(2)}, u32[]{:S(2)}) collective-permute-start(bf16[2,128,2048]{2,1,0:T(8,128)(2,1)} %dynamic-slice_bitcast_fusion), channel_id=1, source_target_pairs={{0,4},{1,5},{2,6},{3,7},{4,0},{5,1},{6,2},{7,3},{8,12},{9,13},{10,... | collective-permute-start | bytes 3145736 | tf_op jit(solution)/shard_map/ppermute | solution.py:351
  452.2 29.2 %collective-permute-start.44 = (bf16[2,128,2048]{2,1,0:T(8,128)(2,1)}, bf16[2,128,2048]{2,1,0:T(8,128)(2,1)}, u32[]{:S(2)}, u32[]{:S(2)}) collective-permute-start(bf16[2,128,2048]{2,1,0:T(8,128)(2,1)} %dynamic-slice_bitcast_fusion.1), channel_id=1, source_target_pairs={{0,2},{1,3},{2,0},{3,1},{4,6},{5,7},{6,4},{7,5},{8,10},{9,11},{10,... | collective-permute-start | bytes 3145736 | tf_op jit(solution)/shard_map/ppermute | solution.py:351
  460.3 20.5 %collective-permute-start.39 = (f32[82,512]{1,0:T(8,128)S(1)}, f32[82,512]{1,0:T(8,128)S(1)}, u32[]{:S(2)}, u32[]{:S(2)}) collective-permute-start(f32[82,512]{1,0:T(8,128)S(1)} %concatenate.94), channel_id=1, source_target_pairs={{0,2},{1,3},{2,0},{3,1},{4,6},{5,7},{6,4},{7,5},{8,10},{9,11},{10,... | collective-permute-start | bytes 503816 | tf_op jit(solution)/shard_map/ppermute | solution.py:351
  (121 other events, 874.8 us)
Sparse Core Ops, SparseCore 0:
  10.5 48.2 all-gather.4
  61.2 56.4 all-gather.6
  120.2 67.6 all-gather.8
  254.7 42.6 reduce-scatter.3
  300.1 45.2 all-gather.10
  348.7 90.2 reduce-scatter.5
  449.9 43.6 reduce-scatter.7

commit v6 on v5

--- a/solution.py
+++ b/solution.py
@@ -15,7 +15,7 @@
 
 
 lane_block = 128
-step = 16
+step = 32
 
 
 def times(a_re, a_im, b_re, b_im):
@@ -548,10 +548,11 @@
 
     d_gate = d_hidden * up_pre * sigmoid * (1.0 + gate_pre * (1.0 - sigmoid))
     d_up = d_hidden * activated
-    d_feed = jnp.concatenate([d_gate.astype(bf16), d_up.astype(bf16)], axis=1)
+    d_gate_low, d_up_low = d_gate.astype(bf16), d_up.astype(bf16)
     along_two = jnp.sum(d_gate * gate_pre + d_up * up_pre, axis=-1)
     along_two = sum_line(along_two.reshape(-1, 128))
-    part_two = dot_rows(d_feed, w_feed).astype(bf16)
+    part_two = (dot_rows(d_gate_low, w_feed[:, :units]) + dot_rows(d_up_low, w_feed[:, units:])).astype(bf16)
+    d_feed = jnp.concatenate(lax.optimization_barrier((d_gate_low, d_up_low, part_two))[:2], axis=1)
     along_two = along_two.reshape(tokens, 1)
     dn_two = lax.psum_scatter(part_two, "fsdp", scatter_dimension=1, tiled=True)
     feed_got = swap_seq(core_give(normed_two, after(d_feed, part_two)), 0)

time: 539 us -> 537 us (level)
    unnamed x201 -> x206, local copies, waits for them, and re-layouts: 14.6 us -> 17.2 us
    dot_general x4 -> x5, matrix products: 19.7 us -> 20.4 us  [dot_rows(): lax.dot_general(left, right, (((1,), (1,)), ((), ())), preferred_element_...]
  transfers between devices with their start and end apart: 55 -> 55, of which waited for: 25 -> 25; matrix products, arithmetic and copies ran while one was open for 31% -> 31% of each run, Pallas kernels for 9% -> 8%
where the time goes in v6:
time: 537 us; the launch traced here: 527 us
  waiting for transfers between devices  162 us (30%)
  starting transfers between devices  102 us (19%)
  other arithmetic  86.4 us (16%)
  matrix products  77.4 us (14%)
  Pallas kernels  44.4 us (8%)
  local copies, waits for them, and re-layouts  38.3 us (7%)
  between operations  16.4 us (3%)
    ppermute x29, starting transfers between devices, along_line(): return lax.ppermute(array, 'fsdp', pairs)  78 us
    ppermute x29, waiting for transfers between devices, along_line(): return lax.ppermute(array, 'fsdp', pairs)  71.3 us
    ppermute x17, waiting for transfers between devices, swap_seq(): lax.ppermute(array, 'seq', [(i, i ^ 1 << bit) for i in range(lax.axis_siz...  43 us
    dot_general x8, matrix products, dot_tokens(): lax.dot_general(left, right, (((0,), (0,)), ((), ())), preferred_element_...  29.2 us
    dot_general x4, matrix products, dot(): return jnp.dot(left, right, preferred_element_type=f32)  27.9 us
    all_gather x1, waiting for transfers between devices, on_device(): d_mix = lax.all_gather(d_share, 'fsdp', axis=1, tiled=True)  25.5 us
    pallas_call x1, Pallas kernels, long_conv_back(): pl.pallas_call(functools.partial(back_kernel, batches), out_shape=(jax.Sh...  22.4 us
    reduce_scatter x1, waiting for transfers between devices, on_device(): dn_two = lax.psum_scatter(part_two, 'fsdp', scatter_dimension=1, tiled=True)  20.4 us
  transfers between devices with their start and end apart: 55, of which 25 were waited for; matrix products, arithmetic and copies ran while one was open for 31% of the time, Pallas kernels for 8%

profile of v6, /device:TPU:0, one launch (start us, length us, event | category | flops | bytes accessed | tf_op | source)
XLA Modules:
  0.0 526.7 jit_solution(2304420579374130150)
XLA Ops:
  32.6 4.9 collective-permute-start.1
  37.5 9.5 %collective-permute-start.4 = (bf16[512,512]{1,0:T(8,128)(2,1)S(1)}, bf16[512,512]{1,0:T(8,128)(2,1)S(1)}, u32[]{:S(2)}, u32[]{:S(2)}) collective-permute-start(bf16[512,512]{1,0:T(8,128)(2,1)S(1)} %collective-permute-done.3), channel_id=1, source_target_pairs={{0,8},{8,0},{16,24},{24,16},{1,9},{9,1},{17,25},{25,17},{2,10},{10... | collective-permute-start | bytes 1572872 | tf_op jit(solution)/shard_map/ppermute | solution.py:273
  50.5 9.8 %collective-permute-done.4 = bf16[512,512]{1,0:T(8,128)(2,1)S(1)} collective-permute-done((bf16[512,512]{1,0:T(8,128)(2,1)S(1)}, bf16[512,512]{1,0:T(8,128)(2,1)S(1)}, u32[]{:S(2)}, u32[]{:S(2)}) %collective-permute-start.4) | collective-permute-done | bytes 524320 | tf_op jit(solution)/shard_map/ppermute | solution.py:273
  66.6 6.9 %fusion.72 = f32[512,1536]{1,0:T(8,128)S(1)} fusion(bf16[512,2048]{1,0:T(8,128)(2,1)} %fusion.14, bf16[2048,1536]{1,0:T(8,128)(2,1)} %all-gather.5.cloned.1.call-done), kind=kOutput, calls=%fused_computation.369 | convolution fusion | flops 3221225472 | bytes 11534336 | tf_op jit(solution)/shard_map/dot_general | solution.py:269
  79.1 6.1 %shard_map.271 = f32[2,2,2,8,512]{4,3,2,1,0:T(8,128)S(1)} custom-call(f32[2,256]{1,0:T(2,128)S(1)} %get-tuple-element.289.keep_ref, bf16[512,512]{1,0:T(8,128)(2,1)S(1)} %multiply_convert_fusion.3.u_ref, f32[4,2,8,512]{3,2,1,0:T(8,128)S(1)} %pad_maximum_fusion.18.par_ref), custom_call_target="tpu_custom_call" | custom-call | tf_op jit(solution)/shard_map/pallas_call | solution.py:210
  93.2 6.9 %collective-permute-done.7 = f32[2,2,2,8,512]{4,3,2,0,1:T(8,128)S(1)} collective-permute-done((f32[2,2,2,8,512]{4,3,2,0,1:T(8,128)S(1)}, f32[2,2,2,8,512]{4,3,2,0,1:T(8,128)S(1)}, u32[]{:S(2)}, u32[]{:S(2)}) %collective-permute-start.7) | collective-permute-done | bytes 131104 | tf_op jit(solution)/shard_map/ppermute | solution.py:351
  109.9 9.9 %shard_map.272 = bf16[512,512]{1,0:T(8,128)(2,1)S(1)} custom-call(f32[2,256]{1,0:T(2,128)S(1)} %get-tuple-element.289.keep_ref, bf16[512,512]{1,0:T(8,128)(2,1)S(1)} %multiply_convert_fusion.3.u_ref, f32[2,2,2,8,512]{4,3,2,1,0:T(8,128)S(1)} %copy.52.into_ref, f32[4,2,8,512]{3,2,1,0:T(8,128)S(1)} %pad_maximum_fusion.18.par_ref, f32[1,512]{1,0:T(1,128)S(1)} %bitcast.359), custom_call_target="tpu_custom_call" | custom-call | tf_op jit(solution)/shard_map/pallas_call | solution.py:221
  129.9 11.1 %collective-permute-done.13 = bf16[512,512]{1,0:T(8,128)(2,1)} collective-permute-done((bf16[512,512]{1,0:T(8,128)(2,1)S(1)}, bf16[512,512]{1,0:T(8,128)(2,1)}, u32[]{:S(2)}, u32[]{:S(2)}) %collective-permute-start.13) | collective-permute-done | bytes 524320 | tf_op jit(solution)/shard_map/ppermute | solution.py:273
  145.6 9.0 %collective-permute-done.16 = bf16[512,512]{1,0:T(8,128)(2,1)} collective-permute-done((bf16[512,512]{1,0:T(8,128)(2,1)S(1)}, bf16[512,512]{1,0:T(8,128)(2,1)}, u32[]{:S(2)}, u32[]{:S(2)}) %collective-permute-start.16) | collective-permute-done | bytes 524320 | tf_op jit(solution)/shard_map/ppermute | solution.py:273
  161.8 12.9 %collective-permute-done.15 = bf16[512,512]{1,0:T(8,128)(2,1)} collective-permute-done((bf16[512,512]{1,0:T(8,128)(2,1)S(1)}, bf16[512,512]{1,0:T(8,128)(2,1)}, u32[]{:S(2)}, u32[]{:S(2)}) %collective-permute-start.15) | collective-permute-done | bytes 524320 | tf_op jit(solution)/shard_map/ppermute | solution.py:273
  179.4 6.4 %collective-permute-done.23 = bf16[512,512]{1,0:T(8,128)(2,1)} collective-permute-done((bf16[512,512]{1,0:T(8,128)(2,1)}, bf16[512,512]{1,0:T(8,128)(2,1)}, u32[]{:S(2)}, u32[]{:S(2)}) %collective-permute-start.23) | collective-permute-done | bytes 524320 | tf_op jit(solution)/shard_map/ppermute | solution.py:273
  193.9 11.9 %collective-permute-start.19 = (bf16[512,512]{1,0:T(8,128)(2,1)S(1)}, bf16[512,512]{1,0:T(8,128)(2,1)S(1)}, u32[]{:S(2)}, u32[]{:S(2)}) collective-permute-start(bf16[512,512]{1,0:T(8,128)(2,1)S(1)} %collective-permute-done.18), channel_id=1, source_target_pairs={{0,8},{8,0},{16,24},{24,16},{1,9},{9,1},{17,25},{25,17},{2,10},{10... | collective-permute-start | bytes 1572872 | tf_op jit(solution)/shard_map/ppermute | solution.py:273
  205.8 5.6 %collective-permute-start.22 = (bf16[512,512]{1,0:T(8,128)(2,1)S(1)}, bf16[512,512]{1,0:T(8,128)(2,1)S(1)}, u32[]{:S(2)}, u32[]{:S(2)}) collective-permute-start(bf16[512,512]{1,0:T(8,128)(2,1)S(1)} %collective-permute-done.21), channel_id=1, source_target_pairs={{0,8},{8,0},{16,24},{24,16},{1,9},{9,1},{17,25},{25,17},{2,10},{10... | collective-permute-start | bytes 1572872 | tf_op jit(solution)/shard_map/ppermute | solution.py:273
  211.4 7.7 %fusion.6 = f32[512,1408]{1,0:T(8,128)} fusion(bf16[512,2048]{1,0:T(8,128)(2,1)S(1)} %pad_maximum_fusion.6, bf16[2048,1920]{0,1:T(8,128)(2,1)} %all-gather.7.cloned.1.call-done), kind=kOutput, calls=%fused_computation.15 | convolution fusion | flops 2952790016 | bytes 10747904 | tf_op jit(solution)/shard_map/dot_general | solution.py:269
  229.0 10.3 %fusion.73 = f32[512,2816]{1,0:T(8,128)S(1)} fusion(bf16[512,2048]{1,0:T(8,128)(2,1)} %copy-done.15, bf16[2048,2816]{1,0:T(8,128)(2,1)} %all-gather.9.cloned.1.call-done), kind=kOutput, calls=%fused_computation.370 | convolution fusion | flops 5905580032 | bytes 19398656 | tf_op jit(solution)/shard_map/dot_general | solution.py:269
  247.6 4.7 add_convert_fusion.3
  254.7 5.1 convolution_convert_fusion
  275.3 20.4 %reduce-scatter.4.cloned.1.call-done = bf16[512,512]{1,0:T(8,128)(2,1)} async-done(((bf16[512,2048]{1,0:T(8,128)(2,1)}), bf16[512,512]{1,0:T(8,128)(2,1)}) %reduce-scatter.4.cloned.1.call-update) | async-done | bytes 524304 | tf_op jit(solution)/shard_map/reduce_scatter | solution.py:557
  300.0 4.5 add_convert_fusion.2
  304.6 4.6 fusion.22
  309.2 5.4 %add_convert_fusion = bf16[1024,2816]{1,0:T(8,128)(2,1)S(1)} fusion(bf16[1024,2816]{1,0:T(8,128)(2,1)} %collective-permute-done.26, bf16[512,1024]{1,0:T(8,128)(2,1)S(1)} %pad_maximum_fusion.8, bf16[512,2816]{1,0:T(8,128)(2,1)S(1)} %copy-done.42), kind=kOutput, calls=%fused_computation | convolution fusion | flops 2961440768 | bytes 15466496 | tf_op jit(solution)/shard_map/dot_general | solution.py:265
  318.4 25.5 %all-gather.11.cloned.1.call-done = bf16[512,2048]{1,0:T(8,128)(2,1)} async-done(((bf16[512,512]{1,0:T(8,128)(2,1)}), bf16[512,2048]{1,0:T(8,128)(2,1)}) %all-gather.11.cloned.1.call-update) | async-done | bytes 2097168 | tf_op jit(solution)/shard_map/all_gather | solution.py:572
  351.6 6.1 %shard_map.273 = f32[2,2,2,8,512]{4,3,2,1,0:T(8,128)S(1)} custom-call(f32[2,256]{1,0:T(2,128)S(1)} %get-tuple-element.289.keep_ref, bf16[512,512]{1,0:T(8,128)(2,1)S(1)} %get-tuple-element.225.u_ref.g_ref, f32[4,2,8,512]{3,2,1,0:T(8,128)S(1)} %pad_maximum_fusion.18.par_ref), custom_call_target="tpu_custom_call" | custom-call | tf_op jit(solution)/shard_map/pallas_call | solution.py:210
  365.4 7.5 %collective-permute-done.34 = f32[2,2,2,8,512]{4,3,2,0,1:T(8,128)S(1)} collective-permute-done((f32[2,2,2,8,512]{4,3,2,0,1:T(8,128)S(1)}, f32[2,2,2,8,512]{4,3,2,0,1:T(8,128)S(1)}, u32[]{:S(2)}, u32[]{:S(2)}) %collective-permute-start.34) | collective-permute-done | bytes 131104 | tf_op jit(solution)/shard_map/ppermute | solution.py:351
  375.4 8.1 %collective-permute-done.31 = bf16[512,512]{1,0:T(8,128)(2,1)S(1)} collective-permute-done((bf16[512,512]{1,0:T(8,128)(2,1)S(1)}, bf16[512,512]{1,0:T(8,128)(2,1)S(1)}, u32[]{:S(2)}, u32[]{:S(2)}) %collective-permute-start.31) | collective-permute-done | bytes 524320 | tf_op jit(solution)/shard_map/ppermute | solution.py:273
  385.5 22.4 %shard_map.274 = (bf16[512,512]{1,0:T(8,128)(2,1)S(1)}, f32[4,2,8,512]{3,2,1,0:T(8,128)S(1)}, f32[1,512]{1,0:T(1,128)S(1)}) custom-call(f32[2,256]{1,0:T(2,128)S(1)} %get-tuple-element.289.keep_ref, bf16[512,512]{1,0:T(8,128)(2,1)S(1)} %multiply_convert_fusion.3.u_ref, bf16[512,512]{1,0:T(8,128)(2,1)S(1)} %get-tuple-element.225.u_ref.g_ref, ...), custom_call_target="tpu_custom_call" | custom-call | tf_op jit(solution)/shard_map/pallas_call | solution.py:233
  416.0 4.8 convolution_convert_fusion.3
  429.7 7.9 %collective-permute-start.30 = (bf16[512,512]{1,0:T(8,128)(2,1)}, bf16[512,512]{1,0:T(8,128)(2,1)}, u32[]{:S(2)}, u32[]{:S(2)}) collective-permute-start(bf16[512,512]{1,0:T(8,128)(2,1)} %get-tuple-element.185), channel_id=1, source_target_pairs={{0,8},{8,0},{16,24},{24,16},{1,9},{9,1},{17,25},{25,17},{2,10},{10... | collective-permute-start | bytes 1572872 | tf_op jit(solution)/shard_map/ppermute | solution.py:273
  450.9 6.8 %multiply_reduce_fusion.2 = (f32[1536]{0:T(1024)S(1)}, f32[1536]{0:T(1024)S(1)}, f32[1536]{0:T(1024)S(1)}) fusion(f32[2,256,1536]{2,1,0:T(8,128)} %bitcast.369, f32[2,256]{1,0:T(2,128)S(1)} %copy-done.78, f32[2,256,1536]{2,1,0:T(8,128)} %bitcast.363, f32[2,2,1536]{2,1,0:T(2,128)S(1)} %copy-done.64, f32[2,256]{1,0:T(2,128)S(1)} %copy-done.82, ...), kind=kLoop, calls=%fused_computation.41 | loop fusion | flops 8646144 | bytes 9486336 | tf_op jit(solution)/shard_map/reduce_sum | solution.py:609
  460.3 10.9 %collective-permute-done.46 = bf16[2,128,2048]{2,1,0:T(8,128)(2,1)} collective-permute-done((bf16[2,128,2048]{2,1,0:T(8,128)(2,1)}, bf16[2,128,2048]{2,1,0:T(8,128)(2,1)}, u32[]{:S(2)}, u32[]{:S(2)}) %collective-permute-start.46) | collective-permute-done | bytes 1048608 | tf_op jit(solution)/shard_map/ppermute | solution.py:351
  474.2 4.4 collective-permute-done.39
  509.2 6.3 %collective-permute-done.47 = bf16[128,2048]{1,0:T(8,128)(2,1)S(1)} collective-permute-done((bf16[128,2048]{1,0:T(8,128)(2,1)S(1)}, bf16[128,2048]{1,0:T(8,128)(2,1)S(1)}, u32[]{:S(2)}, u32[]{:S(2)}) %collective-permute-start.47) | collective-permute-done | bytes 524320 | tf_op jit(solution)/shard_map/ppermute | solution.py:351
  (489 shorter events, 226.2 us)
Async XLA Ops:
  7.2 59.4 %all-gather.5.cloned.1.call-start = ((), (), s32[]{:S(2)}) async-start(), calls=%async_computation.3 | async-start | bytes 7077888 | tf_op jit(solution)/shard_map/all_gather | solution.py:355
  9.5 112.6 %all-gather.7.cloned.1.call-start = ((), (), s32[]{:S(2)}) async-start(), calls=%async_computation.4 | async-start | bytes 8847360 | tf_op jit(solution)/shard_map/all_gather | solution.py:355
  10.6 218.4 %all-gather.9.cloned.1.call-start = ((), (), s32[]{:S(2)}) async-start(), calls=%async_computation.5 | async-start | bytes 12976128 | tf_op jit(solution)/shard_map/all_gather | solution.py:355
  10.6 17.5 %collective-permute-start.2 = (bf16[512,512]{1,0:T(8,128)(2,1)}, bf16[512,512]{1,0:T(8,128)(2,1)}, u32[]{:S(2)}, u32[]{:S(2)}) collective-permute-start(bf16[512,512]{1,0:T(8,128)(2,1)} %bitcast), channel_id=1, source_target_pairs={{0,8},{8,0},{16,24},{24,16},{1,9},{9,1},{17,25},{25,17},{2,10},{10... | collective-permute-start | bytes 1572872 | tf_op jit(solution)/shard_map/ppermute | solution.py:273
  13.7 18.8 %collective-permute-start = (bf16[512,512]{1,0:T(8,128)(2,1)}, bf16[512,512]{1,0:T(8,128)(2,1)}, u32[]{:S(2)}, u32[]{:S(2)}) collective-permute-start(bf16[512,512]{1,0:T(8,128)(2,1)} %bitcast), channel_id=1, source_target_pairs={{8,16},{16,8},{9,17},{17,9},{10,18},{18,10},{11,19},{19,11},{12,20... | collective-permute-start | bytes 1572872 | tf_op jit(solution)/shard_map/ppermute | solution.py:273
  16.4 279.4 %reduce-scatter.4.cloned.1.call-start = ((), (), s32[]{:S(2)}) async-start(), calls=%async_computation.6 | async-start | bytes 2621440 | tf_op jit(solution)/shard_map/reduce_scatter | solution.py:557
  32.6 18.0 %collective-permute-start.1 = (bf16[512,512]{1,0:T(8,128)(2,1)}, bf16[512,512]{1,0:T(8,128)(2,1)S(1)}, u32[]{:S(2)}, u32[]{:S(2)}) collective-permute-start(bf16[512,512]{1,0:T(8,128)(2,1)} %collective-permute-done), channel_id=1, source_target_pairs={{0,8},{8,0},{16,24},{24,16},{1,9},{9,1},{17,25},{25,17},{2,10},{10... | collective-permute-start | bytes 1572872 | tf_op jit(solution)/shard_map/ppermute | solution.py:273
  37.5 22.8 %collective-permute-start.4 = (bf16[512,512]{1,0:T(8,128)(2,1)S(1)}, bf16[512,512]{1,0:T(8,128)(2,1)S(1)}, u32[]{:S(2)}, u32[]{:S(2)}) collective-permute-start(bf16[512,512]{1,0:T(8,128)(2,1)S(1)} %collective-permute-done.3), channel_id=1, source_target_pairs={{0,8},{8,0},{16,24},{24,16},{1,9},{9,1},{17,25},{25,17},{2,10},{10... | collective-permute-start | bytes 1572872 | tf_op jit(solution)/shard_map/ppermute | solution.py:273
  87.8 18.1 %collective-permute-start.9 = (bf16[512,512]{1,0:T(8,128)(2,1)S(1)}, bf16[512,512]{1,0:T(8,128)(2,1)S(1)}, u32[]{:S(2)}, u32[]{:S(2)}) collective-permute-start(bf16[512,512]{1,0:T(8,128)(2,1)S(1)} %bitcast.371), channel_id=1, source_target_pairs={{0,8},{8,0},{16,24},{24,16},{1,9},{9,1},{17,25},{25,17},{2,10},{10... | collective-permute-start | bytes 1572872 | tf_op jit(solution)/shard_map/ppermute | solution.py:273
  103.2 16.7 %collective-permute-start.11 = (bf16[512,512]{1,0:T(8,128)(2,1)S(1)}, bf16[512,512]{1,0:T(8,128)(2,1)S(1)}, u32[]{:S(2)}, u32[]{:S(2)}) collective-permute-start(bf16[512,512]{1,0:T(8,128)(2,1)S(1)} %collective-permute-done.10), channel_id=1, source_target_pairs={{0,8},{8,0},{16,24},{24,16},{1,9},{9,1},{17,25},{25,17},{2,10},{10... | collective-permute-start | bytes 1572872 | tf_op jit(solution)/shard_map/ppermute | solution.py:273
  106.0 13.9 %collective-permute-start.12 = (bf16[512,512]{1,0:T(8,128)(2,1)S(1)}, bf16[512,512]{1,0:T(8,128)(2,1)}, u32[]{:S(2)}, u32[]{:S(2)}) collective-permute-start(bf16[512,512]{1,0:T(8,128)(2,1)S(1)} %collective-permute-done.9), channel_id=1, source_target_pairs={{8,16},{16,8},{9,17},{17,9},{10,18},{18,10},{11,19},{19,11},{12,20... | collective-permute-start | bytes 1572872 | tf_op jit(solution)/shard_map/ppermute | solution.py:273
  127.1 13.9 %collective-permute-start.13 = (bf16[512,512]{1,0:T(8,128)(2,1)S(1)}, bf16[512,512]{1,0:T(8,128)(2,1)}, u32[]{:S(2)}, u32[]{:S(2)}) collective-permute-start(bf16[512,512]{1,0:T(8,128)(2,1)S(1)} %constant_dynamic-slice_fusion.34), channel_id=1, source_target_pairs={{0,8},{8,0},{16,24},{24,16},{1,9},{9,1},{17,25},{25,17},{2,10},{10... | collective-permute-start | bytes 1572872 | tf_op jit(solution)/shard_map/ppermute | solution.py:273
  144.2 13.4 %collective-permute-start.14 = (bf16[512,512]{1,0:T(8,128)(2,1)S(1)}, bf16[512,512]{1,0:T(8,128)(2,1)}, u32[]{:S(2)}, u32[]{:S(2)}) collective-permute-start(bf16[512,512]{1,0:T(8,128)(2,1)S(1)} %get-tuple-element.148), channel_id=1, source_target_pairs={{8,16},{16,8},{9,17},{17,9},{10,18},{18,10},{11,19},{19,11},{12,20... | collective-permute-start | bytes 1572872 | tf_op jit(solution)/shard_map/ppermute | solution.py:273
  158.9 15.7 %collective-permute-start.15 = (bf16[512,512]{1,0:T(8,128)(2,1)S(1)}, bf16[512,512]{1,0:T(8,128)(2,1)}, u32[]{:S(2)}, u32[]{:S(2)}) collective-permute-start(bf16[512,512]{1,0:T(8,128)(2,1)S(1)} %dynamic-slice_add_fusion.3), channel_id=1, source_target_pairs={{0,8},{8,0},{16,24},{24,16},{1,9},{9,1},{17,25},{25,17},{2,10},{10... | collective-permute-start | bytes 1572872 | tf_op jit(solution)/shard_map/ppermute | solution.py:273
  161.7 24.2 %collective-permute-start.23 = (bf16[512,512]{1,0:T(8,128)(2,1)}, bf16[512,512]{1,0:T(8,128)(2,1)}, u32[]{:S(2)}, u32[]{:S(2)}) collective-permute-start(bf16[512,512]{1,0:T(8,128)(2,1)} %collective-permute-done.12), channel_id=1, source_target_pairs={{0,8},{8,0},{16,24},{24,16},{1,9},{9,1},{17,25},{25,17},{2,10},{10... | collective-permute-start | bytes 1572872 | tf_op jit(solution)/shard_map/ppermute | solution.py:273
  177.5 15.2 %collective-permute-start.20 = (bf16[512,512]{1,0:T(8,128)(2,1)S(1)}, bf16[512,512]{1,0:T(8,128)(2,1)S(1)}, u32[]{:S(2)}, u32[]{:S(2)}) collective-permute-start(bf16[512,512]{1,0:T(8,128)(2,1)S(1)} %get-tuple-element.146), channel_id=1, source_target_pairs={{0,8},{8,0},{16,24},{24,16},{1,9},{9,1},{17,25},{25,17},{2,10},{10... | collective-permute-start | bytes 1572872 | tf_op jit(solution)/shard_map/ppermute | solution.py:273
  193.9 25.2 %collective-permute-start.19 = (bf16[512,512]{1,0:T(8,128)(2,1)S(1)}, bf16[512,512]{1,0:T(8,128)(2,1)S(1)}, u32[]{:S(2)}, u32[]{:S(2)}) collective-permute-start(bf16[512,512]{1,0:T(8,128)(2,1)S(1)} %collective-permute-done.18), channel_id=1, source_target_pairs={{0,8},{8,0},{16,24},{24,16},{1,9},{9,1},{17,25},{25,17},{2,10},{10... | collective-permute-start | bytes 1572872 | tf_op jit(solution)/shard_map/ppermute | solution.py:273
  205.8 17.4 %collective-permute-start.22 = (bf16[512,512]{1,0:T(8,128)(2,1)S(1)}, bf16[512,512]{1,0:T(8,128)(2,1)S(1)}, u32[]{:S(2)}, u32[]{:S(2)}) collective-permute-start(bf16[512,512]{1,0:T(8,128)(2,1)S(1)} %collective-permute-done.21), channel_id=1, source_target_pairs={{0,8},{8,0},{16,24},{24,16},{1,9},{9,1},{17,25},{25,17},{2,10},{10... | collective-permute-start | bytes 1572872 | tf_op jit(solution)/shard_map/ppermute | solution.py:273
  252.3 91.6 %all-gather.11.cloned.1.call-start = ((), (), s32[]{:S(2)}) async-start(), calls=%async_computation.7 | async-start | bytes 2621440 | tf_op jit(solution)/shard_map/all_gather | solution.py:572
  259.8 49.4 %collective-permute-start.26 = (bf16[1024,2816]{1,0:T(8,128)(2,1)}, bf16[1024,2816]{1,0:T(8,128)(2,1)}, u32[]{:S(2)}, u32[]{:S(2)}) collective-permute-start(bf16[1024,2816]{1,0:T(8,128)(2,1)} %convolution_convert_fusion), channel_id=1, source_target_pairs={{0,1},{1,0},{2,3},{3,2},{4,5},{5,4},{6,7},{7,6},{8,9},{9,8},{10,11... | collective-permute-start | bytes 17301512 | tf_op jit(solution)/shard_map/ppermute | solution.py:351
  264.6 35.4 %collective-permute-start.27 = (bf16[1024,1408]{1,0:T(8,128)(2,1)}, bf16[1024,1408]{1,0:T(8,128)(2,1)}, u32[]{:S(2)}, u32[]{:S(2)}) collective-permute-start(bf16[1024,1408]{1,0:T(8,128)(2,1)} %convolution_convert_fusion.2), channel_id=1, source_target_pairs={{0,1},{1,0},{2,3},{3,2},{4,5},{5,4},{6,7},{7,6},{8,9},{9,8},{10,11... | collective-permute-start | bytes 8650760 | tf_op jit(solution)/shard_map/ppermute | solution.py:351
  298.4 149.1 %reduce-scatter.6.cloned.1.call-start = ((), (), s32[]{:S(2)}) async-start(), calls=%async_computation.8 | async-start | bytes 10813440 | tf_op jit(solution)/shard_map/reduce_scatter | solution.py:378
  343.9 157.8 %reduce-scatter.8.cloned.1.call-start = ((), (), s32[]{:S(2)}) async-start(), calls=%async_computation.9 | async-start | bytes 2621440 | tf_op jit(solution)/shard_map/reduce_scatter | solution.py:603
  357.9 15.0 %collective-permute-start.28 = (bf16[512,512]{1,0:T(8,128)(2,1)S(1)}, bf16[512,512]{1,0:T(8,128)(2,1)S(1)}, u32[]{:S(2)}, u32[]{:S(2)}) collective-permute-start(bf16[512,512]{1,0:T(8,128)(2,1)S(1)} %get-tuple-element.187), channel_id=1, source_target_pairs={{0,8},{8,0},{16,24},{24,16},{1,9},{9,1},{17,25},{25,17},{2,10},{10... | collective-permute-start | bytes 1572872 | tf_op jit(solution)/shard_map/ppermute | solution.py:273
  358.0 25.5 %collective-permute-start.31 = (bf16[512,512]{1,0:T(8,128)(2,1)S(1)}, bf16[512,512]{1,0:T(8,128)(2,1)S(1)}, u32[]{:S(2)}, u32[]{:S(2)}) collective-permute-start(bf16[512,512]{1,0:T(8,128)(2,1)S(1)} %get-tuple-element.188), channel_id=1, source_target_pairs={{0,8},{8,0},{16,24},{24,16},{1,9},{9,1},{17,25},{25,17},{2,10},{10... | collective-permute-start | bytes 1572872 | tf_op jit(solution)/shard_map/ppermute | solution.py:273
  362.2 45.7 %collective-permute-start.36 = (bf16[1024,512]{1,0:T(8,128)(2,1)}, bf16[1024,512]{1,0:T(8,128)(2,1)S(1)}, u32[]{:S(2)}, u32[]{:S(2)}) collective-permute-start(bf16[1024,512]{1,0:T(8,128)(2,1)} %convolution_convert_fusion.5), channel_id=1, source_target_pairs={{0,1},{1,0},{2,3},{3,2},{4,5},{5,4},{6,7},{7,6},{8,9},{9,8},{10,11... | collective-permute-start | bytes 3145736 | tf_op jit(solution)/shard_map/ppermute | solution.py:351
  384.7 24.9 %collective-permute-start.32 = (bf16[512,512]{1,0:T(8,128)(2,1)S(1)}, bf16[512,512]{1,0:T(8,128)(2,1)S(1)}, u32[]{:S(2)}, u32[]{:S(2)}) collective-permute-start(bf16[512,512]{1,0:T(8,128)(2,1)S(1)} %get-tuple-element.186), channel_id=1, source_target_pairs={{8,16},{16,8},{9,17},{17,9},{10,18},{18,10},{11,19},{19,11},{12,20... | collective-permute-start | bytes 1572872 | tf_op jit(solution)/shard_map/ppermute | solution.py:273
  424.3 13.4 %collective-permute-start.38 = (bf16[1024,1536]{1,0:T(8,128)(2,1)}, bf16[1024,1536]{1,0:T(8,128)(2,1)}, u32[]{:S(2)}, u32[]{:S(2)}) collective-permute-start(bf16[1024,1536]{1,0:T(8,128)(2,1)} %convolution_convert_fusion.1), channel_id=1, source_target_pairs={{0,1},{1,0},{2,3},{3,2},{4,5},{5,4},{6,7},{7,6},{8,9},{9,8},{10,11... | collective-permute-start | bytes 9437192 | tf_op jit(solution)/shard_map/ppermute | solution.py:351
  429.7 75.9 %collective-permute-start.30 = (bf16[512,512]{1,0:T(8,128)(2,1)}, bf16[512,512]{1,0:T(8,128)(2,1)}, u32[]{:S(2)}, u32[]{:S(2)}) collective-permute-start(bf16[512,512]{1,0:T(8,128)(2,1)} %get-tuple-element.185), channel_id=1, source_target_pairs={{0,8},{8,0},{16,24},{24,16},{1,9},{9,1},{17,25},{25,17},{2,10},{10... | collective-permute-start | bytes 1572872 | tf_op jit(solution)/shard_map/ppermute | solution.py:273
  446.1 25.1 %collective-permute-start.46 = (bf16[2,128,2048]{2,1,0:T(8,128)(2,1)}, bf16[2,128,2048]{2,1,0:T(8,128)(2,1)}, u32[]{:S(2)}, u32[]{:S(2)}) collective-permute-start(bf16[2,128,2048]{2,1,0:T(8,128)(2,1)} %dynamic-slice_bitcast_fusion), channel_id=1, source_target_pairs={{0,4},{1,5},{2,6},{3,7},{4,0},{5,1},{6,2},{7,3},{8,12},{9,13},{10,... | collective-permute-start | bytes 3145736 | tf_op jit(solution)/shard_map/ppermute | solution.py:351
  450.1 29.2 %collective-permute-start.44 = (bf16[2,128,2048]{2,1,0:T(8,128)(2,1)}, bf16[2,128,2048]{2,1,0:T(8,128)(2,1)}, u32[]{:S(2)}, u32[]{:S(2)}) collective-permute-start(bf16[2,128,2048]{2,1,0:T(8,128)(2,1)} %dynamic-slice_bitcast_fusion.1), channel_id=1, source_target_pairs={{0,2},{1,3},{2,0},{3,1},{4,6},{5,7},{6,4},{7,5},{8,10},{9,11},{10,... | collective-permute-start | bytes 3145736 | tf_op jit(solution)/shard_map/ppermute | solution.py:351
  458.2 20.4 %collective-permute-start.39 = (f32[82,512]{1,0:T(8,128)S(1)}, f32[82,512]{1,0:T(8,128)S(1)}, u32[]{:S(2)}, u32[]{:S(2)}) collective-permute-start(f32[82,512]{1,0:T(8,128)S(1)} %concatenate.94), channel_id=1, source_target_pairs={{0,2},{1,3},{2,0},{3,1},{4,6},{5,7},{6,4},{7,5},{8,10},{9,11},{10,... | collective-permute-start | bytes 503816 | tf_op jit(solution)/shard_map/ppermute | solution.py:351
  (123 other events, 880.9 us)
Sparse Core Ops, SparseCore 0:
  10.5 48.2 all-gather.4
  61.2 56.4 all-gather.6
  120.1 67.6 all-gather.8
  252.4 43.3 reduce-scatter.3
  298.6 45.2 all-gather.10
  347.2 90.2 reduce-scatter.5
  447.7 43.7 reduce-scatter.7
